TPU v7x, 256 devices: a whole 4x4x8 slice. The times are simulated.
256 devices in a mesh: grp: 8 (over y, core), ctx: 32 (over x, z).
Axes of the slice: x: 4, y: 4, z: 8, core: 2. Of those that a mesh axis runs over, the one named last changes fastest.
Arguments:
- queries: bfloat16 [128, 8192], P('grp'), may hold values from -250 to 250
- resident_key_cache: bfloat16 [128, 4096, 512], P('grp', 'ctx'), may hold values from -6 to 6
- resident_value_cache: bfloat16 [128, 4096, 512], P('grp', 'ctx'), may hold values from -6 to 6
- res_len: int32 [128], P('grp'), may hold values from 2 to 4096, as said below
- visual_page_pool: bfloat16 [4096, 2, 8, 512], P(('grp', 'ctx')), may hold values from -6 to 6
- recall_holder: int32 [32, 128, 16], P('ctx', 'grp'), may hold values from 0 to 255, all different within a row; in each aligned block of 16 rows (0 to 15, 16 to 31, ..., all dimensions but the last counted through in order) at most 2 rows name the same one
- recall_slot: int32 [32, 128, 16], P('ctx', 'grp'), may hold values from 0 to 15
- o_weight: bfloat16 [8192, 4096], P('ctx'), may hold values from -3 to 3
- residual: bfloat16 [128, 4096], P('grp'), may hold values from -60 to 60
- norm_gain: float32 [4096], replicated, may hold values from 0.5 to 1.5
- expert_ids: int32 [128, 8], P('grp'), may hold values from 0 to 63, all different within a row; in each aligned block of 16 rows (0 to 15, 16 to 31, ...) at most 4 rows name the same one
- expert_weights: float32 [128, 8], P('grp'), may hold values from 1 to 4
- w_gate: bfloat16 [256, 192, 4096], P(('grp', 'ctx')), may hold values from -0.09375 to 0.09375
- w_up: bfloat16 [256, 192, 4096], P(('grp', 'ctx')), may hold values from -0.09375 to 0.09375
- w_down: bfloat16 [256, 192, 4096], P(('grp', 'ctx')), may hold values from -0.21875 to 0.21875
Outputs:
- mixed: bfloat16 [128, 4096], P('grp', 'ctx')
Inputs may be any that keep to these rules, and one draw needn't show every extreme that they name: `res_len`: some request has length 4096 and some has length 2. `recall_holder`: the 16 holders of one request on one index of ctx differ; among the rows of one device (one index of ctx, the 16 requests of one group) no holder is named by more than 2 requests, and in some device's rows one holder by exactly 2. `expert_ids`: the 8 experts of a token differ; among the 16 tokens of one group no expert is named more than 4 times, and in some group one expert exactly 4 times.
All inputs are finite; a program needn't handle non-finite values.
Results may differ from a plain program's by a relative error of at most 0.025.
Values may be sent and summed in bfloat16 or wider, within the bound.
No kernel may reach another device: no remote copies, remote signals or barrier semaphores. Data moves between devices by JAX's collectives and lax.ppermute only.
A program may use at most 128 MiB of HBM per device.

v0:
```python
import jax
import jax.numpy as jnp
from jax import lax
from jax.sharding import PartitionSpec as P

QUERY_HEADS = 64
KEY_VALUE_HEADS = 4
HEAD_WIDTH = 128
EXP_GRP = 8
CAPE = 4


VERY_NEGATIVE = -1e30
NORM_EPSILON = 1e-06


def merged_2(value, axis, combine):
    everything = jax.tree.map(lambda part: lax.all_gather(part, axis), value)
    first = jax.tree.map(lambda part: part[0], everything)

    def lap(k, so_far):
        return combine(so_far, jax.tree.map(lambda part: part[k], everything))

    return lax.fori_loop(1, lax.axis_size(axis), lap, first)


def softmax_part(scores, is_valid):
    masked = jnp.where(is_valid, scores, VERY_NEGATIVE)
    row_peak = jnp.max(masked, axis=-1)
    weights = jnp.where(is_valid, jnp.exp(masked - row_peak[..., None]), 0.0)
    return (row_peak, jnp.sum(weights, axis=-1), weights)


def join_parts(earlier, later):
    peak_one, total_one, out_one = earlier
    peak_two, total_two, out_two = later
    new_peak = jnp.maximum(peak_one, peak_two)
    factor_one = jnp.exp(peak_one - new_peak)
    factor_two = jnp.exp(peak_two - new_peak)
    new_total = factor_one * total_one + factor_two * total_two
    new_out = factor_one[..., None] * out_one + factor_two[..., None] * out_two
    return (new_peak, new_total, new_out)


def shards(
    queries,
    resident_key_cache,
    resident_value_cache,
    res_len,
    visual_page_pool,
    recall_holder,
    recall_slot,
    o_weight,
    residual,
    norm_gain,
    expert_ids,
    expert_weights,
    w_gate,
    w_up,
    w_down,
):
    request_total = queries.shape[0]
    each_request = recall_holder.shape[2]
    resident_rows = resident_key_cache.shape[1]
    page_length = visual_page_pool.shape[2]
    head_groups = QUERY_HEADS // KEY_VALUE_HEADS
    ctx_count = lax.axis_size("ctx")
    grp_count = lax.axis_size("grp")
    every_device = ctx_count * grp_count
    ctx_index = lax.axis_index("ctx")
    slot_capacity = max(2, 2 * request_total * each_request // every_device)
    score_scale = HEAD_WIDTH ** (-0.5)
    query_matrix = queries.reshape(request_total, KEY_VALUE_HEADS, head_groups, HEAD_WIDTH)
    positions = ctx_index * resident_rows + jnp.arange(resident_rows, dtype=jnp.int32)
    resident_valid = positions[None, :] < res_len[:, None]
    local_resident_keys = resident_key_cache.reshape(
        request_total, resident_rows, KEY_VALUE_HEADS, HEAD_WIDTH
    )
    local_resident_values = resident_value_cache.reshape(
        request_total, resident_rows, KEY_VALUE_HEADS, HEAD_WIDTH
    )
    resident_scores = (
        jnp.einsum(
            "rkgd,rnkd->rkgn", query_matrix, local_resident_keys, preferred_element_type=jnp.float32
        )
        * score_scale
    )
    peak_res, total_res, weights_res = softmax_part(
        resident_scores, resident_valid[:, None, None, :]
    )
    out_res = jnp.einsum(
        "rkgn,rnkd->rkgd",
        weights_res.astype(jnp.bfloat16),
        local_resident_values,
        preferred_element_type=jnp.float32,
    )
    flat_holder = recall_holder[0].reshape(-1)
    flat_slot = recall_slot[0].reshape(-1)
    holder_hits = (
        flat_holder[:, None] == jnp.arange(every_device, dtype=jnp.int32)[None, :]
    ).astype(jnp.int32)
    holder_rank = jnp.sum((jnp.cumsum(holder_hits, axis=0) - holder_hits) * holder_hits, axis=1)
    slot_position = flat_holder * slot_capacity + holder_rank
    slot_asks = (
        jnp.zeros((every_device * slot_capacity,), jnp.int32)
        .at[slot_position]
        .set(flat_slot)
        .reshape(grp_count, ctx_count, slot_capacity)
    )
    received = lax.all_to_all(
        lax.all_to_all(slot_asks, "grp", split_axis=0, concat_axis=0, tiled=True),
        "ctx",
        split_axis=1,
        concat_axis=1,
        tiled=True,
    )
    found_pages = jnp.take(visual_page_pool, received, axis=0)
    gathered_pages = lax.all_to_all(
        lax.all_to_all(found_pages, "grp", split_axis=0, concat_axis=0, tiled=True),
        "ctx",
        split_axis=1,
        concat_axis=1,
        tiled=True,
    )
    local_pages = jnp.take(
        gathered_pages.reshape(
            every_device * slot_capacity, 2, page_length, KEY_VALUE_HEADS * HEAD_WIDTH
        ),
        slot_position,
        axis=0,
    )
    local_pages = local_pages.reshape(
        request_total, each_request, 2, page_length, KEY_VALUE_HEADS * HEAD_WIDTH
    )
    recall_keys = local_pages[:, :, 0].reshape(
        request_total, each_request * page_length, KEY_VALUE_HEADS, HEAD_WIDTH
    )
    recall_values = local_pages[:, :, 1].reshape(
        request_total, each_request * page_length, KEY_VALUE_HEADS, HEAD_WIDTH
    )
    recalled_scores = (
        jnp.einsum("rkgd,rnkd->rkgn", query_matrix, recall_keys, preferred_element_type=jnp.float32)
        * score_scale
    )
    peak_rec, total_rec, weights_rec = softmax_part(recalled_scores, True)
    out_rec = jnp.einsum(
        "rkgn,rnkd->rkgd",
        weights_rec.astype(jnp.bfloat16),
        recall_values,
        preferred_element_type=jnp.float32,
    )
    stats = join_parts((peak_res, total_res, out_res), (peak_rec, total_rec, out_rec))
    heads_each = o_weight.shape[0] // HEAD_WIDTH
    merged = merged_2(stats, "ctx", join_parts)
    attn_all = (
        (merged[2] / merged[1][..., None])
        .astype(jnp.bfloat16)
        .reshape(request_total, QUERY_HEADS * HEAD_WIDTH)
    )
    attn_mine = lax.dynamic_slice_in_dim(
        attn_all, ctx_index * heads_each * HEAD_WIDTH, heads_each * HEAD_WIDTH, 1
    )
    projected = lax.psum(
        jnp.dot(attn_mine, o_weight, preferred_element_type=jnp.float32).astype(jnp.bfloat16), "ctx"
    ).astype(jnp.float32)
    hidden = residual.astype(jnp.float32) + projected
    normed = (
        hidden
        * lax.rsqrt(jnp.mean(hidden * hidden, axis=-1, keepdims=True) + NORM_EPSILON)
        * norm_gain
    ).astype(jnp.bfloat16)
    parts_count = ctx_count // EXP_GRP
    local_expert = ctx_index // parts_count
    wanted = jnp.arange(grp_count, dtype=jnp.int32) * EXP_GRP + local_expert
    matches = expert_ids[:, :, None] == wanted[None, None, :]
    taken = jnp.any(matches, axis=1).astype(jnp.int32)
    coefficient = jnp.sum(jnp.where(matches, expert_weights[:, :, None], 0.0), axis=1)
    order = jnp.cumsum(taken, axis=0) - taken
    slot_hit = (taken[:, :, None] == 1) & (
        order[:, :, None] == jnp.arange(CAPE, dtype=jnp.int32)[None, None, :]
    )
    picker = slot_hit.astype(jnp.bfloat16)
    outgoing = jnp.einsum("rgs,rd->gsd", picker, normed, preferred_element_type=jnp.float32).astype(
        jnp.bfloat16
    )
    arrived = lax.all_to_all(outgoing, "grp", split_axis=0, concat_axis=0, tiled=True)
    gate_value = jnp.einsum("gsd,fd->gsf", arrived, w_gate[0], preferred_element_type=jnp.float32)
    upward = jnp.einsum("gsd,fd->gsf", arrived, w_up[0], preferred_element_type=jnp.float32)
    activation = (jax.nn.silu(gate_value) * upward).astype(jnp.bfloat16)
    result = jnp.einsum("gsf,fd->gsd", activation, w_down[0], preferred_element_type=jnp.float32)
    returned = lax.all_to_all(
        result.astype(jnp.bfloat16), "grp", split_axis=0, concat_axis=0, tiled=True
    ).astype(result.dtype)
    combine_table = slot_hit.astype(jnp.float32) * coefficient[:, :, None]
    mixture = jnp.einsum("rgs,gsd->rd", combine_table, returned, precision=lax.Precision.HIGHEST)
    share = lax.psum_scatter(
        mixture.astype(jnp.bfloat16), "ctx", scatter_dimension=1, tiled=True
    ).astype(jnp.float32)
    columns = share.shape[1]
    own_hidden = lax.dynamic_slice_in_dim(hidden, ctx_index * columns, columns, 1)
    return (own_hidden + share).astype(jnp.bfloat16)


def solution(mesh):
    placed = (
        P("grp", None),
        P("grp", "ctx", None),
        P("grp", "ctx", None),
        P("grp"),
        P(("grp", "ctx"), None, None, None),
        P("ctx", "grp", None),
        P("ctx", "grp", None),
        P("ctx", None),
        P("grp", None),
        P(),
        P("grp", None),
        P("grp", None),
        P(("grp", "ctx"), None, None),
        P(("grp", "ctx"), None, None),
        P(("grp", "ctx"), None, None),
    )
    return jax.shard_map(
        shards, mesh=mesh, in_specs=placed, out_specs=P("grp", "ctx"), check_vma=False
    )
```

profile of v0, /device:TPU:1, one launch (start us, length us, event | category | flops | bytes accessed | tf_op | source)
XLA Modules:
  0.0 985.8 jit_solution(17099152258480921521)
XLA Ops:
  12.1 10.4 %all_to_all.30 = s32[8,32,2]{1,2,0:T(2,128)S(1)} all-to-all(s32[8,32,2]{1,2,0:T(2,128)S(1)} %copy.132), channel_id=1, replica_groups=mesh['grp'=8,'ctx'=32] {'grp'}, dimensions={0} | all-to-all | bytes 4096 | tf_op jit(solution)/shard_map/all_to_all | solution.py:111
  22.6 19.6 %all_to_all.31 = s32[8,32,2]{0,2,1:T(2,128)S(1)} all-to-all(s32[8,32,2]{0,2,1:T(2,128)S(1)} %copy.133), channel_id=1, replica_groups=mesh['grp'=8,'ctx'=32] {'ctx'}, dimensions={1} | all-to-all | bytes 4096 | tf_op jit(solution)/shard_map/all_to_all | solution.py:110
  43.0 13.2 %gather_fusion = bf16[512,2,8,512]{3,2,1,0:T(8,128)(2,1)} fusion(bf16[16,2,8,512]{3,2,1,0:T(8,128)(2,1)S(1)} %copy-done.2, s32[1024]{0:T(1024)S(1)} %pad_clamp_fusion.1), kind=kCustom, calls=%fused_computation | custom fusion | bytes 16779264 | tf_op jit(solution)/shard_map/jit(_take)/gather | solution.py:117
  56.2 4.5 broadcast_select_fusion
  60.7 100.5 %all_to_all.32 = bf16[8,32,2,2,8,512]{5,4,3,2,1,0:T(8,128)(2,1)} all-to-all(bf16[8,32,2,2,8,512]{5,4,3,2,1,0:T(8,128)(2,1)S(1)} %broadcast_select_fusion), channel_id=1, replica_groups=mesh['grp'=8,'ctx'=32] {'grp'}, dimensions={0} | all-to-all | bytes 16777216 | tf_op jit(solution)/shard_map/all_to_all | solution.py:119
  161.2 8.5 copy.136
  169.7 5.1 all-to-all-start.3
  176.5 185.4 %all-to-all-done.3 = bf16[8,32,2,2,8,512]{5,4,3,2,0,1:T(8,128)(2,1)} async-done(((bf16[8,32,2,2,8,512]{5,4,3,2,0,1:T(8,128)(2,1)}), bf16[8,32,2,2,8,512]{5,4,3,2,0,1:T(8,128)(2,1)}, u32[]{:S(2)}, u32[]{:S(2)}) %all-to-all-start.3) | async-done | bytes 8388640 | tf_op jit(solution)/shard_map/all_to_all | solution.py:118
  361.9 8.5 copy.137
  370.4 6.1 gather_fusion.1
  376.6 2.5 copy_select_fusion
  379.1 1.6 fusion.91
  380.7 2.0 reshape_squeeze.14
  382.7 2.9 fusion.92
  385.6 2.6 reshape_squeeze.15
  388.2 2.3 fusion.38
  390.5 1.5 fusion.29
  393.2 46.0 %all_gather.14 = f32[32,16,4,16]{3,1,2,0:T(8,128)S(1)} all-gather(f32[1,16,4,16]{3,1,2,0:T(8,128)S(1)} %copy.140), channel_id=1, replica_groups=mesh['grp'=8,'ctx'=32] {'ctx'}, dimensions={0}, use_global_device_ids=true | all-gather | bytes 135168 | tf_op jit(solution)/shard_map/all_gather | solution.py:18
  439.2 39.8 %all_gather.15 = f32[32,16,4,16]{3,1,2,0:T(8,128)S(1)} all-gather(f32[1,16,4,16]{3,1,2,0:T(8,128)S(1)} %copy.141), channel_id=1, replica_groups=mesh['grp'=8,'ctx'=32] {'ctx'}, dimensions={0}, use_global_device_ids=true | all-gather | bytes 135168 | tf_op jit(solution)/shard_map/all_gather | solution.py:18
  479.0 69.6 %all-gather.3.cloned.1.call-done = f32[512,4,16,128]{3,2,1,0:T(8,128)} async-done(((f32[16,4,16,128]{3,2,1,0:T(8,128)}), f32[512,4,16,128]{3,2,1,0:T(8,128)}) %all-gather.3.cloned.1.call-update) | async-done | bytes 16777232 | tf_op jit(solution)/shard_map/all_gather | solution.py:18
  549.6 48.0 %while.19 = (s32[]{:T(128)}, f32[16,4,16]{2,1,0:T(4,128)S(1)}, f32[16,4,16]{2,1,0:T(4,128)S(1)}, f32[16,4,16,128]{3,2,1,0:T(8,128)S(1)}, f32[32,16,4,16]{3,1,2,0...) while((s32[]{:T(128)}, f32[16,4,16]{2,1,0:T(4,128)S(1)}, ...), condition=%wide.region_9.10_spmd, body=%wide.region_8.9_spmd.sunk | while | flops 399365 | bytes 1630359 | solution.py:24
  551.3 1.4 fusion.104
  552.9 1.4 fusion.104
  556.0 1.4 fusion.104
  598.1 2.6 convolution_convert_fusion.2
  600.9 135.5 %all-reduce.2.cloned.1.call-done = bf16[16,4096]{1,0:T(8,128)(2,1)} async-done(((bf16[16,4096]{1,0:T(8,128)(2,1)}), bf16[16,4096]{1,0:T(8,128)(2,1)}) %all-reduce.2.cloned.1.call-update) | async-done | bytes 131088 | tf_op jit(solution)/shard_map/psum | solution.py:163
  738.9 15.0 %all_to_all.33 = bf16[8,4,4096]{2,1,0:T(4,128)(2,1)S(1)} all-to-all(bf16[8,4,4096]{2,1,0:T(4,128)(2,1)S(1)} %copy.151), channel_id=1, replica_groups=mesh['grp'=8,'ctx'=32] {'grp'}, dimensions={0} | all-to-all | bytes 524288 | tf_op jit(solution)/shard_map/all_to_all | solution.py:186
  753.9 2.1 fusion.18
  756.1 2.0 fusion.44
  759.4 4.4 all-to-all-start.5
  763.9 6.4 all-to-all-done.5
  772.0 205.8 %reduce-scatter.4.cloned.1.call-done = bf16[128,16]{1,0:T(8,128)(2,1)} async-done(((bf16[4096,16]{1,0:T(8,128)(2,1)}), bf16[128,16]{1,0:T(8,128)(2,1)}) %reduce-scatter.4.cloned.1.call-update) | async-done | bytes 4112
  (181 shorter events, 60.5 us)
Async XLA Ops:
  6.5 168.7 %copy-start = (bf16[16,128,512]{2,1,0:T(8,128)(2,1)S(1)}, bf16[16,128,512]{2,1,0:T(8,128)(2,1)}, u32[]{:S(2)}) copy-start(bf16[16,128,512]{2,1,0:T(8,128)(2,1)} %param.18) | copy-start | bytes 6291460
  6.5 36.4 %copy-start.2 = (bf16[16,2,8,512]{3,2,1,0:T(8,128)(2,1)S(1)}, bf16[16,2,8,512]{3,2,1,0:T(8,128)(2,1)}, u32[]{:S(2)}) copy-start(bf16[16,2,8,512]{3,2,1,0:T(8,128)(2,1)} %param.21) | copy-start | bytes 786436
  169.7 5.4 copy-start.5
  169.7 5.5 copy-start.10
  169.7 5.6 copy-start.6
  169.7 192.3 %all-to-all-start.3 = ((bf16[8,32,2,2,8,512]{5,4,3,2,0,1:T(8,128)(2,1)}), bf16[8,32,2,2,8,512]{5,4,3,2,0,1:T(8,128)(2,1)}, u32[]{:S(2)}, u32[]{:S(2)}) async-start(bf16[8,32,2,2,8,512]{5,4,3,2,0,1:T(8,128)(2,1)} %copy.136), calls=%async_computation.3 | async-start | bytes 16777216 | tf_op jit(solution)/shard_map/all_to_all | solution.py:118
  174.8 373.8 %all-gather.3.cloned.1.call-start = ((), (), s32[]{:S(2)}) async-start(), calls=%async_computation.8 | async-start | bytes 17301504 | tf_op jit(solution)/shard_map/all_gather | solution.py:18
  390.5 1.6 copy-start.8
  392.1 344.4 %all-reduce.2.cloned.1.call-start = ((), (), s32[]{:S(2)}) async-start(), calls=%async_computation.7 | async-start | bytes 262144 | tf_op jit(solution)/shard_map/psum | solution.py:163
  597.7 138.8 %copy-start.4 = (bf16[16,4096]{1,0:T(8,128)(2,1)S(1)}, bf16[16,4096]{1,0:T(8,128)(2,1)}, u32[]{:S(2)}) copy-start(bf16[16,4096]{1,0:T(8,128)(2,1)} %param.25) | copy-start | bytes 393220
  597.7 139.9 %copy-start.7 = (f32[4096]{0:T(1024)S(1)}, f32[4096]{0:T(1024)}, u32[]{:S(2)}) copy-start(f32[4096]{0:T(1024)} %param.26) | copy-start | bytes 49156
  753.9 4.2 copy-start.3
  756.1 7.7 copy-start.9
  758.1 221.2 %copy-start.1 = (bf16[16,128,512]{2,1,0:T(8,128)(2,1)S(1)}, bf16[16,128,512]{2,1,0:T(8,128)(2,1)}, u32[]{:S(2)}) copy-start(bf16[16,128,512]{2,1,0:T(8,128)(2,1)} %param.18) | copy-start | bytes 6291460
  759.4 10.9 %all-to-all-start.5 = ((bf16[8,4,4096]{2,1,0:T(4,128)(2,1)}), bf16[8,4,4096]{2,1,0:T(4,128)(2,1)S(1)}, u32[]{:S(2)}, u32[]{:S(2)}) async-start(bf16[8,4,4096]{2,1,0:T(4,128)(2,1)} %copy.153), calls=%async_computation.5 | async-start | bytes 524288 | tf_op jit(solution)/shard_map/all_to_all | solution.py:191
  763.8 214.1 %reduce-scatter.4.cloned.1.call-start = ((), (), s32[]{:S(2)}) async-start(), calls=%async_computation.9 | async-start | bytes 1081344
Sparse Core Ops, SparseCore 0:
  392.2 156.3 all-gather.2
  600.9 135.5 all-reduce.1
  772.2 205.6 reduce-scatter.3
where the time goes:
time: 993 us; the launch traced here: 986 us
  waiting for transfers between devices  603 us (61%)
  blocking collectives  231 us (23%)
  other arithmetic  57.8 us (6%)
  local copies, waits for them, and re-layouts  53 us (5%)
  matrix products  16.7 us (2%)
  between operations  13.5 us (1%)
    unnamed x4, waiting for transfers between devices  206 us
    all_to_all x1, waiting for transfers between devices, shards(): lax.all_to_all(lax.all_to_all(found_pages, 'grp', split_axis=0, concat_ax...  185 us
    psum x1, waiting for transfers between devices, shards(): lax.psum(jnp.dot(attn_mine, o_weight, preferred_element_type=jnp.float32)...  136 us
    all_to_all x1, blocking collectives, shards(): lax.all_to_all(found_pages, 'grp', split_axis=0, concat_axis=0, tiled=True)  100 us
    all_gather x2, blocking collectives, merged_2(): everything = jax.tree.map(lambda part: lax.all_gather(part, axis), value)  85.7 us
    all_gather x1, waiting for transfers between devices, merged_2(): everything = jax.tree.map(lambda part: lax.all_gather(part, axis), value)  69.6 us
    add x31, other arithmetic, join_parts(): new_out = factor_one[..., None] * out_one + factor_two[..., None] * out_two  44.5 us
  transfers between devices with their start and end apart: 5, of which 5 were waited for; matrix products, arithmetic and copies ran while one was open for 0% of the time, Pallas kernels for 0%

commit v1 on v0

v1 whole, which is shorter than its diff:
```python
import jax
import jax.numpy as jnp
from jax import lax
from jax.experimental import pallas as pl
from jax.experimental.pallas import tpu as pltpu
from jax.sharding import Mesh, PartitionSpec as P

HEADS = 64
KV = 4
HPK = HEADS // KV
HW = 128
T = 16
D = 4096
NC = 32
NG = 8
CAPE = 4
FP = 192
TOK = 8
SLOTS = 16
EPS = 1e-06
NEG = -(2.0**100)
SCALE = HW**-0.5
BF = jnp.bfloat16
F32 = jnp.float32
GRP = ("y", "core")
CTX = ("x", "z")
ALL = GRP + CTX
NT = (((1,), (1,)), ((), ()))
STAT_ROWS = 16
CHUNK = 2 * T + STAT_ROWS


def params(mib):
    return pltpu.CompilerParams(vmem_limit_bytes=mib * 2**20)


def cost(flops, moved, exps=0):
    return pl.CostEstimate(flops=flops, bytes_accessed=moved, transcendentals=exps)


def whole(shape):
    return pl.BlockSpec(shape, lambda *_: (0,) * len(shape))


def prep_kernel(key_ref, ids_ref, weights_ref, lists_ref, picker_ref, combine_ref):
    key = key_ref[...]
    lane = lax.broadcasted_iota(jnp.int32, (T, 128), 1)
    columns = [jnp.broadcast_to(key[:, j : j + 1], (T, 128)) for j in range(key.shape[1])]
    for c in range(NC):
        here = lane + c * 128
        hits = jnp.zeros((T, 128), F32)
        for column in columns:
            hits = hits + jnp.where(column == here, 1.0, 0.0)
        lists_ref[c] = hits.astype(BF)
    rows = NG * NC * CAPE
    place = lax.broadcasted_iota(jnp.int32, (T, rows), 1)
    expert = place // 16
    slot = (place % CAPE).astype(F32)
    taken = jnp.zeros((T, rows), F32)
    coefficient = jnp.zeros((T, rows), F32)
    for j in range(ids_ref.shape[1]):
        hit = jnp.broadcast_to(ids_ref[:, j : j + 1], (T, rows)) == expert
        taken = taken + jnp.where(hit, 1.0, 0.0)
        coefficient = coefficient + jnp.where(hit, jnp.broadcast_to(weights_ref[:, j : j + 1], (T, rows)), 0.0)
    before = (lax.broadcasted_iota(jnp.int32, (T, T), 1) < lax.broadcasted_iota(jnp.int32, (T, T), 0)).astype(F32)
    order = jnp.dot(before.astype(BF), taken.astype(BF), preferred_element_type=F32)
    hit = jnp.where((taken > 0.5) & (order == slot), 1.0, 0.0)
    picker_ref[...] = jnp.transpose(hit).astype(BF)
    table = hit * coefficient
    high = table.astype(BF)
    combine_ref[:T] = high
    combine_ref[T:] = (table - high.astype(F32)).astype(BF)


def resident_kernel(length_ref, start_ref, q_ref, k_ref, v_ref, out_ref, peak_ref, total_ref):
    step = pl.program_id(0)
    each = k_ref.shape[0]
    position = lax.broadcasted_iota(jnp.int32, (HEADS, 128), 1) + start_ref[0]
    for i in range(each):
        t = step * each + i
        valid = position < length_ref[t]
        scores = jnp.concatenate(
            [
                lax.dot_general(
                    q_ref[i, g * HPK : (g + 1) * HPK, :],
                    k_ref[i, :, g * HW : (g + 1) * HW],
                    NT,
                    preferred_element_type=F32,
                )
                for g in range(KV)
            ],
            axis=0,
        )
        scores = jnp.where(valid, scores * SCALE, NEG)
        peak = jnp.max(scores, axis=1, keepdims=True)
        weights = jnp.where(valid, jnp.exp(scores - peak), 0.0)
        total = jnp.sum(weights, axis=1, keepdims=True)
        rounded = weights.astype(BF)
        out = jnp.concatenate(
            [
                jnp.dot(
                    rounded[g * HPK : (g + 1) * HPK, :],
                    v_ref[i, :, g * HW : (g + 1) * HW],
                    preferred_element_type=F32,
                )
                for g in range(KV)
            ],
            axis=0,
        )
        here = pl.ds(t, HEADS, stride=T)
        out_ref[here, :] = out
        peak_ref[here, :] = jnp.broadcast_to(peak, (HEADS, 128))
        total_ref[here, :] = jnp.broadcast_to(total, (HEADS, 128))


def recalled_kernel(lists_ref, q_ref, pages_ref, out_res_ref, peak_res_ref, total_res_ref, send_ref):
    rows = HPK * T
    tokens = NG * SLOTS * TOK
    counts = jnp.sum(lists_ref[...].astype(F32), axis=0).astype(BF)
    spread = (
        lax.broadcasted_iota(jnp.int32, (128, tokens), 1) // TOK == lax.broadcasted_iota(jnp.int32, (128, tokens), 0)
    ).astype(F32)
    times = jnp.dot(counts, spread.astype(BF), preferred_element_type=F32)[None]
    keys = jnp.concatenate([pages_ref[b, :128, :] for b in range(NG)], axis=0)
    values = jnp.concatenate([pages_ref[b, 128:, :] for b in range(NG)], axis=0)
    scores = lax.dot_general(q_ref[...], keys, NT, preferred_element_type=F32)
    scores = jnp.where(times > 0.5, scores.reshape(HPK, T, tokens) * SCALE, NEG)
    peak_res = peak_res_ref[...]
    peak = jnp.max(scores, axis=2, keepdims=True).reshape(rows, 1)
    peak = jnp.maximum(jnp.broadcast_to(peak, (rows, 128)), peak_res)
    peak_high = peak.astype(BF).astype(F32)
    peak_low = (peak - peak_high).astype(BF).astype(F32)
    base = peak_high + peak_low
    weights = jnp.where(times > 0.5, jnp.exp(scores - base[:, :1].reshape(HPK, T, 1)) * times, 0.0)
    total = jnp.sum(weights, axis=2, keepdims=True).reshape(rows, 1)
    out = jnp.dot(weights.reshape(rows, tokens).astype(BF), values, preferred_element_type=F32)
    factor = jnp.exp(peak_res - base)
    out = out + factor * out_res_ref[...]
    total = jnp.broadcast_to(total, (rows, 128)) + factor * total_res_ref[...]
    total_high = total.astype(BF).astype(F32)
    total_low = total - total_high
    lane = lax.broadcasted_iota(jnp.int32, (rows, 128), 1) % 4
    stats = jnp.where(
        lane == 0, peak_high, jnp.where(lane == 1, peak_low, jnp.where(lane == 2, total_high, total_low))
    ).reshape(HPK // 2, 2, T, 128)
    lane = lax.broadcasted_iota(jnp.int32, (HPK // 2, T, 128), 2)
    stats = jnp.where(lane < 4, stats[:, 0], stats[:, 1])
    send_ref[:, : 2 * T, :] = out.reshape(HPK // 2, 2 * T, 128).astype(BF)
    send_ref[:, 2 * T :, :] = stats.astype(BF)


def project_kernel(parts_ref, weight_ref, send_ref):
    stats = parts_ref[:, 2 * T :, :].astype(F32)
    heads = []
    for i in range(2):
        peak = stats[:, :, 4 * i : 4 * i + 1] + stats[:, :, 4 * i + 1 : 4 * i + 2]
        total = stats[:, :, 4 * i + 2 : 4 * i + 3] + stats[:, :, 4 * i + 3 : 4 * i + 4]
        factor = jnp.exp(peak - jnp.max(peak, axis=0, keepdims=True))
        total = jnp.sum(factor * total, axis=0)
        out = jnp.sum(factor * parts_ref[:, i * T : (i + 1) * T, :].astype(F32), axis=0)
        heads.append((out / total).astype(BF))
    attention = jnp.concatenate(heads, axis=1)
    wide = 512
    for j in range(D // wide):
        block = jnp.dot(attention, weight_ref[:, j * wide : (j + 1) * wide], preferred_element_type=F32).astype(BF)
        for i in range(wide // 128):
            send_ref[j * (wide // 128) + i] = block[:, i * 128 : (i + 1) * 128]


def dispatch_kernel(sums_ref, residual_ref, picker_ref, hidden_ref, send_ref):
    hidden = residual_ref[...].astype(F32) + jnp.sum(sums_ref[...].astype(F32), axis=0)
    hidden_ref[...] = hidden
    send_ref[...] = jnp.dot(picker_ref[...], hidden.astype(BF), preferred_element_type=F32).astype(BF)


def expert_kernel(rows_ref, gain_ref, gate_ref, up_ref, down_ref, send_ref, wide_ref, token_ref):
    wide_ref[...] = rows_ref[...].astype(F32)
    for c in range(NC):
        for s in range(CAPE):
            token_ref[s * NG : (s + 1) * NG, c * 128 : (c + 1) * 128] = wide_ref[pl.ds(c * CAPE + s, NG, stride=128), :]
    hidden = token_ref[...]
    normed = (hidden * lax.rsqrt(jnp.mean(hidden * hidden, axis=1, keepdims=True) + EPS) * gain_ref[...]).astype(BF)
    gate = lax.dot_general(normed, gate_ref[...], NT, preferred_element_type=F32)
    up = lax.dot_general(normed, up_ref[...], NT, preferred_element_type=F32)
    act = (gate / (1.0 + jnp.exp(-gate)) * up).astype(BF)
    wide = 512
    for j in range(D // wide):
        block = jnp.dot(act, down_ref[:, j * wide : (j + 1) * wide], preferred_element_type=F32)
        for i in range(wide // 128):
            for s in range(CAPE):
                wide_ref[pl.ds((j * (wide // 128) + i) * CAPE + s, NG, stride=128), :] = block[
                    s * NG : (s + 1) * NG, i * 128 : (i + 1) * 128
                ]
    send_ref[...] = wide_ref[...].astype(BF)


def combine_kernel(rows_ref, table_ref, hidden_ref, out_ref):
    both = jnp.dot(table_ref[...], rows_ref[...], preferred_element_type=F32)
    out_ref[...] = (hidden_ref[...] + both[:T] + both[T:]).astype(BF)


def shards(
    queries,
    resident_key_cache,
    resident_value_cache,
    res_len,
    visual_page_pool,
    recall_holder,
    recall_slot,
    o_weight,
    residual,
    norm_gain,
    expert_ids,
    expert_weights,
    w_gate,
    w_up,
    w_down,
):
    ctx_index = lax.axis_index(CTX)
    rows = NG * NC * CAPE

    own_pages = jnp.swapaxes(visual_page_pool, 0, 1).reshape(2 * SLOTS * TOK, KV * HW)
    pages = lax.all_gather(own_pages, GRP)

    holder = recall_holder[0]
    key = (holder % NC) * 128 + (holder // NC) * SLOTS + recall_slot[0]
    lists, picker, table = pl.pallas_call(
        prep_kernel,
        out_shape=(
            jax.ShapeDtypeStruct((NC, T, 128), BF),
            jax.ShapeDtypeStruct((rows, T), BF),
            jax.ShapeDtypeStruct((2 * T, rows), BF),
        ),
        compiler_params=params(16),
        cost_estimate=cost(4_000_000, 400_000),
        name="prep",
    )(key, expert_ids, expert_weights)
    lists = lax.all_to_all(lists, CTX, split_axis=0, concat_axis=0, tiled=True)

    by_request = queries.reshape(T, HEADS, HW)
    by_head = jnp.swapaxes(by_request, 0, 1).reshape(HEADS * T, HW)
    each = 4
    stat = jax.ShapeDtypeStruct((HEADS * T, 128), F32)
    out_res, peak_res, total_res = pl.pallas_call(
        resident_kernel,
        grid=(T // each,),
        in_specs=[
            pl.BlockSpec(memory_space=pltpu.SMEM),
            pl.BlockSpec(memory_space=pltpu.SMEM),
            pl.BlockSpec((each, HEADS, HW), lambda i: (i, 0, 0)),
            pl.BlockSpec((each, 128, KV * HW), lambda i: (i, 0, 0)),
            pl.BlockSpec((each, 128, KV * HW), lambda i: (i, 0, 0)),
        ],
        out_specs=[whole((HEADS * T, 128))] * 3,
        out_shape=(stat, stat, stat),
        compiler_params=params(24),
        cost_estimate=cost(70_000_000, 6_000_000, 131_072),
        name="resident",
    )(res_len, (ctx_index * 128).reshape(1).astype(jnp.int32), by_request, resident_key_cache, resident_value_cache)

    block = pl.BlockSpec((HPK * T, 128), lambda k: (k, 0))
    parts = pl.pallas_call(
        recalled_kernel,
        grid=(KV,),
        in_specs=[
            whole((NC, T, 128)),
            block,
            pl.BlockSpec((NG, 256, 128), lambda k: (0, 0, k)),
            block,
            block,
            block,
        ],
        out_specs=pl.BlockSpec((HPK // 2, CHUNK, 128), lambda k: (k, 0, 0)),
        out_shape=jax.ShapeDtypeStruct((NC, CHUNK, 128), BF),
        compiler_params=params(40),
        cost_estimate=cost(550_000_000, 5_000_000, 1_048_576),
        name="recalled",
    )(lists, by_head, pages, out_res, peak_res, total_res)
    parts = lax.all_to_all(parts, CTX, split_axis=0, concat_axis=0, tiled=True)

    sums = pl.pallas_call(
        project_kernel,
        out_shape=jax.ShapeDtypeStruct((NC, T, 128), BF),
        compiler_params=params(24),
        cost_estimate=cost(40_000_000, 2_700_000, 2048),
        name="project",
    )(parts, o_weight)
    sums = lax.all_to_all(sums, CTX, split_axis=0, concat_axis=0, tiled=True)

    own_residual = lax.dynamic_slice_in_dim(residual, ctx_index * 128, 128, 1)
    hidden, send = pl.pallas_call(
        dispatch_kernel,
        out_shape=(jax.ShapeDtypeStruct((T, 128), F32), jax.ShapeDtypeStruct((rows, 128), BF)),
        compiler_params=params(16),
        cost_estimate=cost(4_000_000, 500_000),
        name="dispatch",
    )(sums, own_residual, picker)
    arrived = lax.all_to_all(send.reshape(NG * NC, CAPE, 128), ALL, split_axis=0, concat_axis=0, tiled=True)

    results = pl.pallas_call(
        expert_kernel,
        out_shape=jax.ShapeDtypeStruct((rows, 128), BF),
        scratch_shapes=[pltpu.VMEM((rows, 128), F32), pltpu.VMEM((NG * CAPE, D), F32)],
        compiler_params=params(32),
        cost_estimate=cost(160_000_000, 5_300_000, 8192),
        name="experts",
    )(arrived.reshape(rows, 128), norm_gain.reshape(1, D), w_gate[0], w_up[0], w_down[0])
    returned = lax.all_to_all(results.reshape(NG * NC, CAPE, 128), ALL, split_axis=0, concat_axis=0, tiled=True)

    return pl.pallas_call(
        combine_kernel,
        out_shape=jax.ShapeDtypeStruct((T, 128), BF),
        compiler_params=params(16),
        cost_estimate=cost(8_000_000, 400_000),
        name="combine",
    )(returned.reshape(rows, 128), table, hidden)


def solution(mesh):
    fine = Mesh(mesh.devices.reshape(4, 2, 4, 8), ALL)
    placed = (
        P(GRP, None),
        P(GRP, CTX, None),
        P(GRP, CTX, None),
        P(GRP),
        P(ALL, None, None, None),
        P(CTX, GRP, None),
        P(CTX, GRP, None),
        P(CTX, None),
        P(GRP, None),
        P(),
        P(GRP, None),
        P(GRP, None),
        P(ALL, None, None),
        P(ALL, None, None),
        P(ALL, None, None),
    )
    return jax.shard_map(shards, mesh=fine, in_specs=placed, out_specs=P(GRP, CTX), check_vma=False)
```

time: 993 us -> 146 us (0.15)
  waiting for transfers between devices: 603 us -> 15.9 us
  blocking collectives: 231 us -> 65.5 us
  other arithmetic: 57.8 us -> 0.73 us
  local copies, waits for them, and re-layouts: 53 us -> 14.5 us
  matrix products: 16.7 us -> 0 us
  Pallas kernels: 0 us -> 15.2 us
    unnamed x4 -> x1, waiting for transfers between devices: 206 us -> 0.02 us
    all_to_all x2, waiting for transfers between devices: 192 us -> 9.15 us  [the longest x1 9.14 us: shards(): sums = lax.all_to_all(sums, CTX, split_axis=0, concat_axis=0, tiled=True)]
    psum x1 -> x0, waiting for transfers between devices: 136 us -> none  [shards(): lax.psum(jnp.dot(attn_mine, o_weight, preferred_element_type=jnp.float32)...]
    all_gather x2 -> x0, blocking collectives: 85.7 us -> none  [merged_2(): everything = jax.tree.map(lambda part: lax.all_gather(part, axis), value)]
    all_to_all x4 -> x3, blocking collectives: 145 us -> 65.5 us  [the longest x1 23.5 us: shards(): lax.all_to_all(send.reshape(NG * NC, CAPE, 128), ALL, split_axis=0, conca...]
    all_gather x1, waiting for transfers between devices: 69.6 us -> 6.78 us  [shards(): pages = lax.all_gather(own_pages, GRP)]
    add x66 -> x1, other arithmetic: 47.7 us -> 0.73 us  [shards(): key = holder % NC * 128 + holder // NC * SLOTS + recall_slot[0]]
    gather x2 -> x0, local copies, waits for them, and re-layouts: 19.3 us -> none  [the longest x1 13.2 us: shards(): found_pages = jnp.take(visual_page_pool, received, axis=0)]
  transfers between devices with their start and end apart: 5 -> 3, of which waited for: 5 -> 2; matrix products, arithmetic and copies ran while one was open for 0% -> 2% of each run, Pallas kernels for 0% -> 5%
where the time goes in v1:
time: 146 us; the launch traced here: 145 us
  blocking collectives  65.5 us (45%)
  starting transfers between devices  19.5 us (13%)
  waiting for transfers between devices  15.9 us (11%)
  Pallas kernels  15.2 us (10%)
  local copies, waits for them, and re-layouts  14.5 us (10%)
  between operations  13.6 us (9%)
    all_to_all x1, blocking collectives, shards(): lax.all_to_all(send.reshape(NG * NC, CAPE, 128), ALL, split_axis=0, conca...  23.5 us
    all_to_all x1, blocking collectives, shards(): parts = lax.all_to_all(parts, CTX, split_axis=0, concat_axis=0, tiled=True)  21.1 us
    all_to_all x1, blocking collectives, shards(): lax.all_to_all(results.reshape(NG * NC, CAPE, 128), ALL, split_axis=0, co...  20.9 us
    unnamed x35, local copies, waits for them, and re-layouts  12.5 us
    all_to_all x1, starting transfers between devices, shards(): lists = lax.all_to_all(lists, CTX, split_axis=0, concat_axis=0, tiled=True)  11.9 us
    all_to_all x1, waiting for transfers between devices, shards(): sums = lax.all_to_all(sums, CTX, split_axis=0, concat_axis=0, tiled=True)  9.14 us
    all_to_all x1, starting transfers between devices, shards(): sums = lax.all_to_all(sums, CTX, split_axis=0, concat_axis=0, tiled=True)  7.61 us
    all_gather x1, waiting for transfers between devices, shards(): pages = lax.all_gather(own_pages, GRP)  6.78 us
  transfers between devices with their start and end apart: 3, of which 2 were waited for; matrix products, arithmetic and copies ran while one was open for 2% of the time, Pallas kernels for 5%

profile of v1, /device:TPU:1, one launch (start us, length us, event | category | flops | bytes accessed | tf_op | source)
XLA Modules:
  0.0 144.8 jit_solution(9572914699173412962)
XLA Ops:
  6.5 1.8 %copy.23 = bf16[2,16,8,512]{3,2,1,0:T(8,128)(2,1)} copy(bf16[2,16,8,512]{3,2,0,1:T(8,128)(2,1)} %bitcast.50) | data formatting | bytes 524288 | tf_op jit(solution)/shard_map/transpose | solution.py:222
  8.4 0.0 all-gather.2.cloned.1.call-update
  8.4 0.8 copy.20.ids_ref
  9.2 0.8 copy.21.weights_ref
  9.9 0.7 fusion.2.key_ref
  10.6 1.4 prep.1
  12.0 0.7 copy-done.12
  12.7 11.9 %all-to-all-start = ((bf16[32,16,128]{2,1,0:T(8,128)(2,1)}), bf16[32,16,128]{2,1,0:T(8,128)(2,1)S(1)}, u32[]{:S(2)}, u32[]{:S(2)}) async-start(bf16[32,16,128]{2,1,0:T(8,128)(2,1)} %get-tuple-element.13), calls=%async_computation | async-start | bytes 262144 | tf_op jit(solution)/shard_map/all_to_all | solution.py:238
  24.6 1.0 copy.24
  25.6 0.2 copy.22
  25.8 0.0 copy-start.2
  25.8 1.6 %copy-done.2 = bf16[16,128,512]{2,1,0:T(8,128)(2,1)S(1)} copy-done((bf16[16,128,512]{2,1,0:T(8,128)(2,1)S(1)}, bf16[16,128,512]{2,1,0:T(8,128)(2,1)}, u32[]{:S(2)}) %copy-start.2) | copy-done | bytes 2097176
  27.4 5.4 %resident.1 = (f32[1024,128]{1,0:T(8,128)S(1)}, f32[1024,128]{1,0:T(8,128)S(1)}, f32[1024,128]{1,0:T(8,128)S(1)}) custom-call(s32[16]{0:T(128)S(1)} %copy-done.15, s32[1]{0:T(128)} %bitcast.6.start_ref, bf16[16,64,128]{2,1,0:T(8,128)(2,1)S(1)} %bitcast.39, bf16[16,128,512]{2,1,0:T(8,128)(2,1)S(1)} %copy-done.1, bf16[16,128,512]{2,1,0:T(8,128)(2,1)S(1)} %copy-done.2), custom_call_target="tpu_custom_call" | custom-call | flops 70000000 | bytes 6000000 | tf_op jit(solution)/shard_map/resident/pallas_call | solution.py:244
  32.9 0.8 copy-done.8
  33.6 0.8 copy-done.10
  34.4 6.8 %all-gather.2.cloned.1.call-done.pages_ref = bf16[8,256,512]{2,1,0:T(8,128)(2,1)} async-done(((bf16[1,256,512]{2,1,0:T(8,128)(2,1)}), bf16[8,256,512]{2,1,0:T(8,128)(2,1)}) %all-gather.2.cloned.1.call-update) | async-done | bytes 2097168 | tf_op jit(solution)/shard_map/all_gather | solution.py:223
  41.2 1.6 %copy-done.4 = bf16[8,256,512]{2,1,0:T(8,128)(2,1)S(1)} copy-done((bf16[8,256,512]{2,1,0:T(8,128)(2,1)S(1)}, bf16[8,256,512]{2,1,0:T(8,128)(2,1)}, u32[]{:S(2)}) %copy-start.4) | copy-done | bytes 2097176
  42.8 1.0 copy-done.9
  43.8 1.0 copy-done.11
  44.9 4.0 %recalled.1 = bf16[32,48,128]{2,1,0:T(8,128)(2,1)S(1)} custom-call(bf16[32,16,128]{2,1,0:T(8,128)(2,1)S(1)} %all-to-all-done.lists_ref, bf16[1024,128]{1,0:T(8,128)(2,1)S(1)} %bitcast.43, bf16[8,256,512]{2,1,0:T(8,128)(2,1)S(1)} %copy-done.4, f32[1024,128]{1,0:T(8,128)S(1)} %get-tuple-element.14.out_res_ref, f32[1024,128]{1,0:T(8,128)S(1)} %copy-done.9, ...), custom_call_target="tpu_custom_call" | custom-call | flops 550000000 | bytes 5000000 | tf_op jit(solution)/shard_map/recalled/pallas_call | solution.py:262
  48.9 21.1 %all_to_all.25.parts_ref = bf16[32,48,128]{2,1,0:T(8,128)(2,1)S(1)} all-to-all(bf16[32,48,128]{2,1,0:T(8,128)(2,1)S(1)} %recalled.1), channel_id=1, replica_groups=mesh['y'=4,'core'=2,'x'=4,'z'=8] {'x','z'}, dimensions={0} | all-to-all | bytes 786432 | tf_op jit(solution)/shard_map/all_to_all | solution.py:279
  70.1 1.4 project.1
  71.5 7.6 %all-to-all-start.2 = ((bf16[32,16,128]{2,1,0:T(8,128)(2,1)}), bf16[32,16,128]{2,1,0:T(8,128)(2,1)S(1)}, u32[]{:S(2)}, u32[]{:S(2)}) async-start(bf16[32,16,128]{2,1,0:T(8,128)(2,1)} %project.1), calls=%async_computation.2 | async-start | bytes 262144 | tf_op jit(solution)/shard_map/all_to_all | solution.py:288
  79.1 9.1 %all-to-all-done.2.sums_ref = bf16[32,16,128]{2,1,0:T(8,128)(2,1)S(1)} async-done(((bf16[32,16,128]{2,1,0:T(8,128)(2,1)}), bf16[32,16,128]{2,1,0:T(8,128)(2,1)S(1)}, u32[]{:S(2)}, u32[]{:S(2)}) %all-to-all-start.2) | async-done | bytes 131104 | tf_op jit(solution)/shard_map/all_to_all | solution.py:288
  88.3 0.9 copy-done.13
  89.2 0.2 dispatch.1
  89.4 23.5 %all_to_all.26 = bf16[256,4,128]{2,1,0:T(4,128)(2,1)S(1)} all-to-all(bf16[256,4,128]{2,1,0:T(4,128)(2,1)S(1)} %bitcast.47), channel_id=1, replica_groups=mesh['y'=4,'core'=2,'x'=4,'z'=8] {'y','core','x','z'}, dimensions={0} | all-to-all | bytes 524288 | tf_op jit(solution)/shard_map/all_to_all | solution.py:298
  112.9 0.0 copy-start.7
  112.9 1.4 copy-done.7
  114.3 2.0 %experts.1 = bf16[1024,128]{1,0:T(8,128)(2,1)S(1)} custom-call(bf16[1024,128]{1,0:T(8,128)(2,1)S(1)} %bitcast.44, f32[1,4096]{1,0:T(1,128)S(1)} %bitcast.48, bf16[192,4096]{1,0:T(8,128)(2,1)S(1)} %bitcast.40, bf16[192,4096]{1,0:T(8,128)(2,1)S(1)} %bitcast.41, bf16[192,4096]{1,0:T(8,128)(2,1)S(1)} %bitcast.42), custom_call_target="tpu_custom_call" | custom-call | flops 160000000 | bytes 5300000 | tf_op jit(solution)/shard_map/experts/pallas_call | solution.py:300
  116.3 20.9 %all_to_all.27 = bf16[256,4,128]{2,1,0:T(4,128)(2,1)S(1)} all-to-all(bf16[256,4,128]{2,1,0:T(4,128)(2,1)S(1)} %bitcast.45), channel_id=1, replica_groups=mesh['y'=4,'core'=2,'x'=4,'z'=8] {'y','core','x','z'}, dimensions={0} | all-to-all | bytes 524288 | tf_op jit(solution)/shard_map/all_to_all | solution.py:308
  137.2 0.8 combine.1
  (24 shorter events, 0.1 us)
Async XLA Ops:
  6.5 72.6 %copy-start = (bf16[16,4096]{1,0:T(8,128)(2,1)S(1)}, bf16[16,4096]{1,0:T(8,128)(2,1)}, u32[]{:S(2)}) copy-start(bf16[16,4096]{1,0:T(8,128)(2,1)} %param.23) | copy-start | bytes 393220
  6.5 19.3 %copy-start.1 = (bf16[16,128,512]{2,1,0:T(8,128)(2,1)S(1)}, bf16[16,128,512]{2,1,0:T(8,128)(2,1)}, u32[]{:S(2)}) copy-start(bf16[16,128,512]{2,1,0:T(8,128)(2,1)} %k_ref.1) | copy-start | bytes 6291460
  6.5 19.3 %copy-start.15 = (s32[16]{0:T(128)S(1)}, s32[16]{0:T(128)}, u32[]{:S(2)}) copy-start(s32[16]{0:T(128)} %length_ref.1) | copy-start | bytes 196
  6.5 34.7 %all-gather.2.cloned.1.call-start = ((), (), s32[]{:S(2)}) async-start(), calls=%async_computation.5 | async-start | bytes 2359296 | tf_op jit(solution)/shard_map/all_gather | solution.py:223
  12.0 0.7 copy-start.12
  12.7 21.7 %all-to-all-start = ((bf16[32,16,128]{2,1,0:T(8,128)(2,1)}), bf16[32,16,128]{2,1,0:T(8,128)(2,1)S(1)}, u32[]{:S(2)}, u32[]{:S(2)}) async-start(bf16[32,16,128]{2,1,0:T(8,128)(2,1)} %get-tuple-element.13), calls=%async_computation | async-start | bytes 262144 | tf_op jit(solution)/shard_map/all_to_all | solution.py:238
  25.8 1.6 %copy-start.2 = (bf16[16,128,512]{2,1,0:T(8,128)(2,1)S(1)}, bf16[16,128,512]{2,1,0:T(8,128)(2,1)}, u32[]{:S(2)}) copy-start(bf16[16,128,512]{2,1,0:T(8,128)(2,1)} %v_ref.1) | copy-start | bytes 6291460
  32.8 0.8 copy-start.8
  33.6 0.8 copy-start.10
  41.2 1.6 %copy-start.4 = (bf16[8,256,512]{2,1,0:T(8,128)(2,1)S(1)}, bf16[8,256,512]{2,1,0:T(8,128)(2,1)}, u32[]{:S(2)}) copy-start(bf16[8,256,512]{2,1,0:T(8,128)(2,1)} %all-gather.2.cloned.1.call-done.pages_ref) | copy-start | bytes 6291460
  42.8 1.0 copy-start.9
  43.8 1.0 copy-start.11
  44.9 25.2 %copy-start.3 = (bf16[256,4096]{1,0:T(8,128)(2,1)S(1)}, bf16[256,4096]{1,0:T(8,128)(2,1)}, u32[]{:S(2)}) copy-start(bf16[256,4096]{1,0:T(8,128)(2,1)} %weight_ref.1) | copy-start | bytes 6291460
  48.9 64.0 %copy-start.14 = (f32[4096]{0:T(1024)S(1)}, f32[4096]{0:T(1024)}, u32[]{:S(2)}) copy-start(f32[4096]{0:T(1024)} %param.24) | copy-start | bytes 49156
  70.1 42.9 %copy-start.5 = (bf16[1,192,4096]{2,1,0:T(8,128)(2,1)S(1)}, bf16[1,192,4096]{2,1,0:T(8,128)(2,1)}, u32[]{:S(2)}) copy-start(bf16[1,192,4096]{2,1,0:T(8,128)(2,1)} %param.27) | copy-start | bytes 4718596
  70.1 42.9 %copy-start.6 = (bf16[1,192,4096]{2,1,0:T(8,128)(2,1)S(1)}, bf16[1,192,4096]{2,1,0:T(8,128)(2,1)}, u32[]{:S(2)}) copy-start(bf16[1,192,4096]{2,1,0:T(8,128)(2,1)} %param.28) | copy-start | bytes 4718596
  71.5 16.8 %all-to-all-start.2 = ((bf16[32,16,128]{2,1,0:T(8,128)(2,1)}), bf16[32,16,128]{2,1,0:T(8,128)(2,1)S(1)}, u32[]{:S(2)}, u32[]{:S(2)}) async-start(bf16[32,16,128]{2,1,0:T(8,128)(2,1)} %project.1), calls=%async_computation.2 | async-start | bytes 262144 | tf_op jit(solution)/shard_map/all_to_all | solution.py:288
  88.3 1.0 copy-start.13
  112.9 1.4 copy-start.7
Sparse Core Ops, SparseCore 0:
  9.2 31.9 all-gather.1

commit v2 on v1

v2 whole, which is shorter than its diff:
```python
import functools

import jax
import jax.numpy as jnp
from jax import lax
from jax.experimental import pallas as pl
from jax.experimental.pallas import tpu as pltpu
from jax.sharding import Mesh, PartitionSpec as P

HEADS = 64
KV = 4
HPK = HEADS // KV
HW = 128
T = 16
D = 4096
NC = 32
NG = 8
CAPE = 4
FP = 192
TOK = 8
SLOTS = 16
EPS = 1e-06
NEG = -(2.0**100)
SCALE = HW**-0.5
BF = jnp.bfloat16
F32 = jnp.float32
GRP = ("y", "core")
CTX = ("x", "z")
ALL = GRP + CTX
NT = (((1,), (1,)), ((), ()))
STAT_ROWS = 16
EACH = 4
CHUNK = 2 * T + STAT_ROWS


def params(mib):
    return pltpu.CompilerParams(vmem_limit_bytes=mib * 2**20)


def cost(flops, moved, exps=0):
    return pl.CostEstimate(flops=flops, bytes_accessed=moved, transcendentals=exps)


def lists_kernel(key_ref, lists_ref):
    key = key_ref[...]
    lane = lax.broadcasted_iota(jnp.int32, (T, 128), 1)
    columns = [jnp.broadcast_to(key[:, j : j + 1], (T, 128)) - lane for j in range(key.shape[1])]
    for c in range(NC):
        hits = [column == c * 128 for column in columns]
        while len(hits) > 1:
            hits = [hits[i] | hits[i + 1] for i in range(0, len(hits), 2)]
        lists_ref[c] = jnp.where(hits[0], 1.0, 0.0).astype(BF)


def prepare_kernel(ids_ref, weights_ref, picker_ref, combine_ref):
    rows = NG * NC * CAPE
    one = (lax.broadcasted_iota(jnp.int32, (T, T), 1) == lax.broadcasted_iota(jnp.int32, (T, T), 0)).astype(F32)
    exact = dict(preferred_element_type=F32, precision=lax.Precision.HIGHEST)
    ids = lax.dot_general(one, ids_ref[...].astype(F32), NT, **exact)
    weights = lax.dot_general(one, weights_ref[...], NT, **exact)
    place = lax.broadcasted_iota(jnp.int32, (T, rows), 1)
    expert = (place // 16).astype(F32)
    slot = (place % CAPE).astype(F32)
    taken = jnp.zeros((T, rows), F32)
    coefficient = jnp.zeros((T, rows), F32)
    for j in range(ids_ref.shape[0]):
        hit = jnp.abs(jnp.broadcast_to(ids[:, j : j + 1], (T, rows)) - expert) < 0.5
        taken = taken + jnp.where(hit, 1.0, 0.0)
        coefficient = coefficient + jnp.where(hit, jnp.broadcast_to(weights[:, j : j + 1], (T, rows)), 0.0)
    before = (lax.broadcasted_iota(jnp.int32, (T, T), 1) < lax.broadcasted_iota(jnp.int32, (T, T), 0)).astype(F32)
    order = jnp.dot(before.astype(BF), taken.astype(BF), preferred_element_type=F32)
    hit = jnp.where((taken > 0.5) & (order == slot), 1.0, 0.0)
    picker_ref[...] = hit.astype(BF)
    table = hit * coefficient
    high = table.astype(BF)
    combine_ref[:T] = high
    combine_ref[T:] = (table - high.astype(F32)).astype(BF)


def resident_kernel(length_ref, start_ref, q, k, v, out_ref, stats_ref, wide):
    steps = k.shape[0] // EACH
    for h in range(HEADS):
        head = q[:, h * HW : (h + 1) * HW]
        wide[h * T : (h + 1) * T, :] = head.astype(F32)

    position = lax.broadcasted_iota(jnp.int32, (HEADS, 128), 1) + start_ref[0]
    lane = lax.broadcasted_iota(jnp.int32, (HEADS, 128), 1)
    pairs = [(i, g) for i in range(EACH) for g in range(KV)]

    @pl.loop(0, steps)
    def _(step):
        base = step * EACH
        own = [wide[pl.ds(base + i, HEADS, stride=T), :].astype(BF) for i in range(EACH)]
        scores = [
            lax.dot_general(
                own[i][g * HPK : (g + 1) * HPK], k[base + i, :, g * HW : (g + 1) * HW], NT, preferred_element_type=F32
            )
            for i, g in pairs
        ]
        scores = jnp.concatenate(scores, axis=0).reshape(EACH, HEADS, 128)
        valid = [position < length_ref[base + i] for i in range(EACH)]
        scores = jnp.stack([jnp.where(valid[i], scores[i] * SCALE, NEG) for i in range(EACH)])
        peak = jnp.max(scores, axis=2, keepdims=True)
        chances = jnp.exp(scores - peak)
        chances = jnp.stack([jnp.where(valid[i], chances[i], 0.0) for i in range(EACH)])
        total = jnp.sum(chances, axis=2, keepdims=True)
        rounded = chances.astype(BF)
        out = [
            jnp.dot(
                rounded[i, g * HPK : (g + 1) * HPK],
                v[base + i, :, g * HW : (g + 1) * HW],
                preferred_element_type=F32,
            )
            for i, g in pairs
        ]
        for i in range(EACH):
            here = pl.ds(base + i, HEADS, stride=T)
            out_ref[here, :] = jnp.concatenate(out[i * KV : (i + 1) * KV], axis=0)
            stats_ref[here, :] = jnp.where(lane < 64, peak[i], total[i])


def recalled_kernel(half, lists_ref, q_ref, *refs):
    pages, (out_ref, stats_ref, *given) = refs[: NG // 2], refs[NG // 2 :]
    rows = HPK * T
    tokens = len(pages) * SLOTS * TOK
    counts = jnp.sum(lists_ref[...].astype(F32), axis=0).astype(BF)
    spread = (
        lax.broadcasted_iota(jnp.int32, (128, tokens), 1) // TOK + half * (tokens // TOK)
        == lax.broadcasted_iota(jnp.int32, (128, tokens), 0)
    ).astype(F32)
    times = jnp.dot(counts, spread.astype(BF), preferred_element_type=F32)
    bias = jnp.where(times > 0.5, 0.0, NEG)[None]
    times = times[None]
    lanes = lax.broadcasted_iota(jnp.int32, (rows, 128), 1)
    kind = lanes % 4
    lane = lax.broadcasted_iota(jnp.int32, (HPK // 2, T, 128), 2)
    for g in range(KV):
        own = slice(g * rows, (g + 1) * rows)
        columns = slice(g * HW, (g + 1) * HW)
        keys, values = [
            jnp.concatenate([ref[p, m, :, columns] for ref in pages for p in range(SLOTS)], axis=0) for m in range(2)
        ]
        heads = range(g * HPK, (g + 1) * HPK)
        queries = jnp.concatenate([q_ref[:, h * HW : (h + 1) * HW] for h in heads], axis=0)
        scores = lax.dot_general(queries, keys, NT, preferred_element_type=F32)
        scores = scores.reshape(HPK, T, tokens) * SCALE + bias
        stats = stats_ref[own, :]
        before = jnp.broadcast_to(stats[:, :1], (rows, 128))
        peak = jnp.max(scores, axis=2, keepdims=True).reshape(rows, 1)
        peak = jnp.maximum(jnp.broadcast_to(peak, (rows, 128)), before)
        if half:
            peak_high = peak.astype(BF).astype(F32)
            peak_low = (peak - peak_high).astype(BF).astype(F32)
            base = peak_high + peak_low
        else:
            base = peak
        weights = jnp.exp(scores - base[:, :1].reshape(HPK, T, 1)) * times
        total = jnp.sum(weights, axis=2, keepdims=True).reshape(rows, 1)
        out = jnp.dot(weights.reshape(rows, tokens).astype(BF), values, preferred_element_type=F32)
        factor = jnp.exp(before - base)
        out = out + factor * out_ref[own, :]
        total = jnp.broadcast_to(total, (rows, 128)) + factor * jnp.broadcast_to(stats[:, 64:65], (rows, 128))
        if not half:
            given[0][own, :] = out
            given[1][own, :] = jnp.where(lanes < 64, base, total)
            continue
        total_high = total.astype(BF).astype(F32)
        stats = jnp.where(
            kind == 0, peak_high, jnp.where(kind == 1, peak_low, jnp.where(kind == 2, total_high, total - total_high))
        ).reshape(HPK // 2, 2, T, 128)
        here = slice(g * (HPK // 2), (g + 1) * (HPK // 2))
        given[0][here, : 2 * T, :] = out.reshape(HPK // 2, 2 * T, 128).astype(BF)
        given[0][here, 2 * T :, :] = jnp.where(lane < 4, stats[:, 0], stats[:, 1]).astype(BF)


def project_kernel(parts_ref, weight_ref, send_ref):
    stats = parts_ref[:, 2 * T :, :].astype(F32)
    heads = []
    for i in range(2):
        peak = stats[:, :, 4 * i : 4 * i + 1] + stats[:, :, 4 * i + 1 : 4 * i + 2]
        total = stats[:, :, 4 * i + 2 : 4 * i + 3] + stats[:, :, 4 * i + 3 : 4 * i + 4]
        factor = jnp.exp(peak - jnp.max(peak, axis=0, keepdims=True))
        total = jnp.sum(factor * total, axis=0)
        out = jnp.sum(factor * parts_ref[:, i * T : (i + 1) * T, :].astype(F32), axis=0)
        heads.append((out / total).astype(BF))
    attention = jnp.concatenate(heads, axis=1)
    wide = 512
    for j in range(D // wide):
        block = jnp.dot(attention, weight_ref[:, j * wide : (j + 1) * wide], preferred_element_type=F32).astype(BF)
        for i in range(wide // 128):
            send_ref[j * (wide // 128) + i] = block[:, i * 128 : (i + 1) * 128]


def dispatch_kernel(sums_ref, residual_ref, picker_ref, hidden_ref, send_ref):
    hidden = residual_ref[...].astype(F32) + jnp.sum(sums_ref[...].astype(F32), axis=0)
    hidden_ref[...] = hidden
    send_ref[...] = lax.dot_general(
        picker_ref[...], hidden.astype(BF), (((0,), (0,)), ((), ())), preferred_element_type=F32
    ).astype(BF)


def expert_kernel(rows_ref, gain_ref, gate_ref, up_ref, down_hbm, send_ref, wide_ref, token_ref, down_ref, sem):
    late = pltpu.make_async_copy(down_hbm, down_ref, sem)
    late.start()
    wide_ref[...] = rows_ref[...].astype(F32)
    for c in range(NC):
        for s in range(CAPE):
            token_ref[s * NG : (s + 1) * NG, c * 128 : (c + 1) * 128] = wide_ref[pl.ds(c * CAPE + s, NG, stride=128), :]
    hidden = token_ref[...]
    normed = (hidden * lax.rsqrt(jnp.mean(hidden * hidden, axis=1, keepdims=True) + EPS) * gain_ref[...]).astype(BF)
    gate = lax.dot_general(normed, gate_ref[...], NT, preferred_element_type=F32)
    up = lax.dot_general(normed, up_ref[...], NT, preferred_element_type=F32)
    act = (gate / (1.0 + jnp.exp(-gate)) * up).astype(BF)
    wide = 512
    late.wait()
    for j in range(D // wide):
        block = jnp.dot(act, down_ref[:, j * wide : (j + 1) * wide], preferred_element_type=F32)
        for i in range(wide // 128):
            for s in range(CAPE):
                wide_ref[pl.ds((j * (wide // 128) + i) * CAPE + s, NG, stride=128), :] = block[
                    s * NG : (s + 1) * NG, i * 128 : (i + 1) * 128
                ]
    send_ref[...] = wide_ref[...].astype(BF)


def combine_kernel(rows_ref, table_ref, hidden_ref, out_ref):
    both = jnp.dot(table_ref[...], rows_ref[...], preferred_element_type=F32)
    out_ref[...] = (hidden_ref[...] + both[:T] + both[T:]).astype(BF)


def shards(
    queries,
    resident_key_cache,
    resident_value_cache,
    res_len,
    visual_page_pool,
    recall_holder,
    recall_slot,
    o_weight,
    residual,
    norm_gain,
    expert_ids,
    expert_weights,
    w_gate,
    w_up,
    w_down,
):
    ctx_index = lax.axis_index(CTX)
    rows = NG * NC * CAPE

    smem = pl.BlockSpec(memory_space=pltpu.SMEM)
    vmem = pl.BlockSpec(memory_space=pltpu.VMEM)
    hbm = pl.BlockSpec(memory_space=pltpu.HBM)
    pages = [visual_page_pool]
    for k in range(1, 4):
        pages.append(lax.ppermute(visual_page_pool, "y", [(i, (i + k) % 4) for i in range(4)]))
    pages += [lax.ppermute(part, "core", [(0, 1), (1, 0)]) for part in pages]

    holder = recall_holder[0]
    group = holder // NC
    back = (lax.axis_index("y") + 4 - group // 2) % 4
    near = jnp.where(group % 2 == lax.axis_index("core"), back, back + 4)
    key = (holder % NC) * 128 + near * SLOTS + recall_slot[0]
    lists = pl.pallas_call(
        lists_kernel,
        out_shape=jax.ShapeDtypeStruct((NC, T, 128), BF),
        compiler_params=params(4),
        cost_estimate=cost(4_000_000, 140_000),
        name="lists",
    )(key)
    lists = lax.all_to_all(lists, CTX, split_axis=0, concat_axis=0, tiled=True)

    wide = jax.ShapeDtypeStruct((HEADS * T, 128), F32)
    out, stats = pl.pallas_call(
        resident_kernel,
        in_specs=[smem, smem, vmem, vmem, vmem],
        out_shape=(wide, wide),
        scratch_shapes=[pltpu.VMEM((HEADS * T, HW), F32)],
        compiler_params=params(12),
        cost_estimate=cost(70_000_000, 6_000_000, 131_072),
        name="resident",
    )(res_len, (ctx_index * 128).reshape(1).astype(jnp.int32), queries, resident_key_cache, resident_value_cache)

    for half in range(2):
        last = half == 1
        result = pl.pallas_call(
            functools.partial(recalled_kernel, half),
            out_shape=jax.ShapeDtypeStruct((NC, CHUNK, 128), BF) if last else (wide, wide),
            compiler_params=params(16),
            cost_estimate=cost(270_000_000, 4_000_000, 524_288),
            name="recalled",
        )(lists, queries, *pages[half * 4 : half * 4 + 4], out, stats)
        if not last:
            out, stats = result
    parts = result
    parts = lax.all_to_all(parts, CTX, split_axis=0, concat_axis=0, tiled=True)

    sums = pl.pallas_call(
        project_kernel,
        out_shape=jax.ShapeDtypeStruct((NC, T, 128), BF),
        compiler_params=params(8),
        cost_estimate=cost(40_000_000, 2_700_000, 2048),
        name="project",
    )(parts, o_weight)
    ids, chances, _ = lax.optimization_barrier((expert_ids.T, expert_weights.T, sums))
    picker, table = pl.pallas_call(
        prepare_kernel,
        out_shape=(jax.ShapeDtypeStruct((T, rows), BF), jax.ShapeDtypeStruct((2 * T, rows), BF)),
        compiler_params=params(4),
        cost_estimate=cost(4_000_000, 200_000),
        name="prepare",
    )(ids, chances)
    sums = lax.all_to_all(sums, CTX, split_axis=0, concat_axis=0, tiled=True)

    own_residual = lax.dynamic_slice_in_dim(residual, ctx_index * 128, 128, 1)
    hidden, send = pl.pallas_call(
        dispatch_kernel,
        out_shape=(jax.ShapeDtypeStruct((T, 128), F32), jax.ShapeDtypeStruct((rows, 128), BF)),
        compiler_params=params(8),
        cost_estimate=cost(4_000_000, 500_000),
        name="dispatch",
    )(sums, own_residual, picker)
    arrived = lax.all_to_all(send.reshape(NG * NC, CAPE, 128), ALL, split_axis=0, concat_axis=0, tiled=True)

    results = pl.pallas_call(
        expert_kernel,
        in_specs=[vmem, vmem, vmem, vmem, hbm],
        out_shape=jax.ShapeDtypeStruct((rows, 128), BF),
        scratch_shapes=[pltpu.VMEM((rows, 128), F32), pltpu.VMEM((NG * CAPE, D), F32), pltpu.VMEM((FP, D), BF), pltpu.SemaphoreType.DMA(())],
        compiler_params=params(12),
        cost_estimate=cost(160_000_000, 5_300_000, 8192),
        name="experts",
    )(arrived.reshape(rows, 128), norm_gain.reshape(1, D), w_gate[0], w_up[0], w_down[0])
    returned = lax.all_to_all(results.reshape(NG * NC, CAPE, 128), ALL, split_axis=0, concat_axis=0, tiled=True)

    return pl.pallas_call(
        combine_kernel,
        out_shape=jax.ShapeDtypeStruct((T, 128), BF),
        compiler_params=params(8),
        cost_estimate=cost(8_000_000, 400_000),
        name="combine",
    )(returned.reshape(rows, 128), table, hidden)


def solution(mesh):
    fine = Mesh(mesh.devices.reshape(4, 2, 4, 8), ALL)
    placed = (
        P(GRP, None),
        P(GRP, CTX, None),
        P(GRP, CTX, None),
        P(GRP),
        P(ALL, None, None, None),
        P(CTX, GRP, None),
        P(CTX, GRP, None),
        P(CTX, None),
        P(GRP, None),
        P(),
        P(GRP, None),
        P(GRP, None),
        P(ALL, None, None),
        P(ALL, None, None),
        P(ALL, None, None),
    )
    return jax.shard_map(shards, mesh=fine, in_specs=placed, out_specs=P(GRP, CTX), check_vma=False)
```

time: 146 us -> 123 us (0.84)
  between operations: 13.6 us -> 0.22 us
  local copies, waits for them, and re-layouts: 14.5 us -> 6.25 us
  starting transfers between devices: 19.5 us -> 26.9 us
  waiting for transfers between devices: 15.9 us -> 8.72 us
    ppermute x0 -> x7, starting transfers between devices: none -> 8.32 us  [the longest x3 5.81 us: shards(): lax.ppermute(visual_page_pool, 'y', [(i, (i + k) % 4) for i in range(4)])]
    all_gather x1 -> x0, waiting for transfers between devices: 6.78 us -> none  [shards(): pages = lax.all_gather(own_pages, GRP)]
    unnamed x35 -> x28, local copies, waits for them, and re-layouts: 12.5 us -> 6.24 us
    transpose x2 -> x0, local copies, waits for them, and re-layouts: 1.99 us -> none  [the longest x1 1.82 us: shards(): jnp.swapaxes(visual_page_pool, 0, 1).reshape(2 * SLOTS * TOK, KV * HW)]
    pallas_call x4 -> x6, Pallas kernels: 12.8 us -> 11.8 us  [the longest x2 4.99 us: shards(): pl.pallas_call(functools.partial(recalled_kernel, half), out_shape=jax.Sh...]
  transfers between devices with their start and end apart: 3 -> 9, of which waited for: 2 -> 1; matrix products, arithmetic and copies ran while one was open for 2% -> 1% of each run, Pallas kernels for 5% -> 5%
where the time goes in v2:
time: 123 us; the launch traced here: 122 us
  blocking collectives  65.4 us (53%)
  starting transfers between devices  26.9 us (22%)
  Pallas kernels  14.2 us (12%)
  waiting for transfers between devices  8.72 us (7%)
  local copies, waits for them, and re-layouts  6.25 us (5%)
    all_to_all x1, blocking collectives, shards(): lax.all_to_all(send.reshape(NG * NC, CAPE, 128), ALL, split_axis=0, conca...  23.1 us
    all_to_all x1, blocking collectives, shards(): parts = lax.all_to_all(parts, CTX, split_axis=0, concat_axis=0, tiled=True)  21.3 us
    all_to_all x1, blocking collectives, shards(): lax.all_to_all(results.reshape(NG * NC, CAPE, 128), ALL, split_axis=0, co...  20.9 us
    all_to_all x1, starting transfers between devices, shards(): lists = lax.all_to_all(lists, CTX, split_axis=0, concat_axis=0, tiled=True)  11 us
    all_to_all x1, waiting for transfers between devices, shards(): sums = lax.all_to_all(sums, CTX, split_axis=0, concat_axis=0, tiled=True)  8.69 us
    all_to_all x1, starting transfers between devices, shards(): sums = lax.all_to_all(sums, CTX, split_axis=0, concat_axis=0, tiled=True)  7.58 us
    unnamed x28, local copies, waits for them, and re-layouts  6.24 us
    ppermute x3, starting transfers between devices, shards(): lax.ppermute(visual_page_pool, 'y', [(i, (i + k) % 4) for i in range(4)])  5.81 us
  transfers between devices with their start and end apart: 9, of which 1 were waited for; matrix products, arithmetic and copies ran while one was open for 1% of the time, Pallas kernels for 5%

profile of v2, /device:TPU:1, one launch (start us, length us, event | category | flops | bytes accessed | tf_op | source)
XLA Modules:
  0.0 122.5 jit_solution(4549302148141181150)
XLA Ops:
  0.0 2.1 %collective-permute-start.1 = (bf16[16,2,8,512]{3,2,1,0:T(8,128)(2,1)}, bf16[16,2,8,512]{3,2,1,0:T(8,128)(2,1)S(1)}, u32[]{:S(2)}, u32[]{:S(2)}) collective-permute-start(bf16[16,2,8,512]{3,2,1,0:T(8,128)(2,1)} %refs_0_.1), channel_id=1, source_target_pairs={{0,64},{64,128},{128,192},{192,0},{1,65},{65,129},{129,193},{193,1... | collective-permute-start | bytes 786440 | tf_op jit(solution)/shard_map/ppermute | solution.py:256
  2.1 2.6 %collective-permute-start.3 = (bf16[16,2,8,512]{3,2,1,0:T(8,128)(2,1)}, bf16[16,2,8,512]{3,2,1,0:T(8,128)(2,1)S(1)}, u32[]{:S(2)}, u32[]{:S(2)}) collective-permute-start(bf16[16,2,8,512]{3,2,1,0:T(8,128)(2,1)} %refs_0_.1), channel_id=1, source_target_pairs={{0,128},{64,192},{128,0},{192,64},{1,129},{65,193},{129,1},{193,65... | collective-permute-start | bytes 786440 | tf_op jit(solution)/shard_map/ppermute | solution.py:256
  4.8 1.1 collective-permute-start.5
  5.8 0.7 fusion.2.key_ref
  6.6 1.3 %lists.1 = bf16[32,16,128]{2,1,0:T(8,128)(2,1)} custom-call(s32[16,16]{1,0:T(8,128)S(1)} %fusion.2.key_ref), custom_call_target="tpu_custom_call" | custom-call | flops 4000000 | bytes 140000 | tf_op jit(solution)/shard_map/lists/pallas_call | solution.py:264
  7.8 11.0 %all-to-all-start = ((bf16[32,16,128]{2,1,0:T(8,128)(2,1)}), bf16[32,16,128]{2,1,0:T(8,128)(2,1)S(1)}, u32[]{:S(2)}, u32[]{:S(2)}) async-start(bf16[32,16,128]{2,1,0:T(8,128)(2,1)} %lists.1), calls=%async_computation | async-start | bytes 262144 | tf_op jit(solution)/shard_map/all_to_all | solution.py:271
  18.9 1.9 %collective-permute-start = (bf16[16,2,8,512]{3,2,1,0:T(8,128)(2,1)}, bf16[16,2,8,512]{3,2,1,0:T(8,128)(2,1)S(1)}, u32[]{:S(2)}, u32[]{:S(2)}) collective-permute-start(bf16[16,2,8,512]{3,2,1,0:T(8,128)(2,1)} %refs_0_.1), channel_id=1, source_target_pairs={{0,32},{32,0},{1,33},{33,1},{2,34},{34,2},{3,35},{35,3},{4,36},{36... | collective-permute-start | bytes 786440 | tf_op jit(solution)/shard_map/ppermute | solution.py:257
  20.7 0.1 collective-permute-start.2
  20.9 0.4 collective-permute-start.4
  21.3 0.1 collective-permute-start.6
  21.4 0.9 copy-done.1
  22.3 1.6 %copy-done.3 = bf16[16,128,512]{2,1,0:T(8,128)(2,1)S(1)} copy-done((bf16[16,128,512]{2,1,0:T(8,128)(2,1)S(1)}, bf16[16,128,512]{2,1,0:T(8,128)(2,1)}, u32[]{:S(2)}) %copy-start.3) | copy-done | bytes 2097176
  23.9 1.6 %copy-done.4 = bf16[16,128,512]{2,1,0:T(8,128)(2,1)S(1)} copy-done((bf16[16,128,512]{2,1,0:T(8,128)(2,1)S(1)}, bf16[16,128,512]{2,1,0:T(8,128)(2,1)}, u32[]{:S(2)}) %copy-start.4) | copy-done | bytes 2097176
  25.5 0.7 copy-done.11
  26.2 3.0 %resident.1 = (f32[1024,128]{1,0:T(8,128)S(1)}, f32[1024,128]{1,0:T(8,128)S(1)}) custom-call(s32[16]{0:T(128)S(1)} %copy-done.11, s32[1]{0:T(128)} %bitcast.2.start_ref, bf16[16,8192]{1,0:T(8,128)(2,1)S(1)} %copy-done.1, bf16[16,128,512]{2,1,0:T(8,128)(2,1)S(1)} %copy-done.3, bf16[16,128,512]{2,1,0:T(8,128)(2,1)S(1)} %copy-done.4), custom_call_target="tpu_custom_call" | custom-call | flops 70000000 | bytes 6000000 | tf_op jit(solution)/shard_map/resident/pallas_call | solution.py:274
  29.1 0.0 all-to-all-done.lists_ref
  29.2 1.9 %recalled.2 = (f32[1024,128]{1,0:T(8,128)S(1)}, f32[1024,128]{1,0:T(8,128)S(1)}) custom-call(bf16[32,16,128]{2,1,0:T(8,128)(2,1)S(1)} %all-to-all-done.lists_ref, bf16[16,8192]{1,0:T(8,128)(2,1)S(1)} %copy-done.2, bf16[16,2,8,512]{3,2,1,0:T(8,128)(2,1)S(1)} %copy-done.9, bf16[16,2,8,512]{3,2,1,0:T(8,128)(2,1)S(1)} %collective-permute-done.1.refs_1_, ...), custom_call_target="tpu_custom_call" | custom-call | flops 270000000 | bytes 4000000 | tf_op jit(solution)/shard_map/recalled/pallas_call | solution.py:286
  31.1 3.1 %recalled.3 = bf16[32,48,128]{2,1,0:T(8,128)(2,1)S(1)} custom-call(bf16[32,16,128]{2,1,0:T(8,128)(2,1)S(1)} %all-to-all-done.lists_ref, bf16[16,8192]{1,0:T(8,128)(2,1)S(1)} %copy-done.2, bf16[16,2,8,512]{3,2,1,0:T(8,128)(2,1)S(1)} %collective-permute-done.refs_0_, bf16[16,2,8,512]{3,2,1,0:T(8,128)(2,1)S(1)} %collective-permute-done.2.refs_1_, ...), custom_call_target="tpu_custom_call" | custom-call | flops 270000000 | bytes 4000000 | tf_op jit(solution)/shard_map/recalled/pallas_call | solution.py:286
  34.2 0.0 copy-start.12
  34.3 0.0 copy-start.13
  34.3 0.0 copy-start.10
  34.3 21.3 %all_to_all.25.parts_ref = bf16[32,48,128]{2,1,0:T(8,128)(2,1)S(1)} all-to-all(bf16[32,48,128]{2,1,0:T(8,128)(2,1)S(1)} %recalled.3), channel_id=1, replica_groups=mesh['y'=4,'core'=2,'x'=4,'z'=8] {'x','z'}, dimensions={0} | all-to-all | bytes 786432 | tf_op jit(solution)/shard_map/all_to_all | solution.py:296
  55.6 1.4 %project.1 = bf16[32,16,128]{2,1,0:T(8,128)(2,1)} custom-call(bf16[32,48,128]{2,1,0:T(8,128)(2,1)S(1)} %all_to_all.25.parts_ref, bf16[256,4096]{1,0:T(8,128)(2,1)S(1)} %copy-done.5), custom_call_target="tpu_custom_call" | custom-call | flops 40000000 | bytes 2700000 | tf_op jit(solution)/shard_map/project/pallas_call | solution.py:298
  57.1 7.6 %all-to-all-start.2 = ((bf16[32,16,128]{2,1,0:T(8,128)(2,1)}), bf16[32,16,128]{2,1,0:T(8,128)(2,1)S(1)}, u32[]{:S(2)}, u32[]{:S(2)}) async-start(bf16[32,16,128]{2,1,0:T(8,128)(2,1)} %project.1), calls=%async_computation.2 | async-start | bytes 262144 | tf_op jit(solution)/shard_map/all_to_all | solution.py:313
  64.7 0.4 prepare.1
  65.1 8.7 %all-to-all-done.2.sums_ref = bf16[32,16,128]{2,1,0:T(8,128)(2,1)S(1)} async-done(((bf16[32,16,128]{2,1,0:T(8,128)(2,1)}), bf16[32,16,128]{2,1,0:T(8,128)(2,1)S(1)}, u32[]{:S(2)}, u32[]{:S(2)}) %all-to-all-start.2) | async-done | bytes 131104 | tf_op jit(solution)/shard_map/all_to_all | solution.py:313
  73.8 0.3 dispatch.1
  74.1 23.1 %all_to_all.26 = bf16[256,4,128]{2,1,0:T(4,128)(2,1)S(1)} all-to-all(bf16[256,4,128]{2,1,0:T(4,128)(2,1)S(1)} %bitcast.37), channel_id=1, replica_groups=mesh['y'=4,'core'=2,'x'=4,'z'=8] {'y','core','x','z'}, dimensions={0} | all-to-all | bytes 524288 | tf_op jit(solution)/shard_map/all_to_all | solution.py:323
  97.3 1.4 %copy-done.8 = bf16[1,192,4096]{2,1,0:T(8,128)(2,1)S(1)} copy-done((bf16[1,192,4096]{2,1,0:T(8,128)(2,1)S(1)}, bf16[1,192,4096]{2,1,0:T(8,128)(2,1)}, u32[]{:S(2)}) %copy-start.8) | copy-done | bytes 1572888
  98.7 2.1 %experts.1 = bf16[1024,128]{1,0:T(8,128)(2,1)S(1)} custom-call(bf16[1024,128]{1,0:T(8,128)(2,1)S(1)} %bitcast.34, f32[1,4096]{1,0:T(1,128)S(1)} %bitcast.38, bf16[192,4096]{1,0:T(8,128)(2,1)S(1)} %bitcast.31, bf16[192,4096]{1,0:T(8,128)(2,1)S(1)} %bitcast.32, bf16[192,4096]{1,0:T(8,128)(2,1)S(1)} %bitcast.33), custom_call_target="tpu_custom_call" | custom-call | flops 160000000 | bytes 5300000 | tf_op jit(solution)/shard_map/experts/pallas_call | solution.py:325
  100.8 20.9 %all_to_all.27 = bf16[256,4,128]{2,1,0:T(4,128)(2,1)S(1)} all-to-all(bf16[256,4,128]{2,1,0:T(4,128)(2,1)S(1)} %bitcast.35), channel_id=1, replica_groups=mesh['y'=4,'core'=2,'x'=4,'z'=8] {'y','core','x','z'}, dimensions={0} | all-to-all | bytes 524288 | tf_op jit(solution)/shard_map/all_to_all | solution.py:334
  121.7 0.8 combine.1
  (28 shorter events, 0.1 us)
Async XLA Ops:
  0.0 64.7 %copy-start = (bf16[16,4096]{1,0:T(8,128)(2,1)S(1)}, bf16[16,4096]{1,0:T(8,128)(2,1)}, u32[]{:S(2)}) copy-start(bf16[16,4096]{1,0:T(8,128)(2,1)} %param.23) | copy-start | bytes 393220
  0.0 20.7 %collective-permute-start.1 = (bf16[16,2,8,512]{3,2,1,0:T(8,128)(2,1)}, bf16[16,2,8,512]{3,2,1,0:T(8,128)(2,1)S(1)}, u32[]{:S(2)}, u32[]{:S(2)}) collective-permute-start(bf16[16,2,8,512]{3,2,1,0:T(8,128)(2,1)} %refs_0_.1), channel_id=1, source_target_pairs={{0,64},{64,128},{128,192},{192,0},{1,65},{65,129},{129,193},{193,1... | collective-permute-start | bytes 786440 | tf_op jit(solution)/shard_map/ppermute | solution.py:256
  2.1 18.7 %collective-permute-start.3 = (bf16[16,2,8,512]{3,2,1,0:T(8,128)(2,1)}, bf16[16,2,8,512]{3,2,1,0:T(8,128)(2,1)S(1)}, u32[]{:S(2)}, u32[]{:S(2)}) collective-permute-start(bf16[16,2,8,512]{3,2,1,0:T(8,128)(2,1)} %refs_0_.1), channel_id=1, source_target_pairs={{0,128},{64,192},{128,0},{192,64},{1,129},{65,193},{129,1},{193,65... | collective-permute-start | bytes 786440 | tf_op jit(solution)/shard_map/ppermute | solution.py:256
  4.8 16.5 %collective-permute-start.5 = (bf16[16,2,8,512]{3,2,1,0:T(8,128)(2,1)}, bf16[16,2,8,512]{3,2,1,0:T(8,128)(2,1)S(1)}, u32[]{:S(2)}, u32[]{:S(2)}) collective-permute-start(bf16[16,2,8,512]{3,2,1,0:T(8,128)(2,1)} %refs_0_.1), channel_id=1, source_target_pairs={{0,192},{64,0},{128,64},{192,128},{1,193},{65,1},{129,65},{193,129... | collective-permute-start | bytes 786440 | tf_op jit(solution)/shard_map/ppermute | solution.py:256
  7.8 21.3 %all-to-all-start = ((bf16[32,16,128]{2,1,0:T(8,128)(2,1)}), bf16[32,16,128]{2,1,0:T(8,128)(2,1)S(1)}, u32[]{:S(2)}, u32[]{:S(2)}) async-start(bf16[32,16,128]{2,1,0:T(8,128)(2,1)} %lists.1), calls=%async_computation | async-start | bytes 262144 | tf_op jit(solution)/shard_map/all_to_all | solution.py:271
  18.9 12.2 %collective-permute-start = (bf16[16,2,8,512]{3,2,1,0:T(8,128)(2,1)}, bf16[16,2,8,512]{3,2,1,0:T(8,128)(2,1)S(1)}, u32[]{:S(2)}, u32[]{:S(2)}) collective-permute-start(bf16[16,2,8,512]{3,2,1,0:T(8,128)(2,1)} %refs_0_.1), channel_id=1, source_target_pairs={{0,32},{32,0},{1,33},{33,1},{2,34},{34,2},{3,35},{35,3},{4,36},{36... | collective-permute-start | bytes 786440 | tf_op jit(solution)/shard_map/ppermute | solution.py:257
  20.7 10.4 %collective-permute-start.2 = (bf16[16,2,8,512]{3,2,1,0:T(8,128)(2,1)S(1)}, bf16[16,2,8,512]{3,2,1,0:T(8,128)(2,1)S(1)}, u32[]{:S(2)}, u32[]{:S(2)}) collective-permute-start(bf16[16,2,8,512]{3,2,1,0:T(8,128)(2,1)S(1)} %collective-permute-done.1.refs_1_), channel_id=1, source_target_pairs={{0,32},{32,0},{1,33},{33,1},{2,34},{34,2},{3,35},{35,3},{4,36},{36... | collective-permute-start | bytes 786440 | tf_op jit(solution)/shard_map/ppermute | solution.py:257
  20.9 10.3 %collective-permute-start.4 = (bf16[16,2,8,512]{3,2,1,0:T(8,128)(2,1)S(1)}, bf16[16,2,8,512]{3,2,1,0:T(8,128)(2,1)S(1)}, u32[]{:S(2)}, u32[]{:S(2)}) collective-permute-start(bf16[16,2,8,512]{3,2,1,0:T(8,128)(2,1)S(1)} %collective-permute-done.3.refs_2_), channel_id=1, source_target_pairs={{0,32},{32,0},{1,33},{33,1},{2,34},{34,2},{3,35},{35,3},{4,36},{36... | collective-permute-start | bytes 786440 | tf_op jit(solution)/shard_map/ppermute | solution.py:257
  21.3 9.9 %collective-permute-start.6 = (bf16[16,2,8,512]{3,2,1,0:T(8,128)(2,1)S(1)}, bf16[16,2,8,512]{3,2,1,0:T(8,128)(2,1)}, u32[]{:S(2)}, u32[]{:S(2)}) collective-permute-start(bf16[16,2,8,512]{3,2,1,0:T(8,128)(2,1)S(1)} %collective-permute-done.5.refs_3_), channel_id=1, source_target_pairs={{0,32},{32,0},{1,33},{33,1},{2,34},{34,2},{3,35},{35,3},{4,36},{36... | collective-permute-start | bytes 786440 | tf_op jit(solution)/shard_map/ppermute | solution.py:257
  21.4 0.9 copy-start.1
  22.3 1.6 %copy-start.3 = (bf16[16,128,512]{2,1,0:T(8,128)(2,1)S(1)}, bf16[16,128,512]{2,1,0:T(8,128)(2,1)}, u32[]{:S(2)}) copy-start(bf16[16,128,512]{2,1,0:T(8,128)(2,1)} %k.1) | copy-start | bytes 6291460
  23.9 1.6 %copy-start.4 = (bf16[16,128,512]{2,1,0:T(8,128)(2,1)S(1)}, bf16[16,128,512]{2,1,0:T(8,128)(2,1)}, u32[]{:S(2)}) copy-start(bf16[16,128,512]{2,1,0:T(8,128)(2,1)} %v.1) | copy-start | bytes 6291460
  25.5 0.7 copy-start.11
  26.2 3.0 %copy-start.2 = (bf16[16,8192]{1,0:T(8,128)(2,1)S(1)}, bf16[16,8192]{1,0:T(8,128)(2,1)}, u32[]{:S(2)}) copy-start(bf16[16,8192]{1,0:T(8,128)(2,1)} %q_ref.3) | copy-start | bytes 786436
  26.2 3.0 %copy-start.9 = (bf16[16,2,8,512]{3,2,1,0:T(8,128)(2,1)S(1)}, bf16[16,2,8,512]{3,2,1,0:T(8,128)(2,1)}, u32[]{:S(2)}) copy-start(bf16[16,2,8,512]{3,2,1,0:T(8,128)(2,1)} %refs_0_.1) | copy-start | bytes 786436
  31.1 24.5 %copy-start.5 = (bf16[256,4096]{1,0:T(8,128)(2,1)S(1)}, bf16[256,4096]{1,0:T(8,128)(2,1)}, u32[]{:S(2)}) copy-start(bf16[256,4096]{1,0:T(8,128)(2,1)} %weight_ref.1) | copy-start | bytes 6291460
  34.2 30.4 %copy-start.12 = (s32[16,8]{0,1:T(8,128)S(1)}, s32[16,8]{0,1:T(8,128)}, u32[]{:S(2)}) copy-start(s32[16,8]{0,1:T(8,128)} %param.25) | copy-start | bytes 1540
  34.3 30.4 %copy-start.13 = (f32[16,8]{0,1:T(8,128)S(1)}, f32[16,8]{0,1:T(8,128)}, u32[]{:S(2)}) copy-start(f32[16,8]{0,1:T(8,128)} %param.26) | copy-start | bytes 1540
  34.3 63.0 %copy-start.6 = (bf16[1,192,4096]{2,1,0:T(8,128)(2,1)S(1)}, bf16[1,192,4096]{2,1,0:T(8,128)(2,1)}, u32[]{:S(2)}) copy-start(bf16[1,192,4096]{2,1,0:T(8,128)(2,1)} %param.27) | copy-start | bytes 4718596
  34.3 63.0 %copy-start.7 = (bf16[1,192,4096]{2,1,0:T(8,128)(2,1)S(1)}, bf16[1,192,4096]{2,1,0:T(8,128)(2,1)}, u32[]{:S(2)}) copy-start(bf16[1,192,4096]{2,1,0:T(8,128)(2,1)} %param.28) | copy-start | bytes 4718596
  34.3 63.0 %copy-start.10 = (f32[4096]{0:T(1024)S(1)}, f32[4096]{0:T(1024)}, u32[]{:S(2)}) copy-start(f32[4096]{0:T(1024)} %param.24) | copy-start | bytes 49156
  57.1 16.8 %all-to-all-start.2 = ((bf16[32,16,128]{2,1,0:T(8,128)(2,1)}), bf16[32,16,128]{2,1,0:T(8,128)(2,1)S(1)}, u32[]{:S(2)}, u32[]{:S(2)}) async-start(bf16[32,16,128]{2,1,0:T(8,128)(2,1)} %project.1), calls=%async_computation.2 | async-start | bytes 262144 | tf_op jit(solution)/shard_map/all_to_all | solution.py:313
  97.2 1.4 %copy-start.8 = (bf16[1,192,4096]{2,1,0:T(8,128)(2,1)S(1)}, bf16[1,192,4096]{2,1,0:T(8,128)(2,1)}, u32[]{:S(2)}) copy-start(bf16[1,192,4096]{2,1,0:T(8,128)(2,1)} %param.29) | copy-start | bytes 4718596

commit v3 on v2

--- a/solution.py
+++ b/solution.py
@@ -28,7 +28,7 @@
 CTX = ("x", "z")
 ALL = GRP + CTX
 NT = (((1,), (1,)), ((), ()))
-STAT_ROWS = 16
+STAT_ROWS = 8
 EACH = 4
 CHUNK = 2 * T + STAT_ROWS
 
@@ -77,8 +77,22 @@
     combine_ref[T:] = (table - high.astype(F32)).astype(BF)
 
 
-def resident_kernel(length_ref, start_ref, q, k, v, out_ref, stats_ref, wide):
+def resident_kernel(length_ref, start_ref, q_hbm, keys_hbm, values_hbm, out_ref, stats_ref, wide, q, k, v, sems):
     steps = k.shape[0] // EACH
+    first = pltpu.make_async_copy(q_hbm, q, sems.at[2 * steps])
+    first.start()
+
+    def chunk(i):
+        here = pl.ds(i * EACH, EACH)
+        return (
+            pltpu.make_async_copy(keys_hbm.at[here], k.at[here], sems.at[2 * i]),
+            pltpu.make_async_copy(values_hbm.at[here], v.at[here], sems.at[2 * i + 1]),
+        )
+
+    for i in range(steps):
+        for copy in chunk(i):
+            copy.start()
+    first.wait()
     for h in range(HEADS):
         head = q[:, h * HW : (h + 1) * HW]
         wide[h * T : (h + 1) * T, :] = head.astype(F32)
@@ -89,6 +103,8 @@
 
     @pl.loop(0, steps)
     def _(step):
+        for copy in chunk(step):
+            copy.wait()
         base = step * EACH
         own = [wide[pl.ds(base + i, HEADS, stride=T), :].astype(BF) for i in range(EACH)]
         scores = [
@@ -120,7 +136,8 @@
 
 
 def recalled_kernel(half, lists_ref, q_ref, *refs):
-    pages, (out_ref, stats_ref, *given) = refs[: NG // 2], refs[NG // 2 :]
+    pages, given = refs[: NG // 2], refs[NG // 2 :]
+    earlier, given = given[: 4 * half], given[4 * half :]
     rows = HPK * T
     tokens = len(pages) * SLOTS * TOK
     counts = jnp.sum(lists_ref[...].astype(F32), axis=0).astype(BF)
@@ -133,7 +150,7 @@
     times = times[None]
     lanes = lax.broadcasted_iota(jnp.int32, (rows, 128), 1)
     kind = lanes % 4
-    lane = lax.broadcasted_iota(jnp.int32, (HPK // 2, T, 128), 2)
+    lane = lax.broadcasted_iota(jnp.int32, (HPK // 2, 8, 128), 2)
     for g in range(KV):
         own = slice(g * rows, (g + 1) * rows)
         columns = slice(g * HW, (g + 1) * HW)
@@ -144,10 +161,12 @@
         queries = jnp.concatenate([q_ref[:, h * HW : (h + 1) * HW] for h in heads], axis=0)
         scores = lax.dot_general(queries, keys, NT, preferred_element_type=F32)
         scores = scores.reshape(HPK, T, tokens) * SCALE + bias
-        stats = stats_ref[own, :]
-        before = jnp.broadcast_to(stats[:, :1], (rows, 128))
         peak = jnp.max(scores, axis=2, keepdims=True).reshape(rows, 1)
-        peak = jnp.maximum(jnp.broadcast_to(peak, (rows, 128)), before)
+        peak = jnp.broadcast_to(peak, (rows, 128))
+        joined = [(o[own, :], s[own, :]) for o, s in zip(earlier[::2], earlier[1::2], strict=True)]
+        joined = [(o, jnp.broadcast_to(s[:, :1], (rows, 128)), s[:, 64:65]) for o, s in joined]
+        for _, before, _ in joined:
+            peak = jnp.maximum(peak, before)
         if half:
             peak_high = peak.astype(BF).astype(F32)
             peak_low = (peak - peak_high).astype(BF).astype(F32)
@@ -156,10 +175,12 @@
             base = peak
         weights = jnp.exp(scores - base[:, :1].reshape(HPK, T, 1)) * times
         total = jnp.sum(weights, axis=2, keepdims=True).reshape(rows, 1)
+        total = jnp.broadcast_to(total, (rows, 128))
         out = jnp.dot(weights.reshape(rows, tokens).astype(BF), values, preferred_element_type=F32)
-        factor = jnp.exp(before - base)
-        out = out + factor * out_ref[own, :]
-        total = jnp.broadcast_to(total, (rows, 128)) + factor * jnp.broadcast_to(stats[:, 64:65], (rows, 128))
+        for o, before, t in joined:
+            factor = jnp.exp(before - base)
+            out = out + factor * o
+            total = total + factor * jnp.broadcast_to(t, (rows, 128))
         if not half:
             given[0][own, :] = out
             given[1][own, :] = jnp.where(lanes < 64, base, total)
@@ -167,18 +188,23 @@
         total_high = total.astype(BF).astype(F32)
         stats = jnp.where(
             kind == 0, peak_high, jnp.where(kind == 1, peak_low, jnp.where(kind == 2, total_high, total - total_high))
-        ).reshape(HPK // 2, 2, T, 128)
+        ).reshape(HPK // 2, 2, 2, 8, 128)
         here = slice(g * (HPK // 2), (g + 1) * (HPK // 2))
         given[0][here, : 2 * T, :] = out.reshape(HPK // 2, 2 * T, 128).astype(BF)
-        given[0][here, 2 * T :, :] = jnp.where(lane < 4, stats[:, 0], stats[:, 1]).astype(BF)
+        stats = [jnp.where(lane < 4 + b, stats[:, 0, i], stats[:, 1, i]) for i, b in enumerate((0, 8))]
+        given[0][here, 2 * T :, :] = jnp.where(lane < 8, *stats).astype(BF)
 
 
 def project_kernel(parts_ref, weight_ref, send_ref):
     stats = parts_ref[:, 2 * T :, :].astype(F32)
     heads = []
     for i in range(2):
-        peak = stats[:, :, 4 * i : 4 * i + 1] + stats[:, :, 4 * i + 1 : 4 * i + 2]
-        total = stats[:, :, 4 * i + 2 : 4 * i + 3] + stats[:, :, 4 * i + 3 : 4 * i + 4]
+        high, low, total, rest = [
+            jnp.concatenate([stats[:, :, 8 * b + 4 * i + q : 8 * b + 4 * i + q + 1] for b in range(2)], axis=1)
+            for q in range(4)
+        ]
+        peak = high + low
+        total = total + rest
         factor = jnp.exp(peak - jnp.max(peak, axis=0, keepdims=True))
         total = jnp.sum(factor * total, axis=0)
         out = jnp.sum(factor * parts_ref[:, i * T : (i + 1) * T, :].astype(F32), axis=0)
@@ -273,26 +299,34 @@
     wide = jax.ShapeDtypeStruct((HEADS * T, 128), F32)
     out, stats = pl.pallas_call(
         resident_kernel,
-        in_specs=[smem, smem, vmem, vmem, vmem],
+        in_specs=[smem, smem, hbm, hbm, hbm],
         out_shape=(wide, wide),
-        scratch_shapes=[pltpu.VMEM((HEADS * T, HW), F32)],
-        compiler_params=params(12),
+        scratch_shapes=[
+            pltpu.VMEM((HEADS * T, HW), F32),
+            pltpu.VMEM((T, HEADS * HW), BF),
+            pltpu.VMEM((T, 128, KV * HW), BF),
+            pltpu.VMEM((T, 128, KV * HW), BF),
+            pltpu.SemaphoreType.DMA((2 * T // EACH + 1,)),
+        ],
+        compiler_params=params(51),
         cost_estimate=cost(70_000_000, 6_000_000, 131_072),
         name="resident",
     )(res_len, (ctx_index * 128).reshape(1).astype(jnp.int32), queries, resident_key_cache, resident_value_cache)
 
-    for half in range(2):
-        last = half == 1
-        result = pl.pallas_call(
-            functools.partial(recalled_kernel, half),
-            out_shape=jax.ShapeDtypeStruct((NC, CHUNK, 128), BF) if last else (wide, wide),
-            compiler_params=params(16),
-            cost_estimate=cost(270_000_000, 4_000_000, 524_288),
-            name="recalled",
-        )(lists, queries, *pages[half * 4 : half * 4 + 4], out, stats)
-        if not last:
-            out, stats = result
-    parts = result
+    own = pl.pallas_call(
+        functools.partial(recalled_kernel, 0),
+        out_shape=(wide, wide),
+        compiler_params=params(16),
+        cost_estimate=cost(270_000_000, 4_000_000, 524_288),
+        name="recalled_own",
+    )(lists, queries, *pages[:4])
+    parts = pl.pallas_call(
+        functools.partial(recalled_kernel, 1),
+        out_shape=jax.ShapeDtypeStruct((NC, CHUNK, 128), BF),
+        compiler_params=params(16),
+        cost_estimate=cost(270_000_000, 4_000_000, 524_288),
+        name="recalled_other",
+    )(lists, queries, *pages[4:], *own, out, stats)
     parts = lax.all_to_all(parts, CTX, split_axis=0, concat_axis=0, tiled=True)
 
     sums = pl.pallas_call(
@@ -327,7 +361,7 @@
         in_specs=[vmem, vmem, vmem, vmem, hbm],
         out_shape=jax.ShapeDtypeStruct((rows, 128), BF),
         scratch_shapes=[pltpu.VMEM((rows, 128), F32), pltpu.VMEM((NG * CAPE, D), F32), pltpu.VMEM((FP, D), BF), pltpu.SemaphoreType.DMA(())],
-        compiler_params=params(12),
+        compiler_params=params(50),
         cost_estimate=cost(160_000_000, 5_300_000, 8192),
         name="experts",
     )(arrived.reshape(rows, 128), norm_gain.reshape(1, D), w_gate[0], w_up[0], w_down[0])

time: 123 us -> 120 us (0.976)
  local copies, waits for them, and re-layouts: 6.25 us -> 1.67 us
  Pallas kernels: 14.2 us -> 17.1 us
  blocking collectives: 65.4 us -> 63.1 us
    unnamed x28 -> x22, local copies, waits for them, and re-layouts: 6.24 us -> 1.65 us
    all_to_all x1, blocking collectives: 21.3 us -> 19.2 us  [shards(): parts = lax.all_to_all(parts, CTX, split_axis=0, concat_axis=0, tiled=True)]
    pallas_call x3, Pallas kernels: 7.96 us -> 9.61 us  [the longest x1 4.26 us: shards(): pl.pallas_call(resident_kernel, in_specs=[smem, smem, hbm, hbm, hbm], out...]
  transfers between devices with their start and end apart: 9 -> 9, of which waited for: 1 -> 2; matrix products, arithmetic and copies ran while one was open for 1% -> 1% of each run, Pallas kernels for 5% -> 6%
where the time goes in v3:
time: 120 us; the launch traced here: 119 us
  blocking collectives  63.1 us (53%)
  starting transfers between devices  26.9 us (22%)
  Pallas kernels  17.1 us (14%)
  waiting for transfers between devices  9.57 us (8%)
  local copies, waits for them, and re-layouts  1.67 us (1%)
    all_to_all x1, blocking collectives, shards(): lax.all_to_all(send.reshape(NG * NC, CAPE, 128), ALL, split_axis=0, conca...  23 us
    all_to_all x1, blocking collectives, shards(): lax.all_to_all(results.reshape(NG * NC, CAPE, 128), ALL, split_axis=0, co...  20.9 us
    all_to_all x1, blocking collectives, shards(): parts = lax.all_to_all(parts, CTX, split_axis=0, concat_axis=0, tiled=True)  19.2 us
    all_to_all x1, starting transfers between devices, shards(): lists = lax.all_to_all(lists, CTX, split_axis=0, concat_axis=0, tiled=True)  11 us
    all_to_all x1, waiting for transfers between devices, shards(): sums = lax.all_to_all(sums, CTX, split_axis=0, concat_axis=0, tiled=True)  8.69 us
    all_to_all x1, starting transfers between devices, shards(): sums = lax.all_to_all(sums, CTX, split_axis=0, concat_axis=0, tiled=True)  7.52 us
    ppermute x3, starting transfers between devices, shards(): lax.ppermute(visual_page_pool, 'y', [(i, (i + k) % 4) for i in range(4)])  5.81 us
    pallas_call x1, Pallas kernels, shards(): pl.pallas_call(resident_kernel, in_specs=[smem, smem, hbm, hbm, hbm], out...  4.26 us
  transfers between devices with their start and end apart: 9, of which 2 were waited for; matrix products, arithmetic and copies ran while one was open for 1% of the time, Pallas kernels for 6%

profile of v3, /device:TPU:1, one launch (start us, length us, event | category | flops | bytes accessed | tf_op | source)
XLA Modules:
  0.0 119.2 jit_solution(506462666380725293)
XLA Ops:
  0.0 2.1 %collective-permute-start.1 = (bf16[16,2,8,512]{3,2,1,0:T(8,128)(2,1)}, bf16[16,2,8,512]{3,2,1,0:T(8,128)(2,1)S(1)}, u32[]{:S(2)}, u32[]{:S(2)}) collective-permute-start(bf16[16,2,8,512]{3,2,1,0:T(8,128)(2,1)} %refs_0_.1), channel_id=1, source_target_pairs={{0,64},{64,128},{128,192},{192,0},{1,65},{65,129},{129,193},{193,1... | collective-permute-start | bytes 786440 | tf_op jit(solution)/shard_map/ppermute | solution.py:282
  2.1 2.6 %collective-permute-start.3 = (bf16[16,2,8,512]{3,2,1,0:T(8,128)(2,1)}, bf16[16,2,8,512]{3,2,1,0:T(8,128)(2,1)S(1)}, u32[]{:S(2)}, u32[]{:S(2)}) collective-permute-start(bf16[16,2,8,512]{3,2,1,0:T(8,128)(2,1)} %refs_0_.1), channel_id=1, source_target_pairs={{0,128},{64,192},{128,0},{192,64},{1,129},{65,193},{129,1},{193,65... | collective-permute-start | bytes 786440 | tf_op jit(solution)/shard_map/ppermute | solution.py:282
  4.8 1.1 collective-permute-start.5
  5.8 0.7 fusion.2.key_ref
  6.6 1.2 %lists.1 = bf16[32,16,128]{2,1,0:T(8,128)(2,1)} custom-call(s32[16,16]{1,0:T(8,128)S(1)} %fusion.2.key_ref), custom_call_target="tpu_custom_call" | custom-call | flops 4000000 | bytes 140000 | tf_op jit(solution)/shard_map/lists/pallas_call | solution.py:290
  7.8 11.0 %all-to-all-start = ((bf16[32,16,128]{2,1,0:T(8,128)(2,1)}), bf16[32,16,128]{2,1,0:T(8,128)(2,1)S(1)}, u32[]{:S(2)}, u32[]{:S(2)}) async-start(bf16[32,16,128]{2,1,0:T(8,128)(2,1)} %lists.1), calls=%async_computation | async-start | bytes 262144 | tf_op jit(solution)/shard_map/all_to_all | solution.py:297
  18.9 1.9 %collective-permute-start = (bf16[16,2,8,512]{3,2,1,0:T(8,128)(2,1)}, bf16[16,2,8,512]{3,2,1,0:T(8,128)(2,1)S(1)}, u32[]{:S(2)}, u32[]{:S(2)}) collective-permute-start(bf16[16,2,8,512]{3,2,1,0:T(8,128)(2,1)} %refs_0_.1), channel_id=1, source_target_pairs={{0,32},{32,0},{1,33},{33,1},{2,34},{34,2},{3,35},{35,3},{4,36},{36... | collective-permute-start | bytes 786440 | tf_op jit(solution)/shard_map/ppermute | solution.py:283
  20.7 0.1 collective-permute-start.2
  20.9 0.4 collective-permute-start.4
  21.3 0.1 collective-permute-start.6
  21.4 0.9 copy-done.1
  22.3 0.7 copy-done.8
  23.0 4.3 %resident.1 = (f32[1024,128]{1,0:T(8,128)S(1)}, f32[1024,128]{1,0:T(8,128)S(1)}) custom-call(s32[16]{0:T(128)S(1)} %copy-done.8, s32[1]{0:T(128)} %bitcast.2.start_ref, bf16[16,8192]{1,0:T(8,128)(2,1)S(1)} %copy-done.1, bf16[16,128,512]{2,1,0:T(8,128)(2,1)} %keys_hbm.1, bf16[16,128,512]{2,1,0:T(8,128)(2,1)} %values_hbm.1), custom_call_target="tpu_custom_call" | custom-call | flops 70000000 | bytes 6000000 | tf_op jit(solution)/shard_map/resident/pallas_call | solution.py:300
  27.2 0.9 all-to-all-done.lists_ref
  28.1 1.5 %recalled_own.1 = (f32[1024,128]{1,0:T(8,128)S(1)}, f32[1024,128]{1,0:T(8,128)S(1)}) custom-call(bf16[32,16,128]{2,1,0:T(8,128)(2,1)S(1)} %all-to-all-done.lists_ref, bf16[16,8192]{1,0:T(8,128)(2,1)S(1)} %copy-done.2, bf16[16,2,8,512]{3,2,1,0:T(8,128)(2,1)S(1)} %copy-done.6, bf16[16,2,8,512]{3,2,1,0:T(8,128)(2,1)S(1)} %collective-permute-done.1.refs_1_, ...), custom_call_target="tpu_custom_call" | custom-call | flops 270000000 | bytes 4000000 | tf_op jit(solution)/shard_map/recalled_own/pallas_call | solution.py:316
  29.6 0.0 copy-start.3
  29.6 3.9 %recalled_other.1 = bf16[32,40,128]{2,1,0:T(8,128)(2,1)S(1)} custom-call(bf16[32,16,128]{2,1,0:T(8,128)(2,1)S(1)} %all-to-all-done.lists_ref, bf16[16,8192]{1,0:T(8,128)(2,1)S(1)} %copy-done.2, bf16[16,2,8,512]{3,2,1,0:T(8,128)(2,1)S(1)} %collective-permute-done.refs_0_, bf16[16,2,8,512]{3,2,1,0:T(8,128)(2,1)S(1)} %collective-permute-done.2.refs_1_, ...), custom_call_target="tpu_custom_call" | custom-call | flops 270000000 | bytes 4000000 | tf_op jit(solution)/shard_map/recalled_other/pallas_call | solution.py:323
  33.5 0.0 copy-start.9
  33.5 0.0 copy-start.10
  33.6 0.0 copy-start.4
  33.6 0.0 copy-start.5
  33.6 0.0 copy-start.7
  33.6 19.2 %all_to_all.25.parts_ref = bf16[32,40,128]{2,1,0:T(8,128)(2,1)S(1)} all-to-all(bf16[32,40,128]{2,1,0:T(8,128)(2,1)S(1)} %recalled_other.1), channel_id=1, replica_groups=mesh['y'=4,'core'=2,'x'=4,'z'=8] {'x','z'}, dimensions={0} | all-to-all | bytes 655360 | tf_op jit(solution)/shard_map/all_to_all | solution.py:330
  52.8 1.5 %project.1 = bf16[32,16,128]{2,1,0:T(8,128)(2,1)} custom-call(bf16[32,40,128]{2,1,0:T(8,128)(2,1)S(1)} %all_to_all.25.parts_ref, bf16[256,4096]{1,0:T(8,128)(2,1)S(1)} %copy-done.3), custom_call_target="tpu_custom_call" | custom-call | flops 40000000 | bytes 2700000 | tf_op jit(solution)/shard_map/project/pallas_call | solution.py:332
  54.3 7.5 %all-to-all-start.2 = ((bf16[32,16,128]{2,1,0:T(8,128)(2,1)}), bf16[32,16,128]{2,1,0:T(8,128)(2,1)S(1)}, u32[]{:S(2)}, u32[]{:S(2)}) async-start(bf16[32,16,128]{2,1,0:T(8,128)(2,1)} %project.1), calls=%async_computation.2 | async-start | bytes 262144 | tf_op jit(solution)/shard_map/all_to_all | solution.py:347
  61.9 0.4 prepare.1
  62.3 8.7 %all-to-all-done.2.sums_ref = bf16[32,16,128]{2,1,0:T(8,128)(2,1)S(1)} async-done(((bf16[32,16,128]{2,1,0:T(8,128)(2,1)}), bf16[32,16,128]{2,1,0:T(8,128)(2,1)S(1)}, u32[]{:S(2)}, u32[]{:S(2)}) %all-to-all-start.2) | async-done | bytes 131104 | tf_op jit(solution)/shard_map/all_to_all | solution.py:347
  71.0 0.3 dispatch.1
  71.3 23.0 %all_to_all.26 = bf16[256,4,128]{2,1,0:T(4,128)(2,1)S(1)} all-to-all(bf16[256,4,128]{2,1,0:T(4,128)(2,1)S(1)} %bitcast.36), channel_id=1, replica_groups=mesh['y'=4,'core'=2,'x'=4,'z'=8] {'y','core','x','z'}, dimensions={0} | all-to-all | bytes 524288 | tf_op jit(solution)/shard_map/all_to_all | solution.py:357
  94.3 3.2 %experts.1 = bf16[1024,128]{1,0:T(8,128)(2,1)S(1)} custom-call(bf16[1024,128]{1,0:T(8,128)(2,1)S(1)} %bitcast.33, f32[1,4096]{1,0:T(1,128)S(1)} %bitcast.37, bf16[192,4096]{1,0:T(8,128)(2,1)S(1)} %bitcast.31, bf16[192,4096]{1,0:T(8,128)(2,1)S(1)} %bitcast.32, bf16[192,4096]{1,0:T(8,128)(2,1)} %bitcast.40), custom_call_target="tpu_custom_call" | custom-call | flops 160000000 | bytes 5300000 | tf_op jit(solution)/shard_map/experts/pallas_call | solution.py:359
  97.6 20.9 %all_to_all.27 = bf16[256,4,128]{2,1,0:T(4,128)(2,1)S(1)} all-to-all(bf16[256,4,128]{2,1,0:T(4,128)(2,1)S(1)} %bitcast.34), channel_id=1, replica_groups=mesh['y'=4,'core'=2,'x'=4,'z'=8] {'y','core','x','z'}, dimensions={0} | all-to-all | bytes 524288 | tf_op jit(solution)/shard_map/all_to_all | solution.py:368
  118.5 0.8 combine.1
  (22 shorter events, 0.1 us)
Async XLA Ops:
  0.0 61.9 %copy-start = (bf16[16,4096]{1,0:T(8,128)(2,1)S(1)}, bf16[16,4096]{1,0:T(8,128)(2,1)}, u32[]{:S(2)}) copy-start(bf16[16,4096]{1,0:T(8,128)(2,1)} %param.23) | copy-start | bytes 393220
  0.0 20.7 %collective-permute-start.1 = (bf16[16,2,8,512]{3,2,1,0:T(8,128)(2,1)}, bf16[16,2,8,512]{3,2,1,0:T(8,128)(2,1)S(1)}, u32[]{:S(2)}, u32[]{:S(2)}) collective-permute-start(bf16[16,2,8,512]{3,2,1,0:T(8,128)(2,1)} %refs_0_.1), channel_id=1, source_target_pairs={{0,64},{64,128},{128,192},{192,0},{1,65},{65,129},{129,193},{193,1... | collective-permute-start | bytes 786440 | tf_op jit(solution)/shard_map/ppermute | solution.py:282
  2.1 18.7 %collective-permute-start.3 = (bf16[16,2,8,512]{3,2,1,0:T(8,128)(2,1)}, bf16[16,2,8,512]{3,2,1,0:T(8,128)(2,1)S(1)}, u32[]{:S(2)}, u32[]{:S(2)}) collective-permute-start(bf16[16,2,8,512]{3,2,1,0:T(8,128)(2,1)} %refs_0_.1), channel_id=1, source_target_pairs={{0,128},{64,192},{128,0},{192,64},{1,129},{65,193},{129,1},{193,65... | collective-permute-start | bytes 786440 | tf_op jit(solution)/shard_map/ppermute | solution.py:282
  4.8 16.5 %collective-permute-start.5 = (bf16[16,2,8,512]{3,2,1,0:T(8,128)(2,1)}, bf16[16,2,8,512]{3,2,1,0:T(8,128)(2,1)S(1)}, u32[]{:S(2)}, u32[]{:S(2)}) collective-permute-start(bf16[16,2,8,512]{3,2,1,0:T(8,128)(2,1)} %refs_0_.1), channel_id=1, source_target_pairs={{0,192},{64,0},{128,64},{192,128},{1,193},{65,1},{129,65},{193,129... | collective-permute-start | bytes 786440 | tf_op jit(solution)/shard_map/ppermute | solution.py:282
  7.8 20.3 %all-to-all-start = ((bf16[32,16,128]{2,1,0:T(8,128)(2,1)}), bf16[32,16,128]{2,1,0:T(8,128)(2,1)S(1)}, u32[]{:S(2)}, u32[]{:S(2)}) async-start(bf16[32,16,128]{2,1,0:T(8,128)(2,1)} %lists.1), calls=%async_computation | async-start | bytes 262144 | tf_op jit(solution)/shard_map/all_to_all | solution.py:297
  18.9 10.7 %collective-permute-start = (bf16[16,2,8,512]{3,2,1,0:T(8,128)(2,1)}, bf16[16,2,8,512]{3,2,1,0:T(8,128)(2,1)S(1)}, u32[]{:S(2)}, u32[]{:S(2)}) collective-permute-start(bf16[16,2,8,512]{3,2,1,0:T(8,128)(2,1)} %refs_0_.1), channel_id=1, source_target_pairs={{0,32},{32,0},{1,33},{33,1},{2,34},{34,2},{3,35},{35,3},{4,36},{36... | collective-permute-start | bytes 786440 | tf_op jit(solution)/shard_map/ppermute | solution.py:283
  20.7 8.8 %collective-permute-start.2 = (bf16[16,2,8,512]{3,2,1,0:T(8,128)(2,1)S(1)}, bf16[16,2,8,512]{3,2,1,0:T(8,128)(2,1)S(1)}, u32[]{:S(2)}, u32[]{:S(2)}) collective-permute-start(bf16[16,2,8,512]{3,2,1,0:T(8,128)(2,1)S(1)} %collective-permute-done.1.refs_1_), channel_id=1, source_target_pairs={{0,32},{32,0},{1,33},{33,1},{2,34},{34,2},{3,35},{35,3},{4,36},{36... | collective-permute-start | bytes 786440 | tf_op jit(solution)/shard_map/ppermute | solution.py:283
  20.9 8.7 %collective-permute-start.4 = (bf16[16,2,8,512]{3,2,1,0:T(8,128)(2,1)S(1)}, bf16[16,2,8,512]{3,2,1,0:T(8,128)(2,1)S(1)}, u32[]{:S(2)}, u32[]{:S(2)}) collective-permute-start(bf16[16,2,8,512]{3,2,1,0:T(8,128)(2,1)S(1)} %collective-permute-done.3.refs_2_), channel_id=1, source_target_pairs={{0,32},{32,0},{1,33},{33,1},{2,34},{34,2},{3,35},{35,3},{4,36},{36... | collective-permute-start | bytes 786440 | tf_op jit(solution)/shard_map/ppermute | solution.py:283
  21.3 8.3 %collective-permute-start.6 = (bf16[16,2,8,512]{3,2,1,0:T(8,128)(2,1)S(1)}, bf16[16,2,8,512]{3,2,1,0:T(8,128)(2,1)}, u32[]{:S(2)}, u32[]{:S(2)}) collective-permute-start(bf16[16,2,8,512]{3,2,1,0:T(8,128)(2,1)S(1)} %collective-permute-done.5.refs_3_), channel_id=1, source_target_pairs={{0,32},{32,0},{1,33},{33,1},{2,34},{34,2},{3,35},{35,3},{4,36},{36... | collective-permute-start | bytes 786440 | tf_op jit(solution)/shard_map/ppermute | solution.py:283
  21.4 0.9 copy-start.1
  22.3 0.7 copy-start.8
  23.0 5.1 %copy-start.2 = (bf16[16,8192]{1,0:T(8,128)(2,1)S(1)}, bf16[16,8192]{1,0:T(8,128)(2,1)}, u32[]{:S(2)}) copy-start(bf16[16,8192]{1,0:T(8,128)(2,1)} %q_ref.3) | copy-start | bytes 786436
  23.0 5.1 %copy-start.6 = (bf16[16,2,8,512]{3,2,1,0:T(8,128)(2,1)S(1)}, bf16[16,2,8,512]{3,2,1,0:T(8,128)(2,1)}, u32[]{:S(2)}) copy-start(bf16[16,2,8,512]{3,2,1,0:T(8,128)(2,1)} %refs_0_.1) | copy-start | bytes 786436
  29.6 23.2 %copy-start.3 = (bf16[256,4096]{1,0:T(8,128)(2,1)S(1)}, bf16[256,4096]{1,0:T(8,128)(2,1)}, u32[]{:S(2)}) copy-start(bf16[256,4096]{1,0:T(8,128)(2,1)} %weight_ref.1) | copy-start | bytes 6291460
  33.5 28.4 %copy-start.9 = (s32[16,8]{0,1:T(8,128)S(1)}, s32[16,8]{0,1:T(8,128)}, u32[]{:S(2)}) copy-start(s32[16,8]{0,1:T(8,128)} %param.25) | copy-start | bytes 1540
  33.5 28.3 %copy-start.10 = (f32[16,8]{0,1:T(8,128)S(1)}, f32[16,8]{0,1:T(8,128)}, u32[]{:S(2)}) copy-start(f32[16,8]{0,1:T(8,128)} %param.26) | copy-start | bytes 1540
  33.6 60.8 %copy-start.4 = (bf16[1,192,4096]{2,1,0:T(8,128)(2,1)S(1)}, bf16[1,192,4096]{2,1,0:T(8,128)(2,1)}, u32[]{:S(2)}) copy-start(bf16[1,192,4096]{2,1,0:T(8,128)(2,1)} %param.27) | copy-start | bytes 4718596
  33.6 60.8 %copy-start.5 = (bf16[1,192,4096]{2,1,0:T(8,128)(2,1)S(1)}, bf16[1,192,4096]{2,1,0:T(8,128)(2,1)}, u32[]{:S(2)}) copy-start(bf16[1,192,4096]{2,1,0:T(8,128)(2,1)} %param.28) | copy-start | bytes 4718596
  33.6 60.8 %copy-start.7 = (f32[4096]{0:T(1024)S(1)}, f32[4096]{0:T(1024)}, u32[]{:S(2)}) copy-start(f32[4096]{0:T(1024)} %param.24) | copy-start | bytes 49156
  54.3 16.7 %all-to-all-start.2 = ((bf16[32,16,128]{2,1,0:T(8,128)(2,1)}), bf16[32,16,128]{2,1,0:T(8,128)(2,1)S(1)}, u32[]{:S(2)}, u32[]{:S(2)}) async-start(bf16[32,16,128]{2,1,0:T(8,128)(2,1)} %project.1), calls=%async_computation.2 | async-start | bytes 262144 | tf_op jit(solution)/shard_map/all_to_all | solution.py:347

commit v4 on v3

--- a/solution.py
+++ b/solution.py
@@ -217,17 +217,16 @@
             send_ref[j * (wide // 128) + i] = block[:, i * 128 : (i + 1) * 128]
 
 
-def dispatch_kernel(sums_ref, residual_ref, picker_ref, hidden_ref, send_ref):
-    hidden = residual_ref[...].astype(F32) + jnp.sum(sums_ref[...].astype(F32), axis=0)
+def dispatch_kernel(start_ref, sums_ref, residual_ref, picker_ref, hidden_ref, send_ref):
+    here = pl.ds(pl.multiple_of(start_ref[0], 128), 128)
+    hidden = residual_ref[:, here].astype(F32) + jnp.sum(sums_ref[...].astype(F32), axis=0)
     hidden_ref[...] = hidden
     send_ref[...] = lax.dot_general(
         picker_ref[...], hidden.astype(BF), (((0,), (0,)), ((), ())), preferred_element_type=F32
     ).astype(BF)
 
 
-def expert_kernel(rows_ref, gain_ref, gate_ref, up_ref, down_hbm, send_ref, wide_ref, token_ref, down_ref, sem):
-    late = pltpu.make_async_copy(down_hbm, down_ref, sem)
-    late.start()
+def hidden_units_kernel(rows_ref, gain_ref, gate_ref, up_ref, act_ref, wide_ref, token_ref):
     wide_ref[...] = rows_ref[...].astype(F32)
     for c in range(NC):
         for s in range(CAPE):
@@ -236,9 +235,12 @@
     normed = (hidden * lax.rsqrt(jnp.mean(hidden * hidden, axis=1, keepdims=True) + EPS) * gain_ref[...]).astype(BF)
     gate = lax.dot_general(normed, gate_ref[...], NT, preferred_element_type=F32)
     up = lax.dot_general(normed, up_ref[...], NT, preferred_element_type=F32)
-    act = (gate / (1.0 + jnp.exp(-gate)) * up).astype(BF)
+    act_ref[...] = (gate / (1.0 + jnp.exp(-gate)) * up).astype(BF)
+
+
+def down_kernel(act_ref, down_ref, send_ref, wide_ref):
+    act = act_ref[...]
     wide = 512
-    late.wait()
     for j in range(D // wide):
         block = jnp.dot(act, down_ref[:, j * wide : (j + 1) * wide], preferred_element_type=F32)
         for i in range(wide // 128):
@@ -273,6 +275,7 @@
 ):
     ctx_index = lax.axis_index(CTX)
     rows = NG * NC * CAPE
+    start = (ctx_index * 128).reshape(1).astype(jnp.int32)
 
     smem = pl.BlockSpec(memory_space=pltpu.SMEM)
     vmem = pl.BlockSpec(memory_space=pltpu.VMEM)
@@ -311,7 +314,7 @@
         compiler_params=params(51),
         cost_estimate=cost(70_000_000, 6_000_000, 131_072),
         name="resident",
-    )(res_len, (ctx_index * 128).reshape(1).astype(jnp.int32), queries, resident_key_cache, resident_value_cache)
+    )(res_len, start, queries, resident_key_cache, resident_value_cache)
 
     own = pl.pallas_call(
         functools.partial(recalled_kernel, 0),
@@ -346,25 +349,32 @@
     )(ids, chances)
     sums = lax.all_to_all(sums, CTX, split_axis=0, concat_axis=0, tiled=True)
 
-    own_residual = lax.dynamic_slice_in_dim(residual, ctx_index * 128, 128, 1)
     hidden, send = pl.pallas_call(
         dispatch_kernel,
+        in_specs=[smem, vmem, vmem, vmem],
         out_shape=(jax.ShapeDtypeStruct((T, 128), F32), jax.ShapeDtypeStruct((rows, 128), BF)),
         compiler_params=params(8),
         cost_estimate=cost(4_000_000, 500_000),
         name="dispatch",
-    )(sums, own_residual, picker)
+    )(start, sums, residual, picker)
     arrived = lax.all_to_all(send.reshape(NG * NC, CAPE, 128), ALL, split_axis=0, concat_axis=0, tiled=True)
 
+    act = pl.pallas_call(
+        hidden_units_kernel,
+        out_shape=jax.ShapeDtypeStruct((NG * CAPE, FP), BF),
+        scratch_shapes=[pltpu.VMEM((rows, 128), F32), pltpu.VMEM((NG * CAPE, D), F32)],
+        compiler_params=params(8),
+        cost_estimate=cost(100_000_000, 3_500_000, 8192),
+        name="hidden_units",
+    )(arrived.reshape(rows, 128), norm_gain.reshape(1, D), w_gate[0], w_up[0])
     results = pl.pallas_call(
-        expert_kernel,
-        in_specs=[vmem, vmem, vmem, vmem, hbm],
+        down_kernel,
         out_shape=jax.ShapeDtypeStruct((rows, 128), BF),
-        scratch_shapes=[pltpu.VMEM((rows, 128), F32), pltpu.VMEM((NG * CAPE, D), F32), pltpu.VMEM((FP, D), BF), pltpu.SemaphoreType.DMA(())],
-        compiler_params=params(50),
-        cost_estimate=cost(160_000_000, 5_300_000, 8192),
-        name="experts",
-    )(arrived.reshape(rows, 128), norm_gain.reshape(1, D), w_gate[0], w_up[0], w_down[0])
+        scratch_shapes=[pltpu.VMEM((rows, 128), F32)],
+        compiler_params=params(8),
+        cost_estimate=cost(50_000_000, 1_900_000),
+        name="down",
+    )(act, w_down[0])
     returned = lax.all_to_all(results.reshape(NG * NC, CAPE, 128), ALL, split_axis=0, concat_axis=0, tiled=True)
 
     return pl.pallas_call(

time: 120 us -> 118 us (0.983)
  Pallas kernels: 17.1 us -> 14.8 us
    pallas_call x2 -> x3, Pallas kernels: 3.49 us -> 2.27 us  [the longest x1 1.4 us: shards(): pl.pallas_call(hidden_units_kernel, out_shape=jax.ShapeDtypeStruct((NG *...]
where the time goes in v4:
time: 118 us
  blocking collectives  63.3 us (54%)
  starting transfers between devices  27.5 us (23%)
  Pallas kernels  14.8 us (13%)
  waiting for transfers between devices  9.6 us (8%)
  local copies, waits for them, and re-layouts  1.66 us (1%)
    all_to_all x1, blocking collectives, shards(): lax.all_to_all(send.reshape(NG * NC, CAPE, 128), ALL, split_axis=0, conca...  23.2 us
    all_to_all x1, blocking collectives, shards(): lax.all_to_all(results.reshape(NG * NC, CAPE, 128), ALL, split_axis=0, co...  20.9 us
    all_to_all x1, blocking collectives, shards(): parts = lax.all_to_all(parts, CTX, split_axis=0, concat_axis=0, tiled=True)  19.2 us
    all_to_all x1, starting transfers between devices, shards(): lists = lax.all_to_all(lists, CTX, split_axis=0, concat_axis=0, tiled=True)  11 us
    all_to_all x1, waiting for transfers between devices, shards(): sums = lax.all_to_all(sums, CTX, split_axis=0, concat_axis=0, tiled=True)  8.73 us
    all_to_all x1, starting transfers between devices, shards(): sums = lax.all_to_all(sums, CTX, split_axis=0, concat_axis=0, tiled=True)  7.52 us
    ppermute x3, starting transfers between devices, shards(): lax.ppermute(visual_page_pool, 'y', [(i, (i + k) % 4) for i in range(4)])  6.42 us
    pallas_call x1, Pallas kernels, shards(): pl.pallas_call(resident_kernel, in_specs=[smem, smem, hbm, hbm, hbm], out...  4.26 us
  transfers between devices with their start and end apart: 9, of which 2 were waited for; matrix products, arithmetic and copies ran while one was open for 1% of the time, Pallas kernels for 6%

profile of v4, /device:TPU:1, one launch (start us, length us, event | category | flops | bytes accessed | tf_op | source)
XLA Modules:
  0.0 117.7 jit_solution(15084151061382517614)
XLA Ops:
  0.0 3.7 %collective-permute-start.3 = (bf16[16,2,8,512]{3,2,1,0:T(8,128)(2,1)}, bf16[16,2,8,512]{3,2,1,0:T(8,128)(2,1)S(1)}, u32[]{:S(2)}, u32[]{:S(2)}) collective-permute-start(bf16[16,2,8,512]{3,2,1,0:T(8,128)(2,1)} %refs_0_.1), channel_id=1, source_target_pairs={{0,128},{64,192},{128,0},{192,64},{1,129},{65,193},{129,1},{193,65... | collective-permute-start | bytes 786440 | tf_op jit(solution)/shard_map/ppermute | solution.py:285
  3.7 0.4 collective-permute-start.1
  4.1 2.3 %collective-permute-start.5 = (bf16[16,2,8,512]{3,2,1,0:T(8,128)(2,1)}, bf16[16,2,8,512]{3,2,1,0:T(8,128)(2,1)S(1)}, u32[]{:S(2)}, u32[]{:S(2)}) collective-permute-start(bf16[16,2,8,512]{3,2,1,0:T(8,128)(2,1)} %refs_0_.1), channel_id=1, source_target_pairs={{0,192},{64,0},{128,64},{192,128},{1,193},{65,1},{129,65},{193,129... | collective-permute-start | bytes 786440 | tf_op jit(solution)/shard_map/ppermute | solution.py:285
  6.4 0.7 fusion.2.key_ref
  7.2 1.3 %lists.1 = bf16[32,16,128]{2,1,0:T(8,128)(2,1)} custom-call(s32[16,16]{1,0:T(8,128)S(1)} %fusion.2.key_ref), custom_call_target="tpu_custom_call" | custom-call | flops 4000000 | bytes 140000 | tf_op jit(solution)/shard_map/lists/pallas_call | solution.py:293
  8.4 11.0 %all-to-all-start = ((bf16[32,16,128]{2,1,0:T(8,128)(2,1)}), bf16[32,16,128]{2,1,0:T(8,128)(2,1)S(1)}, u32[]{:S(2)}, u32[]{:S(2)}) async-start(bf16[32,16,128]{2,1,0:T(8,128)(2,1)} %lists.1), calls=%async_computation | async-start | bytes 262144 | tf_op jit(solution)/shard_map/all_to_all | solution.py:300
  19.5 1.9 %collective-permute-start = (bf16[16,2,8,512]{3,2,1,0:T(8,128)(2,1)}, bf16[16,2,8,512]{3,2,1,0:T(8,128)(2,1)S(1)}, u32[]{:S(2)}, u32[]{:S(2)}) collective-permute-start(bf16[16,2,8,512]{3,2,1,0:T(8,128)(2,1)} %refs_0_.1), channel_id=1, source_target_pairs={{0,32},{32,0},{1,33},{33,1},{2,34},{34,2},{3,35},{35,3},{4,36},{36... | collective-permute-start | bytes 786440 | tf_op jit(solution)/shard_map/ppermute | solution.py:286
  21.4 0.1 collective-permute-start.4
  21.5 0.4 collective-permute-start.2
  21.9 0.1 collective-permute-start.6
  22.0 0.9 copy-done
  22.9 0.7 copy-done.9
  23.6 4.3 %resident.1 = (f32[1024,128]{1,0:T(8,128)S(1)}, f32[1024,128]{1,0:T(8,128)S(1)}) custom-call(s32[16]{0:T(128)S(1)} %copy-done.9, s32[1]{0:T(128)} %bitcast.start_ref, bf16[16,8192]{1,0:T(8,128)(2,1)S(1)} %copy-done, bf16[16,128,512]{2,1,0:T(8,128)(2,1)} %keys_hbm.1, bf16[16,128,512]{2,1,0:T(8,128)(2,1)} %values_hbm.1), custom_call_target="tpu_custom_call" | custom-call | flops 70000000 | bytes 6000000 | tf_op jit(solution)/shard_map/resident/pallas_call | solution.py:303
  27.9 0.9 all-to-all-done.lists_ref
  28.7 1.5 %recalled_own.1 = (f32[1024,128]{1,0:T(8,128)S(1)}, f32[1024,128]{1,0:T(8,128)S(1)}) custom-call(bf16[32,16,128]{2,1,0:T(8,128)(2,1)S(1)} %all-to-all-done.lists_ref, bf16[16,8192]{1,0:T(8,128)(2,1)S(1)} %copy-done.1, bf16[16,2,8,512]{3,2,1,0:T(8,128)(2,1)S(1)} %copy-done.6, bf16[16,2,8,512]{3,2,1,0:T(8,128)(2,1)S(1)} %collective-permute-done.1.refs_1_, ...), custom_call_target="tpu_custom_call" | custom-call | flops 270000000 | bytes 4000000 | tf_op jit(solution)/shard_map/recalled_own/pallas_call | solution.py:319
  30.2 0.0 copy-start.2
  30.2 2.8 %recalled_other.1 = bf16[32,40,128]{2,1,0:T(8,128)(2,1)S(1)} custom-call(bf16[32,16,128]{2,1,0:T(8,128)(2,1)S(1)} %all-to-all-done.lists_ref, bf16[16,8192]{1,0:T(8,128)(2,1)S(1)} %copy-done.1, bf16[16,2,8,512]{3,2,1,0:T(8,128)(2,1)S(1)} %collective-permute-done.refs_0_, bf16[16,2,8,512]{3,2,1,0:T(8,128)(2,1)S(1)} %collective-permute-done.2.refs_1_, ...), custom_call_target="tpu_custom_call" | custom-call | flops 270000000 | bytes 4000000 | tf_op jit(solution)/shard_map/recalled_other/pallas_call | solution.py:326
  33.0 0.0 copy-start.10
  33.1 0.0 copy-start.11
  33.1 0.0 copy-start.7
  33.1 0.0 copy-start.4
  33.1 19.2 %all_to_all.25.parts_ref = bf16[32,40,128]{2,1,0:T(8,128)(2,1)S(1)} all-to-all(bf16[32,40,128]{2,1,0:T(8,128)(2,1)S(1)} %recalled_other.1), channel_id=1, replica_groups=mesh['y'=4,'core'=2,'x'=4,'z'=8] {'x','z'}, dimensions={0} | all-to-all | bytes 655360 | tf_op jit(solution)/shard_map/all_to_all | solution.py:333
  52.3 1.6 %project.1 = bf16[32,16,128]{2,1,0:T(8,128)(2,1)} custom-call(bf16[32,40,128]{2,1,0:T(8,128)(2,1)S(1)} %all_to_all.25.parts_ref, bf16[256,4096]{1,0:T(8,128)(2,1)S(1)} %copy-done.2), custom_call_target="tpu_custom_call" | custom-call | flops 40000000 | bytes 2700000 | tf_op jit(solution)/shard_map/project/pallas_call | solution.py:335
  53.9 7.5 %all-to-all-start.2 = ((bf16[32,16,128]{2,1,0:T(8,128)(2,1)}), bf16[32,16,128]{2,1,0:T(8,128)(2,1)S(1)}, u32[]{:S(2)}, u32[]{:S(2)}) async-start(bf16[32,16,128]{2,1,0:T(8,128)(2,1)} %project.1), calls=%async_computation.2 | async-start | bytes 262144 | tf_op jit(solution)/shard_map/all_to_all | solution.py:350
  61.4 0.4 prepare.1
  61.8 8.7 %all-to-all-done.2.sums_ref = bf16[32,16,128]{2,1,0:T(8,128)(2,1)S(1)} async-done(((bf16[32,16,128]{2,1,0:T(8,128)(2,1)}), bf16[32,16,128]{2,1,0:T(8,128)(2,1)S(1)}, u32[]{:S(2)}, u32[]{:S(2)}) %all-to-all-start.2) | async-done | bytes 131104 | tf_op jit(solution)/shard_map/all_to_all | solution.py:350
  70.6 0.3 dispatch.1
  70.8 23.2 %all_to_all.26 = bf16[256,4,128]{2,1,0:T(4,128)(2,1)S(1)} all-to-all(bf16[256,4,128]{2,1,0:T(4,128)(2,1)S(1)} %bitcast.37), channel_id=1, replica_groups=mesh['y'=4,'core'=2,'x'=4,'z'=8] {'y','core','x','z'}, dimensions={0} | all-to-all | bytes 524288 | tf_op jit(solution)/shard_map/all_to_all | solution.py:360
  94.0 1.4 %hidden_units.1.act_ref = bf16[32,192]{1,0:T(8,128)(2,1)S(1)} custom-call(bf16[1024,128]{1,0:T(8,128)(2,1)S(1)} %bitcast.36, f32[1,4096]{1,0:T(1,128)S(1)} %bitcast.38, bf16[192,4096]{1,0:T(8,128)(2,1)S(1)} %bitcast.32, bf16[192,4096]{1,0:T(8,128)(2,1)S(1)} %bitcast.33), custom_call_target="tpu_custom_call" | custom-call | flops 100000000 | bytes 3500000 | tf_op jit(solution)/shard_map/hidden_units/pallas_call | solution.py:362
  95.4 0.6 down.1
  96.1 20.9 %all_to_all.27 = bf16[256,4,128]{2,1,0:T(4,128)(2,1)S(1)} all-to-all(bf16[256,4,128]{2,1,0:T(4,128)(2,1)S(1)} %bitcast.34), channel_id=1, replica_groups=mesh['y'=4,'core'=2,'x'=4,'z'=8] {'y','core','x','z'}, dimensions={0} | all-to-all | bytes 524288 | tf_op jit(solution)/shard_map/all_to_all | solution.py:378
  117.0 0.8 combine.1
  (24 shorter events, 0.1 us)
Async XLA Ops:
  0.0 21.4 %collective-permute-start.3 = (bf16[16,2,8,512]{3,2,1,0:T(8,128)(2,1)}, bf16[16,2,8,512]{3,2,1,0:T(8,128)(2,1)S(1)}, u32[]{:S(2)}, u32[]{:S(2)}) collective-permute-start(bf16[16,2,8,512]{3,2,1,0:T(8,128)(2,1)} %refs_0_.1), channel_id=1, source_target_pairs={{0,128},{64,192},{128,0},{192,64},{1,129},{65,193},{129,1},{193,65... | collective-permute-start | bytes 786440 | tf_op jit(solution)/shard_map/ppermute | solution.py:285
  3.7 17.7 %collective-permute-start.1 = (bf16[16,2,8,512]{3,2,1,0:T(8,128)(2,1)}, bf16[16,2,8,512]{3,2,1,0:T(8,128)(2,1)S(1)}, u32[]{:S(2)}, u32[]{:S(2)}) collective-permute-start(bf16[16,2,8,512]{3,2,1,0:T(8,128)(2,1)} %refs_0_.1), channel_id=1, source_target_pairs={{0,64},{64,128},{128,192},{192,0},{1,65},{65,129},{129,193},{193,1... | collective-permute-start | bytes 786440 | tf_op jit(solution)/shard_map/ppermute | solution.py:285
  4.1 17.7 %collective-permute-start.5 = (bf16[16,2,8,512]{3,2,1,0:T(8,128)(2,1)}, bf16[16,2,8,512]{3,2,1,0:T(8,128)(2,1)S(1)}, u32[]{:S(2)}, u32[]{:S(2)}) collective-permute-start(bf16[16,2,8,512]{3,2,1,0:T(8,128)(2,1)} %refs_0_.1), channel_id=1, source_target_pairs={{0,192},{64,0},{128,64},{192,128},{1,193},{65,1},{129,65},{193,129... | collective-permute-start | bytes 786440 | tf_op jit(solution)/shard_map/ppermute | solution.py:285
  8.4 20.3 %all-to-all-start = ((bf16[32,16,128]{2,1,0:T(8,128)(2,1)}), bf16[32,16,128]{2,1,0:T(8,128)(2,1)S(1)}, u32[]{:S(2)}, u32[]{:S(2)}) async-start(bf16[32,16,128]{2,1,0:T(8,128)(2,1)} %lists.1), calls=%async_computation | async-start | bytes 262144 | tf_op jit(solution)/shard_map/all_to_all | solution.py:300
  19.5 10.7 %collective-permute-start = (bf16[16,2,8,512]{3,2,1,0:T(8,128)(2,1)}, bf16[16,2,8,512]{3,2,1,0:T(8,128)(2,1)S(1)}, u32[]{:S(2)}, u32[]{:S(2)}) collective-permute-start(bf16[16,2,8,512]{3,2,1,0:T(8,128)(2,1)} %refs_0_.1), channel_id=1, source_target_pairs={{0,32},{32,0},{1,33},{33,1},{2,34},{34,2},{3,35},{35,3},{4,36},{36... | collective-permute-start | bytes 786440 | tf_op jit(solution)/shard_map/ppermute | solution.py:286
  21.4 8.8 %collective-permute-start.4 = (bf16[16,2,8,512]{3,2,1,0:T(8,128)(2,1)S(1)}, bf16[16,2,8,512]{3,2,1,0:T(8,128)(2,1)S(1)}, u32[]{:S(2)}, u32[]{:S(2)}) collective-permute-start(bf16[16,2,8,512]{3,2,1,0:T(8,128)(2,1)S(1)} %collective-permute-done.3.refs_2_), channel_id=1, source_target_pairs={{0,32},{32,0},{1,33},{33,1},{2,34},{34,2},{3,35},{35,3},{4,36},{36... | collective-permute-start | bytes 786440 | tf_op jit(solution)/shard_map/ppermute | solution.py:286
  21.5 8.7 %collective-permute-start.2 = (bf16[16,2,8,512]{3,2,1,0:T(8,128)(2,1)S(1)}, bf16[16,2,8,512]{3,2,1,0:T(8,128)(2,1)S(1)}, u32[]{:S(2)}, u32[]{:S(2)}) collective-permute-start(bf16[16,2,8,512]{3,2,1,0:T(8,128)(2,1)S(1)} %collective-permute-done.1.refs_1_), channel_id=1, source_target_pairs={{0,32},{32,0},{1,33},{33,1},{2,34},{34,2},{3,35},{35,3},{4,36},{36... | collective-permute-start | bytes 786440 | tf_op jit(solution)/shard_map/ppermute | solution.py:286
  21.9 8.3 %collective-permute-start.6 = (bf16[16,2,8,512]{3,2,1,0:T(8,128)(2,1)S(1)}, bf16[16,2,8,512]{3,2,1,0:T(8,128)(2,1)S(1)}, u32[]{:S(2)}, u32[]{:S(2)}) collective-permute-start(bf16[16,2,8,512]{3,2,1,0:T(8,128)(2,1)S(1)} %collective-permute-done.5.refs_3_), channel_id=1, source_target_pairs={{0,32},{32,0},{1,33},{33,1},{2,34},{34,2},{3,35},{35,3},{4,36},{36... | collective-permute-start | bytes 786440 | tf_op jit(solution)/shard_map/ppermute | solution.py:286
  22.0 0.9 copy-start
  22.9 0.7 copy-start.9
  23.6 5.1 %copy-start.1 = (bf16[16,8192]{1,0:T(8,128)(2,1)S(1)}, bf16[16,8192]{1,0:T(8,128)(2,1)}, u32[]{:S(2)}) copy-start(bf16[16,8192]{1,0:T(8,128)(2,1)} %q_ref.3) | copy-start | bytes 786436
  23.6 5.1 %copy-start.6 = (bf16[16,2,8,512]{3,2,1,0:T(8,128)(2,1)S(1)}, bf16[16,2,8,512]{3,2,1,0:T(8,128)(2,1)}, u32[]{:S(2)}) copy-start(bf16[16,2,8,512]{3,2,1,0:T(8,128)(2,1)} %refs_0_.1) | copy-start | bytes 786436
  30.2 22.1 %copy-start.2 = (bf16[256,4096]{1,0:T(8,128)(2,1)S(1)}, bf16[256,4096]{1,0:T(8,128)(2,1)}, u32[]{:S(2)}) copy-start(bf16[256,4096]{1,0:T(8,128)(2,1)} %weight_ref.1) | copy-start | bytes 6291460
  33.0 28.4 %copy-start.10 = (s32[16,8]{0,1:T(8,128)S(1)}, s32[16,8]{0,1:T(8,128)}, u32[]{:S(2)}) copy-start(s32[16,8]{0,1:T(8,128)} %param.25) | copy-start | bytes 1540
  33.1 28.3 %copy-start.11 = (f32[16,8]{0,1:T(8,128)S(1)}, f32[16,8]{0,1:T(8,128)}, u32[]{:S(2)}) copy-start(f32[16,8]{0,1:T(8,128)} %param.26) | copy-start | bytes 1540
  33.1 37.5 %copy-start.7 = (bf16[16,4096]{1,0:T(8,128)(2,1)S(1)}, bf16[16,4096]{1,0:T(8,128)(2,1)}, u32[]{:S(2)}) copy-start(bf16[16,4096]{1,0:T(8,128)(2,1)} %residual_ref.1) | copy-start | bytes 393220
  33.1 60.9 %copy-start.4 = (bf16[1,192,4096]{2,1,0:T(8,128)(2,1)S(1)}, bf16[1,192,4096]{2,1,0:T(8,128)(2,1)}, u32[]{:S(2)}) copy-start(bf16[1,192,4096]{2,1,0:T(8,128)(2,1)} %param.27) | copy-start | bytes 4718596
  33.1 60.9 %copy-start.5 = (bf16[1,192,4096]{2,1,0:T(8,128)(2,1)S(1)}, bf16[1,192,4096]{2,1,0:T(8,128)(2,1)}, u32[]{:S(2)}) copy-start(bf16[1,192,4096]{2,1,0:T(8,128)(2,1)} %param.28) | copy-start | bytes 4718596
  33.1 60.9 %copy-start.8 = (f32[4096]{0:T(1024)S(1)}, f32[4096]{0:T(1024)}, u32[]{:S(2)}) copy-start(f32[4096]{0:T(1024)} %param.24) | copy-start | bytes 49156
  53.9 16.7 %all-to-all-start.2 = ((bf16[32,16,128]{2,1,0:T(8,128)(2,1)}), bf16[32,16,128]{2,1,0:T(8,128)(2,1)S(1)}, u32[]{:S(2)}, u32[]{:S(2)}) async-start(bf16[32,16,128]{2,1,0:T(8,128)(2,1)} %project.1), calls=%async_computation.2 | async-start | bytes 262144 | tf_op jit(solution)/shard_map/all_to_all | solution.py:350
  70.6 24.9 %copy-start.3 = (bf16[1,192,4096]{2,1,0:T(8,128)(2,1)S(1)}, bf16[1,192,4096]{2,1,0:T(8,128)(2,1)}, u32[]{:S(2)}) copy-start(bf16[1,192,4096]{2,1,0:T(8,128)(2,1)} %param.29) | copy-start | bytes 4718596

commit v5 on v4

--- a/solution.py
+++ b/solution.py
@@ -41,8 +41,9 @@
     return pl.CostEstimate(flops=flops, bytes_accessed=moved, transcendentals=exps)
 
 
-def lists_kernel(key_ref, lists_ref):
-    key = key_ref[...]
+def lists_kernel(key_ref, lists_ref, lengths_ref):
+    key = key_ref[:, :SLOTS]
+    lengths_ref[...] = jnp.broadcast_to(key_ref[:, SLOTS:], (T, 128))
     lane = lax.broadcasted_iota(jnp.int32, (T, 128), 1)
     columns = [jnp.broadcast_to(key[:, j : j + 1], (T, 128)) - lane for j in range(key.shape[1])]
     for c in range(NC):
@@ -52,7 +53,7 @@
         lists_ref[c] = jnp.where(hits[0], 1.0, 0.0).astype(BF)
 
 
-def prepare_kernel(ids_ref, weights_ref, picker_ref, combine_ref):
+def prepare(ids_ref, weights_ref, picker_ref, combine_ref):
     rows = NG * NC * CAPE
     one = (lax.broadcasted_iota(jnp.int32, (T, T), 1) == lax.broadcasted_iota(jnp.int32, (T, T), 0)).astype(F32)
     exact = dict(preferred_element_type=F32, precision=lax.Precision.HIGHEST)
@@ -114,7 +115,7 @@
             for i, g in pairs
         ]
         scores = jnp.concatenate(scores, axis=0).reshape(EACH, HEADS, 128)
-        valid = [position < length_ref[base + i] for i in range(EACH)]
+        valid = [position < length_ref[pl.ds(base + i, 1), :] for i in range(EACH)]
         scores = jnp.stack([jnp.where(valid[i], scores[i] * SCALE, NEG) for i in range(EACH)])
         peak = jnp.max(scores, axis=2, keepdims=True)
         chances = jnp.exp(scores - peak)
@@ -195,7 +196,8 @@
         given[0][here, 2 * T :, :] = jnp.where(lane < 8, *stats).astype(BF)
 
 
-def project_kernel(parts_ref, weight_ref, send_ref):
+def project_kernel(ids_ref, chances_ref, parts_ref, weight_ref, send_ref, picker_ref, combine_ref):
+    prepare(ids_ref, chances_ref, picker_ref, combine_ref)
     stats = parts_ref[:, 2 * T :, :].astype(F32)
     heads = []
     for i in range(2):
@@ -285,14 +287,17 @@
         pages.append(lax.ppermute(visual_page_pool, "y", [(i, (i + k) % 4) for i in range(4)]))
     pages += [lax.ppermute(part, "core", [(0, 1), (1, 0)]) for part in pages]
 
-    holder = recall_holder[0]
+    pad = ((0, 0), (0, 1))
+    holder, slot = jnp.pad(recall_holder[0], pad), jnp.pad(recall_slot[0], pad)
     group = holder // NC
     back = (lax.axis_index("y") + 4 - group // 2) % 4
     near = jnp.where(group % 2 == lax.axis_index("core"), back, back + 4)
-    key = (holder % NC) * 128 + near * SLOTS + recall_slot[0]
-    lists = pl.pallas_call(
+    key = (holder % NC) * 128 + near * SLOTS + slot
+    column = lax.broadcasted_iota(jnp.int32, key.shape, 1)
+    key = jnp.where(column < SLOTS, key, res_len[:, None])
+    lists, lengths = pl.pallas_call(
         lists_kernel,
-        out_shape=jax.ShapeDtypeStruct((NC, T, 128), BF),
+        out_shape=(jax.ShapeDtypeStruct((NC, T, 128), BF), jax.ShapeDtypeStruct((T, 128), jnp.int32)),
         compiler_params=params(4),
         cost_estimate=cost(4_000_000, 140_000),
         name="lists",
@@ -302,7 +307,7 @@
     wide = jax.ShapeDtypeStruct((HEADS * T, 128), F32)
     out, stats = pl.pallas_call(
         resident_kernel,
-        in_specs=[smem, smem, hbm, hbm, hbm],
+        in_specs=[vmem, smem, hbm, hbm, hbm],
         out_shape=(wide, wide),
         scratch_shapes=[
             pltpu.VMEM((HEADS * T, HW), F32),
@@ -314,7 +319,7 @@
         compiler_params=params(51),
         cost_estimate=cost(70_000_000, 6_000_000, 131_072),
         name="resident",
-    )(res_len, start, queries, resident_key_cache, resident_value_cache)
+    )(lengths, start, queries, resident_key_cache, resident_value_cache)
 
     own = pl.pallas_call(
         functools.partial(recalled_kernel, 0),
@@ -332,21 +337,17 @@
     )(lists, queries, *pages[4:], *own, out, stats)
     parts = lax.all_to_all(parts, CTX, split_axis=0, concat_axis=0, tiled=True)
 
-    sums = pl.pallas_call(
+    sums, picker, table = pl.pallas_call(
         project_kernel,
-        out_shape=jax.ShapeDtypeStruct((NC, T, 128), BF),
+        out_shape=(
+            jax.ShapeDtypeStruct((NC, T, 128), BF),
+            jax.ShapeDtypeStruct((T, rows), BF),
+            jax.ShapeDtypeStruct((2 * T, rows), BF),
+        ),
         compiler_params=params(8),
-        cost_estimate=cost(40_000_000, 2_700_000, 2048),
+        cost_estimate=cost(44_000_000, 2_900_000, 2048),
         name="project",
-    )(parts, o_weight)
-    ids, chances, _ = lax.optimization_barrier((expert_ids.T, expert_weights.T, sums))
-    picker, table = pl.pallas_call(
-        prepare_kernel,
-        out_shape=(jax.ShapeDtypeStruct((T, rows), BF), jax.ShapeDtypeStruct((2 * T, rows), BF)),
-        compiler_params=params(4),
-        cost_estimate=cost(4_000_000, 200_000),
-        name="prepare",
-    )(ids, chances)
+    )(expert_ids.T, expert_weights.T, parts, o_weight)
     sums = lax.all_to_all(sums, CTX, split_axis=0, concat_axis=0, tiled=True)
 
     hidden, send = pl.pallas_call(

time: 118 us -> 116 us (0.983)
  blocking collectives: 63.3 us -> 78.6 us
  waiting for transfers between devices: 9.6 us -> 2.02 us
  starting transfers between devices: 27.5 us -> 20 us
  Pallas kernels: 14.8 us -> 13.3 us
    all_to_all x0 -> x1, blocking collectives: none -> 16.5 us  [shards(): sums = lax.all_to_all(sums, CTX, split_axis=0, concat_axis=0, tiled=True)]
    all_to_all x1 -> x0, waiting for transfers between devices: 8.73 us -> none  [shards(): sums = lax.all_to_all(sums, CTX, split_axis=0, concat_axis=0, tiled=True)]
    all_to_all x1 -> x0, starting transfers between devices: 7.52 us -> none  [shards(): sums = lax.all_to_all(sums, CTX, split_axis=0, concat_axis=0, tiled=True)]
    pallas_call x4 -> x3, Pallas kernels: 7.49 us -> 5.96 us  [the longest x1 3.77 us: shards(): pl.pallas_call(resident_kernel, in_specs=[vmem, smem, hbm, hbm, hbm], out...]
  transfers between devices with their start and end apart: 9 -> 8, of which waited for: 2 -> 1; matrix products, arithmetic and copies ran while one was open for 1% -> 1% of each run, Pallas kernels for 6% -> 6%
where the time goes in v5:
time: 116 us
  blocking collectives  78.6 us (68%)
  starting transfers between devices  20 us (17%)
  Pallas kernels  13.3 us (11%)
  waiting for transfers between devices  2.02 us (2%)
    all_to_all x1, blocking collectives, shards(): lax.all_to_all(send.reshape(NG * NC, CAPE, 128), ALL, split_axis=0, conca...  23.2 us
    all_to_all x1, blocking collectives, shards(): lax.all_to_all(results.reshape(NG * NC, CAPE, 128), ALL, split_axis=0, co...  20.9 us
    all_to_all x1, blocking collectives, shards(): parts = lax.all_to_all(parts, CTX, split_axis=0, concat_axis=0, tiled=True)  18 us
    all_to_all x1, blocking collectives, shards(): sums = lax.all_to_all(sums, CTX, split_axis=0, concat_axis=0, tiled=True)  16.5 us
    all_to_all x1, starting transfers between devices, shards(): lists = lax.all_to_all(lists, CTX, split_axis=0, concat_axis=0, tiled=True)  11 us
    ppermute x3, starting transfers between devices, shards(): lax.ppermute(visual_page_pool, 'y', [(i, (i + k) % 4) for i in range(4)])  6.42 us
    pallas_call x1, Pallas kernels, shards(): pl.pallas_call(resident_kernel, in_specs=[vmem, smem, hbm, hbm, hbm], out...  3.77 us
    pallas_call x1, Pallas kernels, shards(): pl.pallas_call(functools.partial(recalled_kernel, 1), out_shape=jax.Shape...  2.8 us
  transfers between devices with their start and end apart: 8, of which 1 were waited for; matrix products, arithmetic and copies ran while one was open for 1% of the time, Pallas kernels for 6%

profile of v5, /device:TPU:1, one launch (start us, length us, event | category | flops | bytes accessed | tf_op | source)
XLA Modules:
  0.0 115.8 jit_solution(18345929886910467434)
XLA Ops:
  0.0 3.7 %collective-permute-start.3 = (bf16[16,2,8,512]{3,2,1,0:T(8,128)(2,1)}, bf16[16,2,8,512]{3,2,1,0:T(8,128)(2,1)S(1)}, u32[]{:S(2)}, u32[]{:S(2)}) collective-permute-start(bf16[16,2,8,512]{3,2,1,0:T(8,128)(2,1)} %refs_0_.1), channel_id=1, source_target_pairs={{0,128},{64,192},{128,0},{192,64},{1,129},{65,193},{129,1},{193,65... | collective-permute-start | bytes 786440 | tf_op jit(solution)/shard_map/ppermute | solution.py:287
  3.7 0.4 collective-permute-start.1
  4.1 2.3 %collective-permute-start.5 = (bf16[16,2,8,512]{3,2,1,0:T(8,128)(2,1)}, bf16[16,2,8,512]{3,2,1,0:T(8,128)(2,1)S(1)}, u32[]{:S(2)}, u32[]{:S(2)}) collective-permute-start(bf16[16,2,8,512]{3,2,1,0:T(8,128)(2,1)} %refs_0_.1), channel_id=1, source_target_pairs={{0,192},{64,0},{128,64},{192,128},{1,193},{65,1},{129,65},{193,129... | collective-permute-start | bytes 786440 | tf_op jit(solution)/shard_map/ppermute | solution.py:287
  6.4 0.8 fusion.3.key_ref
  7.2 1.2 %lists.1 = (bf16[32,16,128]{2,1,0:T(8,128)(2,1)}, s32[16,128]{1,0:T(8,128)S(1)}) custom-call(s32[16,17]{1,0:T(8,128)S(1)} %fusion.3.key_ref), custom_call_target="tpu_custom_call" | custom-call | flops 4000000 | bytes 140000 | tf_op jit(solution)/shard_map/lists/pallas_call | solution.py:298
  8.5 11.0 %all-to-all-start = ((bf16[32,16,128]{2,1,0:T(8,128)(2,1)}), bf16[32,16,128]{2,1,0:T(8,128)(2,1)S(1)}, u32[]{:S(2)}, u32[]{:S(2)}) async-start(bf16[32,16,128]{2,1,0:T(8,128)(2,1)} %get-tuple-element.16), calls=%async_computation | async-start | bytes 262144 | tf_op jit(solution)/shard_map/all_to_all | solution.py:305
  19.5 1.9 %collective-permute-start = (bf16[16,2,8,512]{3,2,1,0:T(8,128)(2,1)}, bf16[16,2,8,512]{3,2,1,0:T(8,128)(2,1)S(1)}, u32[]{:S(2)}, u32[]{:S(2)}) collective-permute-start(bf16[16,2,8,512]{3,2,1,0:T(8,128)(2,1)} %refs_0_.1), channel_id=1, source_target_pairs={{0,32},{32,0},{1,33},{33,1},{2,34},{34,2},{3,35},{35,3},{4,36},{36... | collective-permute-start | bytes 786440 | tf_op jit(solution)/shard_map/ppermute | solution.py:288
  21.4 0.1 collective-permute-start.4
  21.5 0.4 collective-permute-start.2
  21.9 0.1 collective-permute-start.6
  22.0 0.9 copy-done
  23.0 3.8 %resident.1 = (f32[1024,128]{1,0:T(8,128)S(1)}, f32[1024,128]{1,0:T(8,128)S(1)}) custom-call(s32[16,128]{1,0:T(8,128)S(1)} %get-tuple-element.19.length_ref, s32[1]{0:T(128)} %bitcast.start_ref, bf16[16,8192]{1,0:T(8,128)(2,1)S(1)} %copy-done, bf16[16,128,512]{2,1,0:T(8,128)(2,1)} %keys_hbm.1, bf16[16,128,512]{2,1,0:T(8,128)(2,1)} %values_hbm.1), custom_call_target="tpu_custom_call" | custom-call | flops 70000000 | bytes 6000000 | tf_op jit(solution)/shard_map/resident/pallas_call | solution.py:308
  26.8 2.0 %all-to-all-done.lists_ref = bf16[32,16,128]{2,1,0:T(8,128)(2,1)S(1)} async-done(((bf16[32,16,128]{2,1,0:T(8,128)(2,1)}), bf16[32,16,128]{2,1,0:T(8,128)(2,1)S(1)}, u32[]{:S(2)}, u32[]{:S(2)}) %all-to-all-start) | async-done | bytes 131104 | tf_op jit(solution)/shard_map/all_to_all | solution.py:305
  28.8 1.5 %recalled_own.1 = (f32[1024,128]{1,0:T(8,128)S(1)}, f32[1024,128]{1,0:T(8,128)S(1)}) custom-call(bf16[32,16,128]{2,1,0:T(8,128)(2,1)S(1)} %all-to-all-done.lists_ref, bf16[16,8192]{1,0:T(8,128)(2,1)S(1)} %copy-done.1, bf16[16,2,8,512]{3,2,1,0:T(8,128)(2,1)S(1)} %copy-done.6, bf16[16,2,8,512]{3,2,1,0:T(8,128)(2,1)S(1)} %collective-permute-done.1.refs_1_, ...), custom_call_target="tpu_custom_call" | custom-call | flops 270000000 | bytes 4000000 | tf_op jit(solution)/shard_map/recalled_own/pallas_call | solution.py:324
  30.2 0.0 collective-permute-done.4.refs_2_
  30.3 0.0 copy-start.2
  30.3 0.0 copy-start.9
  30.3 0.0 copy-start.10
  30.3 2.8 %recalled_other.1 = bf16[32,40,128]{2,1,0:T(8,128)(2,1)S(1)} custom-call(bf16[32,16,128]{2,1,0:T(8,128)(2,1)S(1)} %all-to-all-done.lists_ref, bf16[16,8192]{1,0:T(8,128)(2,1)S(1)} %copy-done.1, bf16[16,2,8,512]{3,2,1,0:T(8,128)(2,1)S(1)} %collective-permute-done.refs_0_, bf16[16,2,8,512]{3,2,1,0:T(8,128)(2,1)S(1)} %collective-permute-done.2.refs_1_, ...), custom_call_target="tpu_custom_call" | custom-call | flops 270000000 | bytes 4000000 | tf_op jit(solution)/shard_map/recalled_other/pallas_call | solution.py:331
  33.1 0.0 copy-start.7
  33.1 0.0 copy-start.4
  33.1 0.0 copy-start.5
  33.1 0.0 copy-start.8
  33.2 18.0 %all_to_all.25.parts_ref = bf16[32,40,128]{2,1,0:T(8,128)(2,1)S(1)} all-to-all(bf16[32,40,128]{2,1,0:T(8,128)(2,1)S(1)} %recalled_other.1), channel_id=1, replica_groups=mesh['y'=4,'core'=2,'x'=4,'z'=8] {'x','z'}, dimensions={0} | all-to-all | bytes 655360 | tf_op jit(solution)/shard_map/all_to_all | solution.py:338
  51.2 0.9 project.1
  52.2 16.5 %all_to_all.26.sums_ref = bf16[32,16,128]{2,1,0:T(8,128)(2,1)S(1)} all-to-all(bf16[32,16,128]{2,1,0:T(8,128)(2,1)S(1)} %get-tuple-element.22), channel_id=1, replica_groups=mesh['y'=4,'core'=2,'x'=4,'z'=8] {'x','z'}, dimensions={0} | all-to-all | bytes 262144 | tf_op jit(solution)/shard_map/all_to_all | solution.py:351
  68.7 0.3 dispatch.1
  68.9 23.2 %all_to_all.27 = bf16[256,4,128]{2,1,0:T(4,128)(2,1)S(1)} all-to-all(bf16[256,4,128]{2,1,0:T(4,128)(2,1)S(1)} %bitcast.19), channel_id=1, replica_groups=mesh['y'=4,'core'=2,'x'=4,'z'=8] {'y','core','x','z'}, dimensions={0} | all-to-all | bytes 524288 | tf_op jit(solution)/shard_map/all_to_all | solution.py:361
  92.1 1.4 %hidden_units.1.act_ref = bf16[32,192]{1,0:T(8,128)(2,1)S(1)} custom-call(bf16[1024,128]{1,0:T(8,128)(2,1)S(1)} %bitcast.18, f32[1,4096]{1,0:T(1,128)S(1)} %bitcast.20, bf16[192,4096]{1,0:T(8,128)(2,1)S(1)} %bitcast.14, bf16[192,4096]{1,0:T(8,128)(2,1)S(1)} %bitcast.15), custom_call_target="tpu_custom_call" | custom-call | flops 100000000 | bytes 3500000 | tf_op jit(solution)/shard_map/hidden_units/pallas_call | solution.py:363
  93.5 0.6 down.1
  94.1 20.9 %all_to_all.28 = bf16[256,4,128]{2,1,0:T(4,128)(2,1)S(1)} all-to-all(bf16[256,4,128]{2,1,0:T(4,128)(2,1)S(1)} %bitcast.16), channel_id=1, replica_groups=mesh['y'=4,'core'=2,'x'=4,'z'=8] {'y','core','x','z'}, dimensions={0} | all-to-all | bytes 524288 | tf_op jit(solution)/shard_map/all_to_all | solution.py:379
  115.0 0.8 combine.1
  (21 shorter events, 0.0 us)
Async XLA Ops:
  0.0 21.4 %collective-permute-start.3 = (bf16[16,2,8,512]{3,2,1,0:T(8,128)(2,1)}, bf16[16,2,8,512]{3,2,1,0:T(8,128)(2,1)S(1)}, u32[]{:S(2)}, u32[]{:S(2)}) collective-permute-start(bf16[16,2,8,512]{3,2,1,0:T(8,128)(2,1)} %refs_0_.1), channel_id=1, source_target_pairs={{0,128},{64,192},{128,0},{192,64},{1,129},{65,193},{129,1},{193,65... | collective-permute-start | bytes 786440 | tf_op jit(solution)/shard_map/ppermute | solution.py:287
  3.7 17.8 %collective-permute-start.1 = (bf16[16,2,8,512]{3,2,1,0:T(8,128)(2,1)}, bf16[16,2,8,512]{3,2,1,0:T(8,128)(2,1)S(1)}, u32[]{:S(2)}, u32[]{:S(2)}) collective-permute-start(bf16[16,2,8,512]{3,2,1,0:T(8,128)(2,1)} %refs_0_.1), channel_id=1, source_target_pairs={{0,64},{64,128},{128,192},{192,0},{1,65},{65,129},{129,193},{193,1... | collective-permute-start | bytes 786440 | tf_op jit(solution)/shard_map/ppermute | solution.py:287
  4.1 17.8 %collective-permute-start.5 = (bf16[16,2,8,512]{3,2,1,0:T(8,128)(2,1)}, bf16[16,2,8,512]{3,2,1,0:T(8,128)(2,1)S(1)}, u32[]{:S(2)}, u32[]{:S(2)}) collective-permute-start(bf16[16,2,8,512]{3,2,1,0:T(8,128)(2,1)} %refs_0_.1), channel_id=1, source_target_pairs={{0,192},{64,0},{128,64},{192,128},{1,193},{65,1},{129,65},{193,129... | collective-permute-start | bytes 786440 | tf_op jit(solution)/shard_map/ppermute | solution.py:287
  8.5 20.3 %all-to-all-start = ((bf16[32,16,128]{2,1,0:T(8,128)(2,1)}), bf16[32,16,128]{2,1,0:T(8,128)(2,1)S(1)}, u32[]{:S(2)}, u32[]{:S(2)}) async-start(bf16[32,16,128]{2,1,0:T(8,128)(2,1)} %get-tuple-element.16), calls=%async_computation | async-start | bytes 262144 | tf_op jit(solution)/shard_map/all_to_all | solution.py:305
  19.5 10.7 %collective-permute-start = (bf16[16,2,8,512]{3,2,1,0:T(8,128)(2,1)}, bf16[16,2,8,512]{3,2,1,0:T(8,128)(2,1)S(1)}, u32[]{:S(2)}, u32[]{:S(2)}) collective-permute-start(bf16[16,2,8,512]{3,2,1,0:T(8,128)(2,1)} %refs_0_.1), channel_id=1, source_target_pairs={{0,32},{32,0},{1,33},{33,1},{2,34},{34,2},{3,35},{35,3},{4,36},{36... | collective-permute-start | bytes 786440 | tf_op jit(solution)/shard_map/ppermute | solution.py:288
  21.4 8.8 %collective-permute-start.4 = (bf16[16,2,8,512]{3,2,1,0:T(8,128)(2,1)S(1)}, bf16[16,2,8,512]{3,2,1,0:T(8,128)(2,1)S(1)}, u32[]{:S(2)}, u32[]{:S(2)}) collective-permute-start(bf16[16,2,8,512]{3,2,1,0:T(8,128)(2,1)S(1)} %collective-permute-done.3.refs_2_), channel_id=1, source_target_pairs={{0,32},{32,0},{1,33},{33,1},{2,34},{34,2},{3,35},{35,3},{4,36},{36... | collective-permute-start | bytes 786440 | tf_op jit(solution)/shard_map/ppermute | solution.py:288
  21.5 8.7 %collective-permute-start.2 = (bf16[16,2,8,512]{3,2,1,0:T(8,128)(2,1)S(1)}, bf16[16,2,8,512]{3,2,1,0:T(8,128)(2,1)S(1)}, u32[]{:S(2)}, u32[]{:S(2)}) collective-permute-start(bf16[16,2,8,512]{3,2,1,0:T(8,128)(2,1)S(1)} %collective-permute-done.1.refs_1_), channel_id=1, source_target_pairs={{0,32},{32,0},{1,33},{33,1},{2,34},{34,2},{3,35},{35,3},{4,36},{36... | collective-permute-start | bytes 786440 | tf_op jit(solution)/shard_map/ppermute | solution.py:288
  21.9 8.4 %collective-permute-start.6 = (bf16[16,2,8,512]{3,2,1,0:T(8,128)(2,1)S(1)}, bf16[16,2,8,512]{3,2,1,0:T(8,128)(2,1)S(1)}, u32[]{:S(2)}, u32[]{:S(2)}) collective-permute-start(bf16[16,2,8,512]{3,2,1,0:T(8,128)(2,1)S(1)} %collective-permute-done.5.refs_3_), channel_id=1, source_target_pairs={{0,32},{32,0},{1,33},{33,1},{2,34},{34,2},{3,35},{35,3},{4,36},{36... | collective-permute-start | bytes 786440 | tf_op jit(solution)/shard_map/ppermute | solution.py:288
  22.0 0.9 copy-start
  23.0 5.8 %copy-start.1 = (bf16[16,8192]{1,0:T(8,128)(2,1)S(1)}, bf16[16,8192]{1,0:T(8,128)(2,1)}, u32[]{:S(2)}) copy-start(bf16[16,8192]{1,0:T(8,128)(2,1)} %q_ref.3) | copy-start | bytes 786436
  23.0 5.8 %copy-start.6 = (bf16[16,2,8,512]{3,2,1,0:T(8,128)(2,1)S(1)}, bf16[16,2,8,512]{3,2,1,0:T(8,128)(2,1)}, u32[]{:S(2)}) copy-start(bf16[16,2,8,512]{3,2,1,0:T(8,128)(2,1)} %refs_0_.1) | copy-start | bytes 786436
  30.3 20.9 %copy-start.2 = (bf16[256,4096]{1,0:T(8,128)(2,1)S(1)}, bf16[256,4096]{1,0:T(8,128)(2,1)}, u32[]{:S(2)}) copy-start(bf16[256,4096]{1,0:T(8,128)(2,1)} %weight_ref.1) | copy-start | bytes 6291460
  30.3 20.9 %copy-start.9 = (s32[16,8]{0,1:T(8,128)S(1)}, s32[16,8]{0,1:T(8,128)}, u32[]{:S(2)}) copy-start(s32[16,8]{0,1:T(8,128)} %param.25) | copy-start | bytes 1540
  30.3 20.9 %copy-start.10 = (f32[16,8]{0,1:T(8,128)S(1)}, f32[16,8]{0,1:T(8,128)}, u32[]{:S(2)}) copy-start(f32[16,8]{0,1:T(8,128)} %param.26) | copy-start | bytes 1540
  33.1 35.5 %copy-start.7 = (bf16[16,4096]{1,0:T(8,128)(2,1)S(1)}, bf16[16,4096]{1,0:T(8,128)(2,1)}, u32[]{:S(2)}) copy-start(bf16[16,4096]{1,0:T(8,128)(2,1)} %residual_ref.1) | copy-start | bytes 393220
  33.1 59.0 %copy-start.4 = (bf16[1,192,4096]{2,1,0:T(8,128)(2,1)S(1)}, bf16[1,192,4096]{2,1,0:T(8,128)(2,1)}, u32[]{:S(2)}) copy-start(bf16[1,192,4096]{2,1,0:T(8,128)(2,1)} %param.27) | copy-start | bytes 4718596
  33.1 59.0 %copy-start.5 = (bf16[1,192,4096]{2,1,0:T(8,128)(2,1)S(1)}, bf16[1,192,4096]{2,1,0:T(8,128)(2,1)}, u32[]{:S(2)}) copy-start(bf16[1,192,4096]{2,1,0:T(8,128)(2,1)} %param.28) | copy-start | bytes 4718596
  33.1 59.0 %copy-start.8 = (f32[4096]{0:T(1024)S(1)}, f32[4096]{0:T(1024)}, u32[]{:S(2)}) copy-start(f32[4096]{0:T(1024)} %param.24) | copy-start | bytes 49156
  68.7 24.9 %copy-start.3 = (bf16[1,192,4096]{2,1,0:T(8,128)(2,1)S(1)}, bf16[1,192,4096]{2,1,0:T(8,128)(2,1)}, u32[]{:S(2)}) copy-start(bf16[1,192,4096]{2,1,0:T(8,128)(2,1)} %param.29) | copy-start | bytes 4718596

commit v6 on v5

--- a/solution.py
+++ b/solution.py
@@ -29,7 +29,8 @@
 ALL = GRP + CTX
 NT = (((1,), (1,)), ((), ()))
 STAT_ROWS = 8
-EACH = 4
+EACH = 8
+FETCH = 4
 CHUNK = 2 * T + STAT_ROWS
 
 
@@ -79,18 +80,18 @@
 
 
 def resident_kernel(length_ref, start_ref, q_hbm, keys_hbm, values_hbm, out_ref, stats_ref, wide, q, k, v, sems):
-    steps = k.shape[0] // EACH
-    first = pltpu.make_async_copy(q_hbm, q, sems.at[2 * steps])
+    steps, fetches = k.shape[0] // EACH, k.shape[0] // FETCH
+    first = pltpu.make_async_copy(q_hbm, q, sems.at[2 * fetches])
     first.start()
 
     def chunk(i):
-        here = pl.ds(i * EACH, EACH)
+        here = pl.ds(i * FETCH, FETCH)
         return (
             pltpu.make_async_copy(keys_hbm.at[here], k.at[here], sems.at[2 * i]),
             pltpu.make_async_copy(values_hbm.at[here], v.at[here], sems.at[2 * i + 1]),
         )
 
-    for i in range(steps):
+    for i in range(fetches):
         for copy in chunk(i):
             copy.start()
     first.wait()
@@ -104,8 +105,9 @@
 
     @pl.loop(0, steps)
     def _(step):
-        for copy in chunk(step):
-            copy.wait()
+        for i in range(EACH // FETCH):
+            for copy in chunk(step * (EACH // FETCH) + i):
+                copy.wait()
         base = step * EACH
         own = [wide[pl.ds(base + i, HEADS, stride=T), :].astype(BF) for i in range(EACH)]
         scores = [
@@ -314,7 +316,7 @@
             pltpu.VMEM((T, HEADS * HW), BF),
             pltpu.VMEM((T, 128, KV * HW), BF),
             pltpu.VMEM((T, 128, KV * HW), BF),
-            pltpu.SemaphoreType.DMA((2 * T // EACH + 1,)),
+            pltpu.SemaphoreType.DMA((2 * T // FETCH + 1,)),
         ],
         compiler_params=params(51),
         cost_estimate=cost(70_000_000, 6_000_000, 131_072),

time: 116 us -> 116 us (level)
  no operation moved by 1% of the time
where the time goes in v6:
time: 116 us
  blocking collectives  78.6 us (68%)
  starting transfers between devices  20 us (17%)
  Pallas kernels  13.2 us (11%)
  waiting for transfers between devices  2.06 us (2%)
    all_to_all x1, blocking collectives, shards(): lax.all_to_all(send.reshape(NG * NC, CAPE, 128), ALL, split_axis=0, conca...  23.2 us
    all_to_all x1, blocking collectives, shards(): lax.all_to_all(results.reshape(NG * NC, CAPE, 128), ALL, split_axis=0, co...  20.9 us
    all_to_all x1, blocking collectives, shards(): parts = lax.all_to_all(parts, CTX, split_axis=0, concat_axis=0, tiled=True)  18 us
    all_to_all x1, blocking collectives, shards(): sums = lax.all_to_all(sums, CTX, split_axis=0, concat_axis=0, tiled=True)  16.5 us
    all_to_all x1, starting transfers between devices, shards(): lists = lax.all_to_all(lists, CTX, split_axis=0, concat_axis=0, tiled=True)  11 us
    ppermute x3, starting transfers between devices, shards(): lax.ppermute(visual_page_pool, 'y', [(i, (i + k) % 4) for i in range(4)])  6.42 us
    pallas_call x1, Pallas kernels, shards(): pl.pallas_call(resident_kernel, in_specs=[vmem, smem, hbm, hbm, hbm], out...  3.73 us
    pallas_call x1, Pallas kernels, shards(): pl.pallas_call(functools.partial(recalled_kernel, 1), out_shape=jax.Shape...  2.8 us
  transfers between devices with their start and end apart: 8, of which 1 were waited for; matrix products, arithmetic and copies ran while one was open for 1% of the time, Pallas kernels for 6%

profile of v6, /device:TPU:1, one launch (start us, length us, event | category | flops | bytes accessed | tf_op | source)
XLA Modules:
  0.0 115.8 jit_solution(15550469210211455902)
XLA Ops:
  0.0 3.7 %collective-permute-start.3 = (bf16[16,2,8,512]{3,2,1,0:T(8,128)(2,1)}, bf16[16,2,8,512]{3,2,1,0:T(8,128)(2,1)S(1)}, u32[]{:S(2)}, u32[]{:S(2)}) collective-permute-start(bf16[16,2,8,512]{3,2,1,0:T(8,128)(2,1)} %refs_0_.1), channel_id=1, source_target_pairs={{0,128},{64,192},{128,0},{192,64},{1,129},{65,193},{129,1},{193,65... | collective-permute-start | bytes 786440 | tf_op jit(solution)/shard_map/ppermute | solution.py:289
  3.7 0.4 collective-permute-start.1
  4.1 2.3 %collective-permute-start.5 = (bf16[16,2,8,512]{3,2,1,0:T(8,128)(2,1)}, bf16[16,2,8,512]{3,2,1,0:T(8,128)(2,1)S(1)}, u32[]{:S(2)}, u32[]{:S(2)}) collective-permute-start(bf16[16,2,8,512]{3,2,1,0:T(8,128)(2,1)} %refs_0_.1), channel_id=1, source_target_pairs={{0,192},{64,0},{128,64},{192,128},{1,193},{65,1},{129,65},{193,129... | collective-permute-start | bytes 786440 | tf_op jit(solution)/shard_map/ppermute | solution.py:289
  6.4 0.8 fusion.3.key_ref
  7.2 1.2 %lists.1 = (bf16[32,16,128]{2,1,0:T(8,128)(2,1)}, s32[16,128]{1,0:T(8,128)S(1)}) custom-call(s32[16,17]{1,0:T(8,128)S(1)} %fusion.3.key_ref), custom_call_target="tpu_custom_call" | custom-call | flops 4000000 | bytes 140000 | tf_op jit(solution)/shard_map/lists/pallas_call | solution.py:300
  8.5 11.0 %all-to-all-start = ((bf16[32,16,128]{2,1,0:T(8,128)(2,1)}), bf16[32,16,128]{2,1,0:T(8,128)(2,1)S(1)}, u32[]{:S(2)}, u32[]{:S(2)}) async-start(bf16[32,16,128]{2,1,0:T(8,128)(2,1)} %get-tuple-element.16), calls=%async_computation | async-start | bytes 262144 | tf_op jit(solution)/shard_map/all_to_all | solution.py:307
  19.5 1.9 %collective-permute-start = (bf16[16,2,8,512]{3,2,1,0:T(8,128)(2,1)}, bf16[16,2,8,512]{3,2,1,0:T(8,128)(2,1)S(1)}, u32[]{:S(2)}, u32[]{:S(2)}) collective-permute-start(bf16[16,2,8,512]{3,2,1,0:T(8,128)(2,1)} %refs_0_.1), channel_id=1, source_target_pairs={{0,32},{32,0},{1,33},{33,1},{2,34},{34,2},{3,35},{35,3},{4,36},{36... | collective-permute-start | bytes 786440 | tf_op jit(solution)/shard_map/ppermute | solution.py:290
  21.4 0.1 collective-permute-start.4
  21.5 0.4 collective-permute-start.2
  21.9 0.1 collective-permute-start.6
  22.0 0.9 copy-done
  23.0 3.7 %resident.1 = (f32[1024,128]{1,0:T(8,128)S(1)}, f32[1024,128]{1,0:T(8,128)S(1)}) custom-call(s32[16,128]{1,0:T(8,128)S(1)} %get-tuple-element.19.length_ref, s32[1]{0:T(128)} %bitcast.start_ref, bf16[16,8192]{1,0:T(8,128)(2,1)S(1)} %copy-done, bf16[16,128,512]{2,1,0:T(8,128)(2,1)} %keys_hbm.1, bf16[16,128,512]{2,1,0:T(8,128)(2,1)} %values_hbm.1), custom_call_target="tpu_custom_call" | custom-call | flops 70000000 | bytes 6000000 | tf_op jit(solution)/shard_map/resident/pallas_call | solution.py:310
  26.7 2.0 %all-to-all-done.lists_ref = bf16[32,16,128]{2,1,0:T(8,128)(2,1)S(1)} async-done(((bf16[32,16,128]{2,1,0:T(8,128)(2,1)}), bf16[32,16,128]{2,1,0:T(8,128)(2,1)S(1)}, u32[]{:S(2)}, u32[]{:S(2)}) %all-to-all-start) | async-done | bytes 131104 | tf_op jit(solution)/shard_map/all_to_all | solution.py:307
  28.8 1.5 %recalled_own.1 = (f32[1024,128]{1,0:T(8,128)S(1)}, f32[1024,128]{1,0:T(8,128)S(1)}) custom-call(bf16[32,16,128]{2,1,0:T(8,128)(2,1)S(1)} %all-to-all-done.lists_ref, bf16[16,8192]{1,0:T(8,128)(2,1)S(1)} %copy-done.1, bf16[16,2,8,512]{3,2,1,0:T(8,128)(2,1)S(1)} %copy-done.6, bf16[16,2,8,512]{3,2,1,0:T(8,128)(2,1)S(1)} %collective-permute-done.1.refs_1_, ...), custom_call_target="tpu_custom_call" | custom-call | flops 270000000 | bytes 4000000 | tf_op jit(solution)/shard_map/recalled_own/pallas_call | solution.py:326
  30.2 0.0 collective-permute-done.4.refs_2_
  30.3 0.0 copy-start.2
  30.3 0.0 copy-start.9
  30.3 0.0 copy-start.10
  30.3 2.8 %recalled_other.1 = bf16[32,40,128]{2,1,0:T(8,128)(2,1)S(1)} custom-call(bf16[32,16,128]{2,1,0:T(8,128)(2,1)S(1)} %all-to-all-done.lists_ref, bf16[16,8192]{1,0:T(8,128)(2,1)S(1)} %copy-done.1, bf16[16,2,8,512]{3,2,1,0:T(8,128)(2,1)S(1)} %collective-permute-done.refs_0_, bf16[16,2,8,512]{3,2,1,0:T(8,128)(2,1)S(1)} %collective-permute-done.2.refs_1_, ...), custom_call_target="tpu_custom_call" | custom-call | flops 270000000 | bytes 4000000 | tf_op jit(solution)/shard_map/recalled_other/pallas_call | solution.py:333
  33.1 0.0 copy-start.7
  33.1 0.0 copy-start.4
  33.1 0.0 copy-start.5
  33.1 0.0 copy-start.8
  33.2 18.0 %all_to_all.25.parts_ref = bf16[32,40,128]{2,1,0:T(8,128)(2,1)S(1)} all-to-all(bf16[32,40,128]{2,1,0:T(8,128)(2,1)S(1)} %recalled_other.1), channel_id=1, replica_groups=mesh['y'=4,'core'=2,'x'=4,'z'=8] {'x','z'}, dimensions={0} | all-to-all | bytes 655360 | tf_op jit(solution)/shard_map/all_to_all | solution.py:340
  51.2 0.9 project.1
  52.1 16.5 %all_to_all.26.sums_ref = bf16[32,16,128]{2,1,0:T(8,128)(2,1)S(1)} all-to-all(bf16[32,16,128]{2,1,0:T(8,128)(2,1)S(1)} %get-tuple-element.22), channel_id=1, replica_groups=mesh['y'=4,'core'=2,'x'=4,'z'=8] {'x','z'}, dimensions={0} | all-to-all | bytes 262144 | tf_op jit(solution)/shard_map/all_to_all | solution.py:353
  68.6 0.3 dispatch.1
  68.9 23.2 %all_to_all.27 = bf16[256,4,128]{2,1,0:T(4,128)(2,1)S(1)} all-to-all(bf16[256,4,128]{2,1,0:T(4,128)(2,1)S(1)} %bitcast.19), channel_id=1, replica_groups=mesh['y'=4,'core'=2,'x'=4,'z'=8] {'y','core','x','z'}, dimensions={0} | all-to-all | bytes 524288 | tf_op jit(solution)/shard_map/all_to_all | solution.py:363
  92.1 1.4 %hidden_units.1.act_ref = bf16[32,192]{1,0:T(8,128)(2,1)S(1)} custom-call(bf16[1024,128]{1,0:T(8,128)(2,1)S(1)} %bitcast.18, f32[1,4096]{1,0:T(1,128)S(1)} %bitcast.20, bf16[192,4096]{1,0:T(8,128)(2,1)S(1)} %bitcast.14, bf16[192,4096]{1,0:T(8,128)(2,1)S(1)} %bitcast.15), custom_call_target="tpu_custom_call" | custom-call | flops 100000000 | bytes 3500000 | tf_op jit(solution)/shard_map/hidden_units/pallas_call | solution.py:365
  93.5 0.6 down.1
  94.1 20.9 %all_to_all.28 = bf16[256,4,128]{2,1,0:T(4,128)(2,1)S(1)} all-to-all(bf16[256,4,128]{2,1,0:T(4,128)(2,1)S(1)} %bitcast.16), channel_id=1, replica_groups=mesh['y'=4,'core'=2,'x'=4,'z'=8] {'y','core','x','z'}, dimensions={0} | all-to-all | bytes 524288 | tf_op jit(solution)/shard_map/all_to_all | solution.py:381
  115.0 0.8 combine.1
  (21 shorter events, 0.0 us)
Async XLA Ops:
  0.0 21.4 %collective-permute-start.3 = (bf16[16,2,8,512]{3,2,1,0:T(8,128)(2,1)}, bf16[16,2,8,512]{3,2,1,0:T(8,128)(2,1)S(1)}, u32[]{:S(2)}, u32[]{:S(2)}) collective-permute-start(bf16[16,2,8,512]{3,2,1,0:T(8,128)(2,1)} %refs_0_.1), channel_id=1, source_target_pairs={{0,128},{64,192},{128,0},{192,64},{1,129},{65,193},{129,1},{193,65... | collective-permute-start | bytes 786440 | tf_op jit(solution)/shard_map/ppermute | solution.py:289
  3.7 17.8 %collective-permute-start.1 = (bf16[16,2,8,512]{3,2,1,0:T(8,128)(2,1)}, bf16[16,2,8,512]{3,2,1,0:T(8,128)(2,1)S(1)}, u32[]{:S(2)}, u32[]{:S(2)}) collective-permute-start(bf16[16,2,8,512]{3,2,1,0:T(8,128)(2,1)} %refs_0_.1), channel_id=1, source_target_pairs={{0,64},{64,128},{128,192},{192,0},{1,65},{65,129},{129,193},{193,1... | collective-permute-start | bytes 786440 | tf_op jit(solution)/shard_map/ppermute | solution.py:289
  4.1 17.8 %collective-permute-start.5 = (bf16[16,2,8,512]{3,2,1,0:T(8,128)(2,1)}, bf16[16,2,8,512]{3,2,1,0:T(8,128)(2,1)S(1)}, u32[]{:S(2)}, u32[]{:S(2)}) collective-permute-start(bf16[16,2,8,512]{3,2,1,0:T(8,128)(2,1)} %refs_0_.1), channel_id=1, source_target_pairs={{0,192},{64,0},{128,64},{192,128},{1,193},{65,1},{129,65},{193,129... | collective-permute-start | bytes 786440 | tf_op jit(solution)/shard_map/ppermute | solution.py:289
  8.5 20.3 %all-to-all-start = ((bf16[32,16,128]{2,1,0:T(8,128)(2,1)}), bf16[32,16,128]{2,1,0:T(8,128)(2,1)S(1)}, u32[]{:S(2)}, u32[]{:S(2)}) async-start(bf16[32,16,128]{2,1,0:T(8,128)(2,1)} %get-tuple-element.16), calls=%async_computation | async-start | bytes 262144 | tf_op jit(solution)/shard_map/all_to_all | solution.py:307
  19.5 10.7 %collective-permute-start = (bf16[16,2,8,512]{3,2,1,0:T(8,128)(2,1)}, bf16[16,2,8,512]{3,2,1,0:T(8,128)(2,1)S(1)}, u32[]{:S(2)}, u32[]{:S(2)}) collective-permute-start(bf16[16,2,8,512]{3,2,1,0:T(8,128)(2,1)} %refs_0_.1), channel_id=1, source_target_pairs={{0,32},{32,0},{1,33},{33,1},{2,34},{34,2},{3,35},{35,3},{4,36},{36... | collective-permute-start | bytes 786440 | tf_op jit(solution)/shard_map/ppermute | solution.py:290
  21.4 8.8 %collective-permute-start.4 = (bf16[16,2,8,512]{3,2,1,0:T(8,128)(2,1)S(1)}, bf16[16,2,8,512]{3,2,1,0:T(8,128)(2,1)S(1)}, u32[]{:S(2)}, u32[]{:S(2)}) collective-permute-start(bf16[16,2,8,512]{3,2,1,0:T(8,128)(2,1)S(1)} %collective-permute-done.3.refs_2_), channel_id=1, source_target_pairs={{0,32},{32,0},{1,33},{33,1},{2,34},{34,2},{3,35},{35,3},{4,36},{36... | collective-permute-start | bytes 786440 | tf_op jit(solution)/shard_map/ppermute | solution.py:290
  21.5 8.7 %collective-permute-start.2 = (bf16[16,2,8,512]{3,2,1,0:T(8,128)(2,1)S(1)}, bf16[16,2,8,512]{3,2,1,0:T(8,128)(2,1)S(1)}, u32[]{:S(2)}, u32[]{:S(2)}) collective-permute-start(bf16[16,2,8,512]{3,2,1,0:T(8,128)(2,1)S(1)} %collective-permute-done.1.refs_1_), channel_id=1, source_target_pairs={{0,32},{32,0},{1,33},{33,1},{2,34},{34,2},{3,35},{35,3},{4,36},{36... | collective-permute-start | bytes 786440 | tf_op jit(solution)/shard_map/ppermute | solution.py:290
  21.9 8.4 %collective-permute-start.6 = (bf16[16,2,8,512]{3,2,1,0:T(8,128)(2,1)S(1)}, bf16[16,2,8,512]{3,2,1,0:T(8,128)(2,1)S(1)}, u32[]{:S(2)}, u32[]{:S(2)}) collective-permute-start(bf16[16,2,8,512]{3,2,1,0:T(8,128)(2,1)S(1)} %collective-permute-done.5.refs_3_), channel_id=1, source_target_pairs={{0,32},{32,0},{1,33},{33,1},{2,34},{34,2},{3,35},{35,3},{4,36},{36... | collective-permute-start | bytes 786440 | tf_op jit(solution)/shard_map/ppermute | solution.py:290
  22.0 0.9 copy-start
  23.0 5.8 %copy-start.1 = (bf16[16,8192]{1,0:T(8,128)(2,1)S(1)}, bf16[16,8192]{1,0:T(8,128)(2,1)}, u32[]{:S(2)}) copy-start(bf16[16,8192]{1,0:T(8,128)(2,1)} %q_ref.3) | copy-start | bytes 786436
  23.0 5.8 %copy-start.6 = (bf16[16,2,8,512]{3,2,1,0:T(8,128)(2,1)S(1)}, bf16[16,2,8,512]{3,2,1,0:T(8,128)(2,1)}, u32[]{:S(2)}) copy-start(bf16[16,2,8,512]{3,2,1,0:T(8,128)(2,1)} %refs_0_.1) | copy-start | bytes 786436
  30.3 20.9 %copy-start.2 = (bf16[256,4096]{1,0:T(8,128)(2,1)S(1)}, bf16[256,4096]{1,0:T(8,128)(2,1)}, u32[]{:S(2)}) copy-start(bf16[256,4096]{1,0:T(8,128)(2,1)} %weight_ref.1) | copy-start | bytes 6291460
  30.3 20.9 %copy-start.9 = (s32[16,8]{0,1:T(8,128)S(1)}, s32[16,8]{0,1:T(8,128)}, u32[]{:S(2)}) copy-start(s32[16,8]{0,1:T(8,128)} %param.25) | copy-start | bytes 1540
  30.3 20.9 %copy-start.10 = (f32[16,8]{0,1:T(8,128)S(1)}, f32[16,8]{0,1:T(8,128)}, u32[]{:S(2)}) copy-start(f32[16,8]{0,1:T(8,128)} %param.26) | copy-start | bytes 1540
  33.1 35.5 %copy-start.7 = (bf16[16,4096]{1,0:T(8,128)(2,1)S(1)}, bf16[16,4096]{1,0:T(8,128)(2,1)}, u32[]{:S(2)}) copy-start(bf16[16,4096]{1,0:T(8,128)(2,1)} %residual_ref.1) | copy-start | bytes 393220
  33.1 58.9 %copy-start.4 = (bf16[1,192,4096]{2,1,0:T(8,128)(2,1)S(1)}, bf16[1,192,4096]{2,1,0:T(8,128)(2,1)}, u32[]{:S(2)}) copy-start(bf16[1,192,4096]{2,1,0:T(8,128)(2,1)} %param.27) | copy-start | bytes 4718596
  33.1 58.9 %copy-start.5 = (bf16[1,192,4096]{2,1,0:T(8,128)(2,1)S(1)}, bf16[1,192,4096]{2,1,0:T(8,128)(2,1)}, u32[]{:S(2)}) copy-start(bf16[1,192,4096]{2,1,0:T(8,128)(2,1)} %param.28) | copy-start | bytes 4718596
  33.1 58.9 %copy-start.8 = (f32[4096]{0:T(1024)S(1)}, f32[4096]{0:T(1024)}, u32[]{:S(2)}) copy-start(f32[4096]{0:T(1024)} %param.24) | copy-start | bytes 49156
  68.6 24.9 %copy-start.3 = (bf16[1,192,4096]{2,1,0:T(8,128)(2,1)S(1)}, bf16[1,192,4096]{2,1,0:T(8,128)(2,1)}, u32[]{:S(2)}) copy-start(bf16[1,192,4096]{2,1,0:T(8,128)(2,1)} %param.29) | copy-start | bytes 4718596
